TPU v7x, 32 devices: a whole 2x2x4 slice. The times are simulated.
32 devices in a mesh: fsdp: 4 (over y, x), seq: 8 (over z, core).
Axes of the slice: x: 2, y: 2, z: 4, core: 2. Of those that a mesh axis runs over, the one named last changes fastest.
Arguments:
- conv_input: bfloat16 [4, 1024, 3712], P('fsdp', 'seq'), may hold values from -6 to 6
- gate_input: bfloat16 [4, 1024, 3584], P('fsdp', 'seq'), may hold values from -6 to 6
- dt_raw: float32 [4, 1024, 56], P('fsdp', 'seq'), may hold values from -4 to 10
- grad_output: bfloat16 [4, 1024, 3584], P('fsdp', 'seq'), may hold values from -6 to 6
- conv_weight: float32 [4, 3712], P(None, 'fsdp'), may hold values from -3 to 3
- conv_bias: float32 [3712], P('fsdp'), may hold values from -0.5 to 0.5
- dt_bias: float32 [56], P('fsdp'), may hold values from -1 to 0.5
- a_log: float32 [56], P('fsdp'), may hold values from -14 to -2
- skip: float32 [56], P('fsdp'), may hold values from 0.5 to 2
- norm_gain: float32 [3584], P('fsdp'), may hold values from 0.5 to 1.5
Outputs:
- grad_conv_input: bfloat16 [4, 1024, 3712], P('fsdp', 'seq')
- grad_gate_input: bfloat16 [4, 1024, 3584], P('fsdp', 'seq')
- grad_dt_raw: float32 [4, 1024, 56], P('fsdp', 'seq')
- grad_conv_weight: float32 [4, 3712], P(None, 'fsdp')
- grad_conv_bias: float32 [3712], P('fsdp')
- grad_dt_bias: float32 [56], P('fsdp')
- grad_a_log: float32 [56], P('fsdp')
- grad_skip: float32 [56], P('fsdp')
- grad_norm_gain: float32 [3584], P('fsdp')
All inputs are finite; a program needn't handle non-finite values.
Results may differ from a plain program's by a relative error of at most 0.012.
Values may be sent and summed in bfloat16 or wider, within the bound.
No kernel may reach another device: no remote copies, remote signals or barrier semaphores. Data moves between devices by JAX's collectives and lax.ppermute only.
A program may use at most 512 MiB of HBM per device.

v0:
```python
import jax
import jax.numpy as jnp
from jax import lax
from jax.sharding import PartitionSpec as P

P_SIZE = 64
N = 64


EPS = 1e-05
HIGH = lax.Precision.HIGHEST


def from_behind(block, axis, distance):
    devices = range(lax.axis_size(axis))
    route = [(i - distance, i) for i in devices if i - distance in devices]
    return lax.ppermute(block, axis, route)


def entering_2(value, axis, join, neutral, backward):
    count, mine = (lax.axis_size(axis), lax.axis_index(axis))
    pieces = jax.tree.map(lambda part: lax.all_gather(part, axis), value)
    if backward:
        pieces = jax.tree.map(lambda part: part[::-1], pieces)
        mine = count - 1 - mine
    subtotal = jax.tree.map(
        lambda part, zero: jnp.full_like(part, 0) + jnp.asarray(zero, part.dtype), value, neutral
    )

    def turn(position, subtotal):
        longer = join(subtotal, jax.tree.map(lambda part: part[position], pieces))
        return jax.tree.map(lambda new, old: jnp.where(position < mine, new, old), longer, subtotal)

    return lax.fori_loop(0, count - 1, turn, subtotal)


def convolve(padded, conv_weight, conv_bias):
    length = padded.shape[0] - conv_weight.shape[0] + 1
    summed = jnp.zeros((length, padded.shape[1]), jnp.float32) + conv_bias[None, :]
    for kernel_tap in range(conv_weight.shape[0]):
        summed = (
            summed + conv_weight[kernel_tap][None, :] * padded[kernel_tap : kernel_tap + length]
        )
    rounded = jax.nn.silu(summed).astype(jnp.bfloat16)
    return lax.optimization_barrier(rounded).astype(jnp.float32)


def inner_part(padded, raw_step, conv_weight, conv_bias, dt_bias, a_log):
    conv_out = convolve(padded, conv_weight, conv_bias)
    length = conv_out.shape[0]
    head_count = a_log.shape[0]
    inner_width = head_count * P_SIZE
    step_size = jax.nn.softplus(raw_step + dt_bias[None, :])
    running = jnp.cumsum(-jnp.exp(a_log)[None, :] * step_size, axis=0)
    values = conv_out[:, :inner_width].reshape(length, head_count, P_SIZE)
    input_projector = conv_out[:, inner_width : inner_width + N]
    read_vec = conv_out[:, inner_width + N :]
    scores = jnp.dot(read_vec, input_projector.T, precision=HIGH)
    by_head = running.T
    log_gap = by_head[:, :, None] - by_head[:, None, :]
    causal = lax.broadcasted_iota(jnp.int32, (length, length), 0) >= lax.broadcasted_iota(
        jnp.int32, (length, length), 1
    )
    decay = jnp.exp(jnp.where(causal[None], log_gap, -jnp.inf))
    weights = decay * scores[None] * step_size.T[:, None, :]
    intra_out = jnp.einsum("hts,shp->thp", weights, values, precision=HIGH)
    tail_weight = jnp.exp(running[-1][None, :] - running) * step_size
    local_state = jnp.einsum("sh,shp,sn->hpn", tail_weight, values, input_projector, precision=HIGH)
    return (conv_out, running, intra_out, local_state)


def outer_part(conv_out, running, intra_out, gate_rows, skip, norm_gain, state_in):
    length, head_count = running.shape
    inner_width = head_count * P_SIZE
    values = conv_out[:, :inner_width].reshape(length, head_count, P_SIZE)
    read_vec = conv_out[:, inner_width + N :]
    carried = jnp.einsum("tn,hpn->thp", read_vec, state_in, precision=HIGH)
    mixed = intra_out + jnp.exp(running)[:, :, None] * carried + skip[None, :, None] * values
    gated = mixed.reshape(length, inner_width) * jax.nn.silu(gate_rows.astype(jnp.float32))
    scale = lax.rsqrt(jnp.mean(gated * gated, axis=-1, keepdims=True) + EPS)
    return gated * scale * norm_gain[None, :]


def combine(earlier, later):
    return (earlier[0] * later[0], later[0][:, None, None] * earlier[1] + later[1])


def own_share(whole, along, position, share_count):
    piece = whole.shape[along] // share_count
    return lax.dynamic_slice_in_dim(whole, position * piece, piece, along)


def shards(
    conv_input,
    gate_input,
    dt_raw,
    grad_output,
    conv_weight,
    conv_bias,
    dt_bias,
    a_log,
    skip,
    norm_gain,
):
    gathered = (
        lax.all_gather(conv_weight, "fsdp", axis=1, tiled=True),
        lax.all_gather(conv_bias, "fsdp", axis=0, tiled=True),
        lax.all_gather(dt_bias, "fsdp", axis=0, tiled=True),
        lax.all_gather(a_log, "fsdp", axis=0, tiled=True),
        lax.all_gather(skip, "fsdp", axis=0, tiled=True),
        lax.all_gather(norm_gain, "fsdp", axis=0, tiled=True),
    )
    full_conv, full_bias, full_dt_bias, full_a_log, full_skip, full_gain = gathered
    local_rows = conv_input[0]
    margin = full_conv.shape[0] - 1
    earlier_rows = from_behind(local_rows[local_rows.shape[0] - margin :], "seq", 1)
    padded = jnp.concatenate([earlier_rows, local_rows], axis=0).astype(jnp.float32)
    raw_step = dt_raw[0]
    inner_vals, inner_back = jax.vjp(
        inner_part, padded, raw_step, full_conv, full_bias, full_dt_bias, full_a_log
    )
    conv_out, running, intra_out, local_state = inner_vals
    head_count = full_a_log.shape[0]
    slab_decay = jnp.exp(running[-1])
    identity = (jnp.ones((head_count,), jnp.float32), jnp.zeros(local_state.shape, jnp.float32))
    entering = entering_2((slab_decay, local_state), "seq", combine, identity, False)
    state_in = entering[1]
    normed, outer_back = jax.vjp(
        outer_part, conv_out, running, intra_out, gate_input[0], full_skip, full_gain, state_in
    )
    outer_grads = outer_back(grad_output[0].astype(jnp.float32))
    grad_conv_out, grad_running, grad_intra, grad_gate, grad_skip, gain_gradient, state_grad = (
        outer_grads
    )
    leaving = entering_2((slab_decay, state_grad), "seq", combine, identity, True)
    grad_end = leaving[1]
    grad_running = grad_running.at[-1].add(slab_decay * jnp.sum(grad_end * state_in, axis=(1, 2)))
    inner_grads = inner_back((grad_conv_out, grad_running, grad_intra, grad_end))
    grad_padded, grad_step, grad_conv, grad_bias, grad_dt_bias, grad_a_log = inner_grads
    back_rows = from_behind(grad_padded[:margin].astype(jnp.bfloat16), "seq", -1).astype(
        jnp.float32
    )
    own_rows = grad_padded[margin:]
    length = own_rows.shape[0]
    summed = own_rows + jnp.concatenate(
        [jnp.zeros((length - margin, own_rows.shape[1]), jnp.float32), back_rows], axis=0
    )
    grad_rows = summed.astype(jnp.bfloat16)
    local_grads = (grad_conv, grad_bias, grad_dt_bias, grad_a_log, grad_skip, gain_gradient)
    summed_all = lax.psum(
        (
            local_grads[0],
            local_grads[1],
            local_grads[2],
            local_grads[3],
            local_grads[4],
            local_grads[5],
        ),
        ("fsdp", "seq"),
    )
    position = lax.axis_index("fsdp")
    share_count = lax.axis_size("fsdp")
    aggregate_sums = (
        own_share(summed_all[0], 1, position, share_count),
        own_share(summed_all[1], 0, position, share_count),
        own_share(summed_all[2], 0, position, share_count),
        own_share(summed_all[3], 0, position, share_count),
        own_share(summed_all[4], 0, position, share_count),
        own_share(summed_all[5], 0, position, share_count),
    )
    return (
        grad_rows[None],
        grad_gate[None],
        grad_step[None],
        aggregate_sums[0],
        aggregate_sums[1],
        aggregate_sums[2],
        aggregate_sums[3],
        aggregate_sums[4],
        aggregate_sums[5],
    )


def solution(mesh):
    in_specs = (
        P("fsdp", "seq", None),
        P("fsdp", "seq", None),
        P("fsdp", "seq", None),
        P("fsdp", "seq", None),
        P(None, "fsdp"),
        P("fsdp"),
        P("fsdp"),
        P("fsdp"),
        P("fsdp"),
        P("fsdp"),
    )
    out_specs = (
        P("fsdp", "seq", None),
        P("fsdp", "seq", None),
        P("fsdp", "seq", None),
        P(None, "fsdp"),
        P("fsdp"),
        P("fsdp"),
        P("fsdp"),
        P("fsdp"),
        P("fsdp"),
    )
    return jax.shard_map(shards, mesh=mesh, in_specs=in_specs, out_specs=out_specs, check_vma=False)
```

profile of v0, /device:TPU:0, one launch (start us, length us, event | category | flops | bytes accessed | tf_op | source)
XLA Modules:
  0.0 551.5 jit_solution(15300236721050351691)
XLA Ops:
  16.4 17.2 %all-reduce.20 = (f32[56]{0:T(128)S(1)}, f32[56]{0:T(128)S(1)}, f32[3712]{0:T(1024)S(1)}, f32[56]{0:T(128)S(1)}) all-reduce(f32[56]{0:T(128)S(1)} %dynamic-update-slice.3, f32[56]{0:T(128)S(1)} %dynamic-update-slice.4, f32[3712]{0:T(1024)S(1)} %dynamic-update-slice.5, ...), channel_id=1, replica_groups=mesh['fsdp'=4,'seq'=8] {'fsdp'}, use_global_device_ids=true, to_apply=%add.15 | all-reduce | flops 3880 | bytes 31040
  35.8 7.4 %all-gather.2 = f32[4,928,4]{1,2,0:T(4,128)S(1)} all-gather(f32[1,928,4]{1,2,0:T(4,128)} %bitcast.135), channel_id=1, replica_groups=mesh['fsdp'=4,'seq'=8] {'fsdp'}, dimensions={0}, use_global_device_ids=true | all-gather | bytes 74240 | tf_op jit(solution)/shard_map/all_gather | solution.py:106
  47.0 6.1 %multiply_convert_fusion = (bf16[128,3712]{0,1:T(8,128)(2,1)S(1)}, f32[128,3712]{0,1:T(8,128)}) fusion(f32[131,3712]{0,1:T(8,128)S(1)} %maximum_convert_fusion, f32[3712]{0:T(1024)S(1)} %get-tuple-element.306, f32[3712]{0:T(1024)S(1)} %get-tuple-element.307, f32[3712]{0:T(1024)S(1)} %get-tuple-element.308, f32[3712]{0:T(1024)S(1)} %get-tuple-element.309, ...), kind=kLoop, calls=%fused_computation.40 | loop fusion | flops 6176768 | bytes 10527232 | tf_op jit(solution)/shard_map/jvp()/convert_element_type | solution.py:44
  58.9 8.0 %all-gather.3 = f32[4,1,896]{2,1,0:T(1,128)S(1)} all-gather(f32[1,1,896]{2,1,0:T(1,128)S(1)} %reshape.234), channel_id=1, replica_groups=mesh['fsdp'=4,'seq'=8] {'fsdp'}, dimensions={0}, use_global_device_ids=true | all-gather | bytes 17920 | tf_op jit(solution)/shard_map/all_gather | solution.py:111
  67.0 2.6 copy.101
  69.6 12.2 %all-gather.4 = f32[8,1,56]{2,1,0:T(1,128)S(1)} all-gather(f32[1,1,56]{2,1,0:T(1,128)S(1)} %bitcast.138), channel_id=1, replica_groups=mesh['fsdp'=4,'seq'=8] {'seq'}, dimensions={0}, use_global_device_ids=true | all-gather | bytes 2016 | tf_op jit(solution)/shard_map/all_gather | solution.py:22
  82.8 108.0 %all-gather.8.cloned.1.call-done = f32[448,64,64]{2,1,0:T(8,128)} async-done(((f32[56,64,64]{2,1,0:T(8,128)}), f32[448,64,64]{2,1,0:T(8,128)}) %all-gather.8.cloned.1.call-update) | async-done | bytes 7340048 | tf_op jit(solution)/shard_map/all_gather | solution.py:22
  190.8 13.7 %while.29 = (s32[]{:T(128)}, f32[56,64,64]{2,1,0:T(8,128)S(1)}, s32[]{:T(128)}, f32[8,56]{1,0:T(8,128)S(1)}, f32[8,56,64,64]{3,2,1,0:T(8,128)}, /*index=5*/s32[]{:T(128)}, s32[]{:T(128)}) while((s32[]{:T(128)}, f32[56,64,64]{2,1,0:T(8,128)S(1)}, s32[]{:T(128)}, f32[8,56]{1,0:T(8,128)S(1)}, f32[8,56,64,64]{3,2,1,0:T(8,128)}, ...), condition=%wide.region_2.3_spmd.clone, body=%wide.region_1.2_spmd.clone.sunk | while | flops 917508 | bytes 2753289 | solution.py:34
  206.7 5.4 multiply_reduce_fusion.10
  216.8 2.9 fusion.38
  220.7 2.8 copy.114
  223.5 7.0 %fusion.11 = (f32[56,128]{1,0:T(8,128)S(1)}, f32[56,128]{1,0:T(8,128)S(1)}, f32[56,128]{1,0:T(8,128)S(1)}, f32[128,128]{1,0:T(8,128)S(1)}) fusion(f32[56,128]{1,0:T(8,128)S(1)} %get-tuple-element.358, f32[128,128]{1,0:T(8,128)S(1)} %fusion.74, f32[56,128]{1,0:T(8,128)S(1)} %copy.104, pred[128,128]{1,0:T(8,128)(4,1)S(1)} %iota_compare_fusion, ...), kind=kOutput, calls=%fused_computation.28 | convolution fusion | flops 716532736 | bytes 3043328 | tf_op jit(solution)/shard_map/transpose(jvp(hts,shp->thp))/dot_general | solution.py:66
  231.5 3.2 fusion.48
  236.9 115.2 %all-gather.10.cloned.1.call-done = f32[448,64,64]{2,1,0:T(8,128)} async-done(((f32[56,64,64]{2,1,0:T(8,128)}), f32[448,64,64]{2,1,0:T(8,128)}) %all-gather.10.cloned.1.call-update) | async-done | bytes 7340048 | tf_op jit(solution)/shard_map/all_gather | solution.py:22
  352.1 13.6 %rev.7 = f32[8,56,64,64]{3,2,1,0:T(8,128)} reverse(f32[8,56,64,64]{3,2,1,0:T(8,128)} %bitcast.119), dimensions={0} | reverse | bytes 14680064 | tf_op jit(solution)/shard_map/rev | solution.py:24
  365.8 13.9 %while.30 = (s32[]{:T(128)}, f32[56,64,64]{2,1,0:T(8,128)S(1)}, s32[]{:T(128)}, f32[8,56]{1,0:T(8,128)S(1)}, f32[8,56,64,64]{3,2,1,0:T(8,128)}, /*index=5*/s32[]{:T(128)}, s32[]{:T(128)}) while((s32[]{:T(128)}, f32[56,64,64]{2,1,0:T(8,128)S(1)}, s32[]{:T(128)}, f32[8,56]{1,0:T(8,128)S(1)}, f32[8,56,64,64]{3,2,1,0:T(8,128)}, ...), condition=%wide.region_7.8_spmd.clone, body=%wide.region_6.7_spmd.clone.sunk | while | flops 917508 | bytes 2753289 | solution.py:34
  379.7 3.2 fusion.51
  382.9 3.7 fusion.21
  388.1 4.1 bitcast_add_fusion.2
  394.3 4.9 multiply_reduce_fusion.5
  401.5 2.6 broadcast_multiply_fusion.3
  404.1 3.0 pad_add_fusion
  413.8 2.9 fusion.52
  418.6 118.3 %all-reduce.23.cloned.1.call-done = (f32[4,3712]{1,0:T(4,128)}, f32[3712]{0:T(1024)}, f32[56]{0:T(128)}, f32[56]{0:T(128)}, f32[56]{0:T(128)}, /*index=5*/f32[3584]{0:T(1024)}) async-done(((f32[4,3712]{1,0:T(4,128)}, f32[3712]{0:T(1024)}, f32[56]{0:T(128)}, f32[56]{0:T(128)}, f32[56]{0:T(128)}, /*index=5*/f32[3584]{0:T(1024)}), (f32[4,3712]{1,0:T(4,128)}, f32[3712]{0:T(1024)}, f32[56]{0:T(128)}, ...) | async-done | bytes 89264 | tf_op jit(solution)/shard_map/psum | solution.py:150
  (151 shorter events, 80.5 us)
Async XLA Ops:
  7.2 183.6 %all-gather.8.cloned.1.call-start = ((), (), s32[]{:S(2)}) async-start(), calls=%async_computation | async-start | bytes 16515072 | tf_op jit(solution)/shard_map/all_gather | solution.py:22
  8.1 37.6 %collective-permute-start = (bf16[3,3712]{1,0:T(4,128)(2,1)S(1)}, bf16[3,3712]{1,0:T(4,128)(2,1)S(1)}, u32[]{:S(2)}, u32[]{:S(2)}) collective-permute-start(bf16[3,3712]{1,0:T(4,128)(2,1)S(1)} %slice_bitcast_fusion), channel_id=1, source_target_pairs={{0,1},{1,2},{2,3},{3,4},{4,5},{5,6},{6,7},{8,9},{9,10},{10,11},{11... | collective-permute-start | bytes 66824 | tf_op jit(solution)/shard_map/ppermute | solution.py:17
  47.0 6.1 %copy-start.3 = (f32[131,3712]{0,1:T(8,128)}, f32[131,3712]{0,1:T(8,128)S(1)}, u32[]{:S(2)}) copy-start(f32[131,3712]{0,1:T(8,128)S(1)} %maximum_convert_fusion) | copy-start | bytes 5835268
  56.3 2.6 copy-start.19
  56.3 295.8 %all-gather.10.cloned.1.call-start = ((), (), s32[]{:S(2)}) async-start(), calls=%async_computation.1 | async-start | bytes 16515072 | tf_op jit(solution)/shard_map/all_gather | solution.py:22
  204.5 1.9 copy-start
  204.5 2.2 copy-start.14
  206.5 5.6 %copy-start.11 = (f32[128,56,64]{0,2,1:T(8,128)}, f32[128,56,64]{0,2,1:T(8,128)S(1)}, u32[]{:S(2)}) copy-start(f32[128,56,64]{0,2,1:T(8,128)S(1)} %fusion.68) | copy-start | bytes 5505028
  206.7 5.4 copy-start.8
  215.6 1.3 copy-start.5
  219.8 317.0 %all-reduce.23.cloned.1.call-start = ((), (), s32[]{:S(2)}) async-start(), calls=%async_computation.2 | async-start | bytes 187392 | tf_op jit(solution)/shard_map/psum | solution.py:150
  223.5 7.9 %copy-start.1 = (f32[56,64,64]{2,1,0:T(8,128)S(1)}, f32[56,64,64]{2,1,0:T(8,128)}, u32[]{:S(2)}) copy-start(f32[56,64,64]{2,1,0:T(8,128)} %copy-done) | copy-start | bytes 2752516
  223.5 8.0 %copy-start.6 = (f32[128,56,64]{0,2,1:T(8,128)S(1)}, f32[128,56,64]{0,2,1:T(8,128)}, u32[]{:S(2)}) copy-start(f32[128,56,64]{0,2,1:T(8,128)} %copy-done.5) | copy-start | bytes 5505028
  231.5 3.3 copy-start.12
  231.5 3.3 copy-start.16
  231.5 3.3 copy-start.17
  379.7 3.2 copy-start.7
  382.9 3.7 copy-start.2
  388.1 4.2 copy-start.13
  388.1 4.4 copy-start.10
  392.3 2.1 copy-start.4
  394.3 5.1 copy-start.18
  407.1 1.8 copy-start.9
  409.4 3.9 collective-permute-start.1
  (1 other events, 0.9 us)
Sparse Core Ops, SparseCore 0:
  56.4 134.3 all-gather.7
  219.9 132.1 all-gather.9
  413.4 123.3 all-reduce.22
where the time goes:
time: 561 us; the launch traced here: 552 us
  waiting for transfers between devices  342 us (61%)
  other arithmetic  59.5 us (11%)
  local copies, waits for them, and re-layouts  48.7 us (9%)
  blocking collectives  44.7 us (8%)
  matrix products  36.4 us (6%)
  between operations  16 us (3%)
    all_gather x2, waiting for transfers between devices, entering_2(): pieces = jax.tree.map(lambda part: lax.all_gather(part, axis), value)  223 us
    psum x1, waiting for transfers between devices, shards(): lax.psum((local_grads[0], local_grads[1], local_grads[2], local_grads[3],...  118 us
    select_n x14, other arithmetic, turn(): jnp.where(position < mine, new, old)  26.9 us
    unnamed x1, blocking collectives  17.2 us
    dot_general x3, matrix products, inner_part(): intra_out = jnp.einsum('hts,shp->thp', weights, values, precision=HIGH)  16.5 us
    unnamed x54, local copies, waits for them, and re-layouts  14.8 us
    rev x2, local copies, waits for them, and re-layouts, entering_2(): pieces = jax.tree.map(lambda part: part[::-1], pieces)  13.7 us
    all_gather x1, blocking collectives, entering_2(): pieces = jax.tree.map(lambda part: lax.all_gather(part, axis), value)  12.2 us
  transfers between devices with their start and end apart: 5, of which 3 were waited for; matrix products, arithmetic and copies ran while one was open for 7% of the time, Pallas kernels for 0%

commit v1 on v0

v1 whole, which is shorter than its diff:
```python
import functools

import jax
import jax.numpy as jnp
from jax import lax
from jax.experimental import pallas as pl
from jax.experimental.pallas import tpu as pltpu
from jax.sharding import PartitionSpec as P

P_SIZE = 64
N = 64
EPS = 1e-05
LANES = 2 * P_SIZE
HALO = 8
SMALL = 8
DEC_ROWS = 32
F32, BF16 = jnp.float32, jnp.bfloat16
HIGH = lax.Precision.HIGHEST


def dot(a, b, over=(1, 0), precision=None):
    return lax.dot_general(
        a, b, (((over[0],), (over[1],)), ((), ())), precision=precision, preferred_element_type=F32
    )


def iota(shape, axis):
    return lax.broadcasted_iota(jnp.int32, shape, axis)


def sigmoid(x):
    return 0.5 * jnp.tanh(0.5 * x) + 0.5


def split(x):
    high = x.astype(BF16)
    return high, (x - high.astype(F32)).astype(BF16)


def block(position):
    return slice(position * LANES, (position + 1) * LANES)


def by_head(columns, pair, shape):
    first = jnp.broadcast_to(columns[:, 2 * pair : 2 * pair + 1], shape)
    second = jnp.broadcast_to(columns[:, 2 * pair + 1 : 2 * pair + 2], shape)
    return jnp.where(iota(shape, 1) < P_SIZE, first, second)


def apart(pair_block):
    first = iota(pair_block.shape, 1) < P_SIZE
    zero = jnp.zeros_like(pair_block)
    return jnp.concatenate(
        [jnp.where(first, pair_block, zero), jnp.where(first, zero, pair_block)], axis=0
    )


def head_sums(product, pair):
    shape = (LANES, LANES)
    pick = (iota(shape, 1) == 2 * pair + (iota(shape, 0) >= P_SIZE).astype(jnp.int32)).astype(BF16)
    high, low = split(product)
    return dot(jnp.concatenate([high, low], axis=1), jnp.concatenate([pick, pick], axis=0))


def fill_rows(rows, x_ref, halo_ref):
    rows[0:HALO, :] = halo_ref[...].astype(F32)
    rows[HALO:, :] = x_ref[...].astype(F32)


def before_silu(rows, full, cols, taps, length):
    start = HALO - (taps - 1)
    total = full[taps : taps + 1, cols] + full[0:1, cols] * rows[start : start + length, cols]
    for tap in range(1, taps):
        total = total + full[tap : tap + 1, cols] * rows[start + tap : start + tap + length, cols]
    return total


def pack_kernel(cw, cb, dtb, al, sk, gain, out):
    out[...] = jnp.zeros_like(out)
    taps, width = cw.shape
    out[0:taps, 0:width] = cw[...]
    out[taps : taps + 1, 0:width] = cb[...]
    out[taps + 1 : taps + 2, 0 : gain.shape[1]] = gain[...]
    for number, ref in enumerate((dtb, al, sk)):
        out[taps + 2 : taps + 3, number * LANES : number * LANES + ref.shape[1]] = ref[...]


def placement(position, width):
    start = position * width
    base = start // LANES * LANES
    return base, start - base


def front_kernel(
    taps, sizes, core, x, halo, pieces, dt, conv, full, gain, small, cols, rows_out, mine, other, decs, rows, states, wide
):
    length, channels = x.shape
    parts, _, piece_width = pieces.shape
    width, gain_width, heads_here = sizes
    heads = heads_here * parts
    pairs = heads // 2
    half = pairs // 2
    features = heads * P_SIZE
    fill_rows(rows, x, halo)
    full[...] = jnp.zeros_like(full)
    small[...] = jnp.zeros_like(small)
    for part in range(parts):
        base, shift = placement(part, width)
        piece = jnp.concatenate([pieces[part], jnp.zeros((SMALL, LANES), F32)], axis=1)
        if shift:
            piece = pltpu.roll(piece, shift, 1)
        full[:, base : base + piece_width + LANES] += piece
        gain[:, part * gain_width : (part + 1) * gain_width] = pieces[
            part, taps + 1 : taps + 2, 0:gain_width
        ]
        for number in range(3):
            row = pieces[part, taps + 2 : taps + 3, block(number)]
            if part:
                row = pltpu.roll(row, part * heads_here, 1)
            small[number : number + 1, :] += row
    wide[...] = jnp.zeros_like(wide)
    wide[:, 0:heads] = dt[...]
    raw = wide[...] + small[0:1, :]
    step = jnp.maximum(raw, 0.0) + jnp.log1p(jnp.exp(-jnp.abs(raw)))
    logs = -jnp.exp(small[1:2, :]) * step
    square = (length, length)
    lower = (iota(square, 0) >= iota(square, 1)).astype(F32)
    running = dot(lower, logs, precision=HIGH)
    running_t = running.T
    step_t = step.T
    last = jnp.broadcast_to(running_t[:, length - 1 : length], running_t.shape)
    tail_t = jnp.exp(last - running_t) * step_t
    cols[0] = step
    cols[1] = running
    rows_out[0] = step_t
    rows_out[1] = running_t
    rows_out[2] = tail_t
    wide[...] = jnp.exp(last)[:, 0:LANES]
    first = iota((half, LANES), 1) < P_SIZE
    for side in range(2):
        even = wide[pl.ds(2 * half * side, half, stride=2), :]
        odd = wide[pl.ds(2 * half * side + 1, half, stride=2), :]
        high, low = split(jnp.where(first, even, odd))
        decay_rows = jnp.zeros((DEC_ROWS // 2 - half, LANES), BF16)
        decs[side] = jnp.concatenate([high, decay_rows, low, decay_rows], axis=0)
    for position in list(range(pairs, channels // LANES)) + list(range(pairs)):
        here = block(position)
        pre = before_silu(rows, full, here, taps, length)
        out = (pre * sigmoid(pre)).astype(BF16)
        conv[:, here] = out
        if position == pairs:
            write_t = out.astype(F32).T[0:N, :]
        else:
            scaled = jnp.concatenate(
                [
                    (write_t * tail_t[2 * position + which : 2 * position + which + 1, :]).astype(BF16)
                    for which in range(2)
                ],
                axis=1,
            )
            start = position % half * N
            states[position // half, start : start + N, :] = dot(scaled, apart(out)).astype(BF16)
    end = half * N
    states[:, end : end + DEC_ROWS, :] = decs[...]
    mine[...] = states[core[0]]
    other[...] = states[1 - core[0]]


def head_weights(cols, rows_ref, head, causal, scores):
    gap = cols[1, :, head : head + 1] - rows_ref[1, head : head + 1, :]
    scaled = jnp.exp(jnp.where(causal, gap, -1e30)) * rows_ref[0, head : head + 1, :]
    return scaled, (scaled * scores).astype(BF16)


def intra_kernel(taps, x, halo, full, conv, cols, rows_ref, small, local, slope, rows):
    length, channels = x.shape
    features = local.shape[1]
    pairs = features // LANES
    write = conv[:, features : features + N]
    read = conv[:, features + N : features + 2 * N]
    scores = dot(read, write, (1, 1))
    square = (length, length)
    causal = iota(square, 0) >= iota(square, 1)
    for pair in range(pairs):
        weights = jnp.concatenate(
            [head_weights(cols, rows_ref, 2 * pair + which, causal, scores)[1] for which in range(2)],
            axis=1,
        )
        values = conv[:, block(pair)]
        skip = by_head(small[2:3, :], pair, (1, LANES))
        local[:, block(pair)] = dot(weights, apart(values)) + skip * values.astype(F32)
    fill_rows(rows, x, halo)
    for position in range(channels // LANES):
        here = block(position)
        pre = before_silu(rows, full, here, taps, length)
        gate = sigmoid(pre)
        slope[:, here] = gate * (1.0 + pre * (1.0 - gate))


def norm_kernel(
    core, local, conv, cols, gate, grad, gain, own, got, decs, mixed, stats, mine, other, entry, gated, silus, states
):
    length, features = local.shape
    pairs = features // LANES
    half = pairs // 2
    shape = (length, LANES)
    entry[core[0]] = own[...]
    entry[1 - core[0]] = got[...]
    read = conv[:, features + N : features + 2 * N]
    decay = jnp.exp(cols[1])
    square_sum = jnp.zeros(shape, F32)
    cross_sum = jnp.zeros(shape, F32)
    for pair in range(pairs):
        here = block(pair)
        start = pair % half * N
        carried = dot(read, entry[pair // half, start : start + N, :])
        mix = local[:, here] + by_head(decay, pair, shape) * carried
        mixed[:, here] = mix
        z = gate[:, here].astype(F32)
        silu = z * sigmoid(z)
        silus[:, here] = silu
        product = mix * silu
        gated[:, here] = product
        square_sum += product * product
        cross_sum += product * (grad[:, here].astype(F32) * gain[:, here])
    scale = lax.rsqrt(jnp.sum(square_sum, axis=1, keepdims=True) * (1.0 / features) + EPS)
    cross = jnp.sum(cross_sum, axis=1, keepdims=True)
    factor = scale * scale * scale * cross * (1.0 / features)
    lane = iota(shape, 1)
    stats[...] = jnp.where(lane == 0, scale, jnp.where(lane == 1, factor, 0.0))
    scale_wide = jnp.broadcast_to(scale, shape)
    factor_wide = jnp.broadcast_to(factor, shape)
    for pair in range(pairs):
        here = block(pair)
        grad_gated = scale_wide * (grad[:, here].astype(F32) * gain[:, here]) - factor_wide * gated[:, here]
        weighted = by_head(decay, pair, shape) * (grad_gated * silus[:, here])
        start = pair % half * N
        states[pair // half, start : start + N, :] = dot(read, weighted.astype(BF16), (0, 0)).astype(BF16)
    end = half * N
    states[:, end : end + DEC_ROWS, :] = decs[...]
    mine[...] = states[core[0]]
    other[...] = states[1 - core[0]]


def back_kernel(
    core, mixed, conv, cols, rows_ref, small, gate, grad, gain, stats, own, got, grad_gate, grad_values, sums, grad_gain, grad_small, grad_vecs, entry
):
    length, features = mixed.shape
    pairs = features // LANES
    half = pairs // 2
    shape = (length, LANES)
    entry[core[0]] = own[...]
    entry[1 - core[0]] = got[...]
    write = conv[:, features : features + N]
    read = conv[:, features + N : features + 2 * N]
    scores = dot(read, write, (1, 1))
    square = (length, length)
    causal = iota(square, 0) >= iota(square, 1)
    scale = jnp.broadcast_to(stats[:, 0:1], shape)
    factor = jnp.broadcast_to(stats[:, 1:2], shape)
    decay = jnp.exp(cols[1])
    read_grad = jnp.zeros((length, N), F32)
    score_grad = jnp.zeros(square, F32)
    out_sums = jnp.zeros(shape, F32)
    in_sums = jnp.zeros(shape, F32)
    skip_sums = jnp.zeros(shape, F32)
    first = iota(shape, 1) < P_SIZE
    for pair in range(pairs):
        here = block(pair)
        start = pair % half * N
        z = gate[:, here].astype(F32)
        sig = sigmoid(z)
        silu = z * sig
        mix = mixed[:, here]
        product = mix * silu
        grads = grad[:, here].astype(F32)
        gain_row = gain[:, here]
        grad_gain[:, here] = jnp.sum(grads * (product * scale), axis=0, keepdims=True)
        grad_gated = scale * (grads * gain_row) - factor * product
        grad_mix = grad_gated * silu
        grad_gate[:, here] = (grad_gated * mix * (sig * (1.0 + z * (1.0 - sig)))).astype(BF16)
        values = conv[:, here]
        values_wide = values.astype(F32)
        skip = by_head(small[2:3, :], pair, (1, LANES))
        rounded = grad_mix.astype(BF16)
        inner = mix - skip * values_wide
        out_sums += head_sums(rounded.astype(F32) * inner, pair)
        skip_sums += head_sums(grad_mix * values_wide, pair)
        weighted = (by_head(decay, pair, shape) * grad_mix).astype(BF16)
        read_grad += dot(weighted, entry[pair // half, start : start + N, :], (1, 1))
        scaled = [head_weights(cols, rows_ref, 2 * pair + which, causal, scores) for which in range(2)]
        weight_grad = dot(rounded, apart(values), (1, 1))
        score_grad += weight_grad[:, 0:length] * scaled[0][0] + weight_grad[:, length:] * scaled[1][0]
        both = dot(jnp.concatenate([scaled[0][1], scaled[1][1]], axis=1), rounded, (0, 0))
        value_grad = jnp.where(first, both[0:length], both[length:])
        in_sums += head_sums(values_wide * value_grad, pair)
        grad_values[:, here] = value_grad + skip * grad_mix
    sums[0] = out_sums
    sums[1] = in_sums
    high, low = split(score_grad)
    read_grad += dot(high, write) + dot(low, write)
    write_grad = dot(high, read, (0, 0)) + dot(low, read, (0, 0))
    grad_vecs[...] = jnp.concatenate([write_grad, read_grad], axis=1)
    grad_small[...] = jnp.zeros_like(grad_small)
    grad_small[2:3, :] = jnp.sum(skip_sums, axis=0, keepdims=True)


def close_kernel(
    taps, sizes, place, x, halo, full, conv, slope, cols, rows_ref, small, decs, entry_own, entry_got, leave_own, leave_got,
    grad_values, grad_vecs, sums, grad_gain, grad_small, grad_x, back, ending, grad_dt, *rest
):
    parts = len(rest) - 6
    outs, (entry, leave, rows, slopes, whole, cut) = rest[:parts], rest[parts:]
    core, position_here = place[0], place[1]
    length, channels = x.shape
    features = grad_values.shape[1]
    pairs = features // LANES
    half = pairs // 2
    width, gain_width, heads_here = sizes
    heads = heads_here * parts
    shape = (length, LANES)
    entry[core] = entry_own[...]
    entry[1 - core] = entry_got[...]
    leave[core] = leave_own[...]
    leave[1 - core] = leave_got[...]
    fill_rows(rows, x, halo)
    slopes[...] = jnp.zeros_like(slopes)
    whole[...] = jnp.zeros_like(whole)
    write = conv[:, features : features + N]
    step = cols[0]
    running = cols[1]
    last = running[length - 1 : length, :]
    tail = jnp.exp(last - running) * step
    state_sums = jnp.zeros(shape, F32)
    end_sums = jnp.zeros((8, LANES), F32)
    write_grad = jnp.zeros((length, N), F32)

    def through_conv(position, grad_out):
        here = block(position)
        grad_pre = grad_out.astype(BF16).astype(F32) * slope[:, here]
        slopes[HALO : HALO + length, here] = grad_pre
        start = HALO - (taps - 1)
        for tap in range(taps):
            whole[tap : tap + 1, here] = jnp.sum(
                grad_pre * rows[start + tap : start + tap + length, here], axis=0, keepdims=True
            )
        whole[taps : taps + 1, here] = jnp.sum(grad_pre, axis=0, keepdims=True)
        total = jnp.zeros((HALO + length, LANES), F32)
        for tap in range(taps):
            ahead = taps - 1 - tap
            total += full[tap : tap + 1, here] * slopes[ahead : ahead + HALO + length, here]
        back[:, here] = total[0:HALO].astype(BF16)
        grad_x[:, here] = total[HALO:].astype(BF16)
        ending[:, here] = total[length:]

    for pair in range(pairs):
        here = block(pair)
        start = pair % half * N
        leaving = leave[pair // half, start : start + N, :]
        values = conv[:, here].astype(F32)
        tail_wide = by_head(tail, pair, shape)
        state_grad = tail_wide * dot(write, leaving)
        state_sums += head_sums(values * state_grad, pair)
        write_grad += dot((tail_wide * values).astype(BF16), leaving, (1, 1))
        entering = entry[pair // half, start : start + N, :].astype(F32)
        overlap = jnp.sum(leaving.astype(F32) * entering, axis=0, keepdims=True)
        end_sums += head_sums(jnp.broadcast_to(overlap, (8, LANES)), pair)
        through_conv(pair, grad_values[:, here] + state_grad)
    vecs = grad_vecs[...]
    vecs = vecs + jnp.concatenate([write_grad, jnp.zeros_like(write_grad)], axis=1)
    through_conv(pairs, vecs)

    into = sums[1] + state_sums
    change = sums[0] - into
    end_grad = jnp.sum(state_sums, axis=0, keepdims=True) + jnp.exp(last) * end_sums[0:1, :]
    square = (length, length)
    upper = (iota(square, 0) <= iota(square, 1)).astype(F32)
    log_grad = dot(upper, change, precision=HIGH) + end_grad
    rate = jnp.exp(small[1:2, :])
    raw_grad = (into / step - rate * log_grad) * (1.0 - jnp.exp(-step))
    grad_dt[...] = raw_grad[:, 0:heads]
    vectors = (
        jnp.sum(raw_grad, axis=0, keepdims=True),
        jnp.sum(-rate * step * log_grad, axis=0, keepdims=True),
        grad_small[2:3, :],
    )
    piece_width = cut.shape[2]
    for part in range(parts):
        base, shift = placement(part, width)
        piece = whole[:, base : base + piece_width + LANES]
        if shift:
            piece = pltpu.roll(piece, piece_width + LANES - shift, 1)
        cut[part] = piece[:, 0:piece_width]
        cut[part, taps + 1 : taps + 2, 0:gain_width] = grad_gain[:, part * gain_width : (part + 1) * gain_width]
        for number, vector in enumerate(vectors):
            row = pltpu.roll(vector, LANES - part * heads_here, 1) if part else vector
            cut[part, taps + 2 : taps + 3, block(number)] = row
    for distance in range(parts):
        outs[distance][...] = cut[lax.rem(position_here + distance, parts)]


def patch_kernel(whole, ending, back, out):
    rows = ending.shape[0]
    keep = out.shape[0] - rows
    patched = ending[...] + back[...].astype(F32)
    out[...] = jnp.concatenate([whole[0:keep, :].astype(F32), patched], axis=0).astype(BF16)


def unpack_kernel(terms, *refs):
    total = refs[0][...]
    for ref in refs[1:terms]:
        total = total + ref[...]
    cw, cb, dtb, al, sk, gain = refs[terms:]
    taps, width = cw.shape
    cw[...] = total[0:taps, 0:width]
    cb[...] = total[taps : taps + 1, 0:width]
    gain[...] = total[taps + 1 : taps + 2, 0 : gain.shape[1]]
    for number, ref in enumerate((dtb, al, sk)):
        ref[...] = total[taps + 2 : taps + 3, number * LANES : number * LANES + ref.shape[1]]


def add_kernel(*refs):
    total = refs[0][...]
    for ref in refs[1:-1]:
        total = total + ref[...]
    refs[-1][...] = total


def parts_of(message):
    end = message.shape[0] - DEC_ROWS
    half = end // N
    state = message[0:end, :].astype(F32).reshape(half, N, LANES)
    middle = end + DEC_ROWS // 2
    decay = message[end:middle, :].astype(F32) + message[middle:, :].astype(F32)
    return state, decay


def joined(first, second):
    state, decay = second
    half = state.shape[0]
    return decay[0:half].reshape(half, 1, LANES) * first[0] + state, decay * first[1]


def store(out, value):
    state, decay = value
    end = state.shape[0] * N
    middle = end + DEC_ROWS // 2
    out[0:end, :] = state.reshape(end, LANES).astype(BF16)
    high, low = split(decay)
    out[end:middle, :] = high
    out[middle:, :] = low


def meet_kernel(role, mine, got, out):
    later = role[0] == 1
    a, b = mine[...], got[...]
    first, second = jnp.where(later, b, a), jnp.where(later, a, b)
    store(out, joined(parts_of(first), parts_of(second)))


def join_kernel(first, second, out):
    store(out, joined(parts_of(first[...]), parts_of(second[...])))


def enter_kernel(role, entering, mine, got, own, send):
    later = role[0] == 1
    a, b = mine[...], got[...]
    before = parts_of(entering[...])
    state, _ = joined(before, parts_of(jnp.where(later, b, a)))
    after = state.reshape(own.shape)
    start = before[0].reshape(own.shape)
    own[...] = jnp.where(later, after, start).astype(BF16)
    send[...] = jnp.where(later, start, after).astype(BF16)


def call(kernel, outs, args, scratch=(), scalars=0, megabytes=16, flops=0, name=None):
    specs = [pl.BlockSpec(memory_space=pltpu.SMEM)] * scalars
    specs += [pl.BlockSpec(memory_space=pltpu.VMEM)] * (len(args) - scalars)
    moved = sum(a.size * a.dtype.itemsize for a in args)
    moved += sum(o.size * o.dtype.itemsize for o in outs)
    return pl.pallas_call(
        kernel,
        out_shape=outs,
        in_specs=specs,
        out_specs=[pl.BlockSpec(memory_space=pltpu.VMEM)] * len(outs),
        scratch_shapes=list(scratch),
        compiler_params=pltpu.CompilerParams(vmem_limit_bytes=megabytes << 20),
        cost_estimate=pl.CostEstimate(flops=flops, bytes_accessed=moved, transcendentals=0),
        name=name,
    )(*args)


def like(shape, dtype=F32):
    return jax.ShapeDtypeStruct(shape, dtype)


def shift(value, axis, route):
    count = lax.axis_size(axis)
    pairs = [(i, route(i)) for i in range(count)]
    return lax.ppermute(value, axis, [(i, j) for i, j in pairs if 0 <= j < count])


def entering_states(mine, other, core, reverse):
    chips = lax.axis_size("seq") // 2
    sign = -1 if reverse else 1
    role = 1 - core if reverse else core
    message = like(mine.shape, BF16)
    half = like((mine.shape[0] - DEC_ROWS, LANES), BF16)
    got = shift(other, "seq", lambda i: i ^ 1)
    chip = call(meet_kernel, [message], [role, mine, got], scalars=1, name="meet")[0]
    before = shift(chip, "seq", lambda i: i + 2 * sign)
    window = 1
    while window < chips - 1:
        longer = call(join_kernel, [message], [before, chip], name="join")[0]
        distance = window + 1
        far = shift(longer, "seq", lambda i: i + 2 * distance * sign)
        before = call(join_kernel, [message], [far, before], name="join")[0]
        window = 2 * window + 1
    own, send = call(
        enter_kernel, [half, half], [role, before, mine, got], scalars=1, name="enter"
    )
    return own, shift(send, "seq", lambda i: i ^ 1)


def shards(
    conv_input, gate_input, dt_raw, grad_output, conv_weight, conv_bias, dt_bias, a_log, skip, norm_gain
):
    x, gate, dt, grad = conv_input[0], gate_input[0], dt_raw[0], grad_output[0]
    length, channels = x.shape
    features = gate.shape[1]
    heads = dt.shape[1]
    pairs = heads // 2
    half = pairs // 2
    taps, width = conv_weight.shape
    gain_width = norm_gain.shape[0]
    heads_here = dt_bias.shape[0]
    parts = lax.axis_size("fsdp")
    devices = lax.axis_size("seq")
    sizes = (width, gain_width, heads_here)
    piece_width = -(-width // LANES) * LANES
    place_base = placement(parts - 1, width)[0]
    full_width = place_base + piece_width + LANES
    core = jnp.reshape(lax.axis_index("seq") % 2, (1,)).astype(jnp.int32)
    fsdp_index = jnp.reshape(lax.axis_index("fsdp"), (1,)).astype(jnp.int32)
    place = jnp.concatenate([core, fsdp_index])

    halo = shift(x[length - HALO :], "seq", lambda i: i + 1)
    piece = call(
        pack_kernel,
        [like((SMALL, piece_width))],
        [
            conv_weight,
            conv_bias.reshape(1, -1),
            dt_bias.reshape(1, -1),
            a_log.reshape(1, -1),
            skip.reshape(1, -1),
            norm_gain.reshape(1, -1),
        ],
        name="pack",
    )[0]
    pieces = lax.all_gather(piece, "fsdp")

    message = half * N + DEC_ROWS
    conv, full, gain, small, cols, rows, mine, other, decs = call(
        functools.partial(front_kernel, taps, sizes),
        [
            like((length, channels), BF16),
            like((SMALL, full_width)),
            like((1, features)),
            like((8, LANES)),
            like((2, length, LANES)),
            like((3, LANES, length)),
            like((message, LANES), BF16),
            like((message, LANES), BF16),
            like((2, DEC_ROWS, LANES), BF16),
        ],
        [core, x, halo, pieces, dt],
        [
            pltpu.VMEM((HALO + length, channels), F32),
            pltpu.VMEM((2, message, LANES), BF16),
            pltpu.VMEM((length, LANES), F32),
        ],
        scalars=1,
        name="front",
    )
    local, slope = call(
        functools.partial(intra_kernel, taps),
        [like((length, features)), like((length, channels))],
        [x, halo, full, conv, cols, rows, small],
        [pltpu.VMEM((HALO + length, channels), F32)],
        flops=2 * length * length * features,
        name="intra",
    )
    entry_own, entry_got = entering_states(mine, other, core, False)
    mixed, stats, mine, other = call(
        norm_kernel,
        [
            like((length, features)),
            like((length, LANES)),
            like((message, LANES), BF16),
            like((message, LANES), BF16),
        ],
        [core, local, conv, cols, gate, grad, gain, entry_own, entry_got, decs],
        [
            pltpu.VMEM((2, half * N, LANES), BF16),
            pltpu.VMEM((length, features), F32),
            pltpu.VMEM((length, features), F32),
            pltpu.VMEM((2, message, LANES), BF16),
        ],
        scalars=1,
        name="norm",
    )
    leave_own, leave_got = entering_states(mine, other, core, True)
    grad_gate, grad_values, sums, grad_gain, grad_small, grad_vecs = call(
        back_kernel,
        [
            like((length, features), BF16),
            like((length, features)),
            like((2, length, LANES)),
            like((1, features)),
            like((8, LANES)),
            like((length, LANES)),
        ],
        [core, mixed, conv, cols, rows, small, gate, grad, gain, stats, entry_own, entry_got],
        [pltpu.VMEM((2, half * N, LANES), BF16)],
        scalars=1,
        flops=6 * length * length * features,
        name="back",
    )
    grad_x, back, ending, grad_dt, *shares = call(
        functools.partial(close_kernel, taps, sizes),
        [
            like((length, channels), BF16),
            like((HALO, channels), BF16),
            like((HALO, channels)),
            like((length, heads)),
        ]
        + [like((SMALL, piece_width))] * parts,
        [
            place, x, halo, full, conv, slope, cols, rows, small, decs, entry_own, entry_got, leave_own, leave_got,
            grad_values, grad_vecs, sums, grad_gain, grad_small,
        ],
        [
            pltpu.VMEM((2, half * N, LANES), BF16),
            pltpu.VMEM((2, half * N, LANES), BF16),
            pltpu.VMEM((HALO + length, channels), F32),
            pltpu.VMEM((2 * HALO + length, channels), F32),
            pltpu.VMEM((SMALL, full_width), F32),
            pltpu.VMEM((parts, SMALL, piece_width), F32),
        ],
        scalars=1,
        megabytes=24,
        name="close",
    )
    piece_like = like((SMALL, piece_width))
    terms = [shares[0]]
    for distance in range(1, parts):
        terms.append(shift(shares[distance], "fsdp", lambda i: (i + distance) % parts))
    back = shift(back, "seq", lambda i: i - 1)
    total = call(add_kernel, [piece_like], terms, name="add")[0]
    total = call(
        add_kernel, [piece_like], [total, shift(total, "seq", lambda i: i ^ 1)], name="add"
    )[0]
    chips = devices // 2
    if chips <= 4:
        terms = [total] + [
            shift(total, "seq", lambda i: (i + 2 * distance) % devices) for distance in range(1, chips)
        ]
    else:
        terms = [lax.psum(total, "seq") * 0.5]
    outputs = call(
        functools.partial(unpack_kernel, len(terms)),
        [
            like((taps, width)),
            like((1, width)),
            like((1, heads_here)),
            like((1, heads_here)),
            like((1, heads_here)),
            like((1, gain_width)),
        ],
        terms,
        name="unpack",
    )
    grad_x = pl.pallas_call(
        patch_kernel,
        grid=(1,),
        out_shape=like((length, channels), BF16),
        in_specs=[
            pl.BlockSpec((2 * HALO, channels), lambda i: (length // (2 * HALO) - 1, 0)),
            pl.BlockSpec((HALO, channels), lambda i: (0, 0)),
            pl.BlockSpec((HALO, channels), lambda i: (0, 0)),
        ],
        out_specs=pl.BlockSpec((2 * HALO, channels), lambda i: (length // (2 * HALO) - 1, 0)),
        input_output_aliases={0: 0},
        name="patch",
    )(grad_x, ending, back)
    cw, cb, dtb, al, sk, gn = outputs
    return (
        grad_x[None],
        grad_gate[None],
        grad_dt[None],
        cw,
        cb.reshape(-1),
        dtb.reshape(-1),
        al.reshape(-1),
        sk.reshape(-1),
        gn.reshape(-1),
    )


def solution(mesh):
    tokens = P("fsdp", "seq", None)
    in_specs = (tokens,) * 4 + (P(None, "fsdp"),) + (P("fsdp"),) * 5
    out_specs = (tokens,) * 3 + (P(None, "fsdp"),) + (P("fsdp"),) * 5
    return jax.shard_map(shards, mesh=mesh, in_specs=in_specs, out_specs=out_specs, check_vma=False)
```

time: 561 us -> 123 us (0.22); the launches traced: 552 us -> 122 us
  waiting for transfers between devices: 342 us -> 44 us
  other arithmetic: 59.5 us -> 0.68 us
  matrix products: 36.4 us -> 0 us
  blocking collectives: 44.7 us -> 9.63 us
  local copies, waits for them, and re-layouts: 48.7 us -> 15.8 us
  Pallas kernels: 0 us -> 25.9 us
  starting transfers between devices: 3.95 us -> 25 us
  between operations: 16 us -> 0.93 us
    all_gather x2 -> x0, waiting for transfers between devices: 223 us -> none  [entering_2(): pieces = jax.tree.map(lambda part: lax.all_gather(part, axis), value)]
    psum x1 -> x0, waiting for transfers between devices: 118 us -> none  [shards(): lax.psum((local_grads[0], local_grads[1], local_grads[2], local_grads[3],...]
    ppermute x2 -> x17, waiting for transfers between devices: 0.01 us -> 44 us  [shift(): lax.ppermute(value, axis, [(i, j) for i, j in pairs if 0 <= j < count])]
    dot_general x12 -> x0, matrix products: 36.4 us -> none  [the longest x3 16.5 us: inner_part(): intra_out = jnp.einsum('hts,shp->thp', weights, values, precision=HIGH)]
    select_n x14 -> x0, other arithmetic: 26.9 us -> none  [turn(): jnp.where(position < mine, new, old)]
    pallas_call x0 -> x18, Pallas kernels: none -> 25.9 us  [the longest x17 24.3 us: call(): pl.pallas_call(kernel, out_shape=outs, in_specs=specs, out_specs=[pl.Bloc...]
    ppermute x2 -> x17, starting transfers between devices: 3.65 us -> 25 us  [shift(): lax.ppermute(value, axis, [(i, j) for i, j in pairs if 0 <= j < count])]
    all_gather x3 -> x1, blocking collectives: 27.6 us -> 9.63 us  [shards(): pieces = lax.all_gather(piece, 'fsdp')]
  transfers between devices with their start and end apart: 5 -> 17, of which waited for: 3 -> 11; matrix products, arithmetic and copies ran while one was open for 7% -> 2% of each run, Pallas kernels for 0% -> 9%
where the time goes in v1:
time: 123 us; the launch traced here: 122 us
  waiting for transfers between devices  44 us (36%)
  Pallas kernels  25.9 us (21%)
  starting transfers between devices  25 us (20%)
  local copies, waits for them, and re-layouts  15.8 us (13%)
  blocking collectives  9.63 us (8%)
    ppermute x17, waiting for transfers between devices, shift(): lax.ppermute(value, axis, [(i, j) for i, j in pairs if 0 <= j < count])  44 us
    ppermute x17, starting transfers between devices, shift(): lax.ppermute(value, axis, [(i, j) for i, j in pairs if 0 <= j < count])  25 us
    pallas_call x17, Pallas kernels, call(): pl.pallas_call(kernel, out_shape=outs, in_specs=specs, out_specs=[pl.Bloc...  24.3 us
    unnamed x50, local copies, waits for them, and re-layouts  14.3 us
    all_gather x1, blocking collectives, shards(): pieces = lax.all_gather(piece, 'fsdp')  9.63 us
  transfers between devices with their start and end apart: 17, of which 11 were waited for; matrix products, arithmetic and copies ran while one was open for 2% of the time, Pallas kernels for 9%

profile of v1, /device:TPU:0, one launch (start us, length us, event | category | flops | bytes accessed | tf_op | source)
XLA Modules:
  0.0 121.9 jit_solution(14286001836158284327)
XLA Ops:
  1.5 2.3 %collective-permute-start = (bf16[8,3712]{1,0:T(8,128)(2,1)S(1)}, bf16[8,3712]{1,0:T(8,128)(2,1)S(1)}, u32[]{:S(2)}, u32[]{:S(2)}) collective-permute-start(bf16[8,3712]{1,0:T(8,128)(2,1)S(1)} %slice_bitcast_fusion), channel_id=1, source_target_pairs={{0,1},{1,2},{2,3},{3,4},{4,5},{5,6},{6,7},{8,9},{9,10},{10,11},{11... | collective-permute-start | bytes 178184 | tf_op jit(solution)/shard_map/ppermute | solution.py:500
  8.8 9.6 %all-gather = f32[32,1024]{1,0:T(8,128)S(1)} all-gather(f32[8,1024]{1,0:T(8,128)S(1)} %pack.1), channel_id=2, replica_groups=mesh['fsdp'=4,'seq'=8] {'fsdp'}, dimensions={0}, use_global_device_ids=true | all-gather | bytes 163840 | tf_op jit(solution)/shard_map/all_gather | solution.py:561
  19.6 3.2 %front.1 = (bf16[128,3712]{1,0:T(8,128)(2,1)S(1)}, f32[8,3840]{1,0:T(8,128)S(1)}, f32[1,3584]{1,0:T(1,128)S(1)}, f32[8,128]{1,0:T(8,128)S(1)}, f32[2,128,128]{2,...) custom-call(s32[1]{0:T(128)} %bitcast.core.role, ...), custom_call_target="tpu_custom_call" | custom-call | bytes 3080196 | tf_op jit(solution)/shard_map/front/pallas_call | solution.py:481
  23.0 1.4 %collective-permute-done.1.got = bf16[928,128]{1,0:T(8,128)(2,1)S(1)} collective-permute-done((bf16[928,128]{1,0:T(8,128)(2,1)S(1)}, bf16[928,128]{1,0:T(8,128)(2,1)S(1)}, u32[]{:S(2)}, u32[]{:S(2)}) %collective-permute-start.1) | collective-permute-done | bytes 237600 | tf_op jit(solution)/shard_map/ppermute | solution.py:500
  24.5 3.5 %collective-permute-start.2 = (bf16[928,128]{1,0:T(8,128)(2,1)S(1)}, bf16[928,128]{1,0:T(8,128)(2,1)S(1)}, u32[]{:S(2)}, u32[]{:S(2)}) collective-permute-start(bf16[928,128]{1,0:T(8,128)(2,1)S(1)} %meet.2.second), channel_id=1, source_target_pairs={{0,2},{1,3},{2,4},{3,5},{4,6},{5,7},{8,10},{9,11},{10,12},{11,13},... | collective-permute-start | bytes 712712 | tf_op jit(solution)/shard_map/ppermute | solution.py:500
  28.1 5.3 %collective-permute-done.2.first.second = bf16[928,128]{1,0:T(8,128)(2,1)S(1)} collective-permute-done((bf16[928,128]{1,0:T(8,128)(2,1)S(1)}, bf16[928,128]{1,0:T(8,128)(2,1)S(1)}, u32[]{:S(2)}, u32[]{:S(2)}) %collective-permute-start.2) | collective-permute-done | bytes 237600 | tf_op jit(solution)/shard_map/ppermute | solution.py:500
  33.5 5.5 %collective-permute-start.3 = (bf16[928,128]{1,0:T(8,128)(2,1)S(1)}, bf16[928,128]{1,0:T(8,128)(2,1)S(1)}, u32[]{:S(2)}, u32[]{:S(2)}) collective-permute-start(bf16[928,128]{1,0:T(8,128)(2,1)S(1)} %join.4), channel_id=1, source_target_pairs={{0,4},{1,5},{2,6},{3,7},{8,12},{9,13},{10,14},{11,15},{16,20},{17,... | collective-permute-start | bytes 712712 | tf_op jit(solution)/shard_map/ppermute | solution.py:500
  39.0 4.5 %collective-permute-done.3.first = bf16[928,128]{1,0:T(8,128)(2,1)S(1)} collective-permute-done((bf16[928,128]{1,0:T(8,128)(2,1)S(1)}, bf16[928,128]{1,0:T(8,128)(2,1)S(1)}, u32[]{:S(2)}, u32[]{:S(2)}) %collective-permute-start.3) | collective-permute-done | bytes 237600 | tf_op jit(solution)/shard_map/ppermute | solution.py:500
  43.9 3.1 %intra.1 = (f32[128,3584]{1,0:T(8,128)S(1)}, f32[128,3712]{1,0:T(8,128)S(1)}) custom-call(bf16[128,3712]{1,0:T(8,128)(2,1)S(1)} %bitcast.21, bf16[8,3712]{1,0:T(8,128)(2,1)S(1)} %collective-permute-done.halo, f32[8,3840]{1,0:T(8,128)S(1)} %get-tuple-element.48.full, bf16[128,3712]{1,0:T(8,128)(2,1)S(1)} %get-tuple-element.49.conv, ...), custom_call_target="tpu_custom_call" | custom-call | flops 117440512 | bytes 6150144 | tf_op jit(solution)/shard_map/intra/pallas_call | solution.py:481
  48.3 2.3 %norm.1 = (f32[128,3584]{1,0:T(8,128)S(1)}, f32[128,128]{1,0:T(8,128)S(1)}, bf16[928,128]{1,0:T(8,128)(2,1)S(1)}, bf16[928,128]{1,0:T(8,128)(2,1)S(1)}) custom-call(s32[1]{0:T(128)} %bitcast.core.role, f32[128,3584]{1,0:T(8,128)S(1)} %get-tuple-element.59.local, bf16[128,3712]{1,0:T(8,128)(2,1)S(1)} %get-tuple-element.49.conv, ...), custom_call_target="tpu_custom_call" | custom-call | bytes 7616516 | tf_op jit(solution)/shard_map/norm/pallas_call | solution.py:481
  53.6 1.3 %collective-permute-start.6 = (bf16[928,128]{1,0:T(8,128)(2,1)S(1)}, bf16[928,128]{1,0:T(8,128)(2,1)S(1)}, u32[]{:S(2)}, u32[]{:S(2)}) collective-permute-start(bf16[928,128]{1,0:T(8,128)(2,1)S(1)} %meet.3.second), channel_id=1, source_target_pairs={{2,0},{3,1},{4,2},{5,3},{6,4},{7,5},{10,8},{11,9},{12,10},{13,11},... | collective-permute-start | bytes 712712 | tf_op jit(solution)/shard_map/ppermute | solution.py:500
  54.9 13.3 %collective-permute-done.6.first.second = bf16[928,128]{1,0:T(8,128)(2,1)S(1)} collective-permute-done((bf16[928,128]{1,0:T(8,128)(2,1)S(1)}, bf16[928,128]{1,0:T(8,128)(2,1)S(1)}, u32[]{:S(2)}, u32[]{:S(2)}) %collective-permute-start.6) | collective-permute-done | bytes 237600 | tf_op jit(solution)/shard_map/ppermute | solution.py:500
  68.3 1.5 %collective-permute-start.7 = (bf16[928,128]{1,0:T(8,128)(2,1)S(1)}, bf16[928,128]{1,0:T(8,128)(2,1)S(1)}, u32[]{:S(2)}, u32[]{:S(2)}) collective-permute-start(bf16[928,128]{1,0:T(8,128)(2,1)S(1)} %join.6), channel_id=1, source_target_pairs={{4,0},{5,1},{6,2},{7,3},{12,8},{13,9},{14,10},{15,11},{20,16},{21,... | collective-permute-start | bytes 712712 | tf_op jit(solution)/shard_map/ppermute | solution.py:500
  69.8 13.9 %collective-permute-done.7.first = bf16[928,128]{1,0:T(8,128)(2,1)S(1)} collective-permute-done((bf16[928,128]{1,0:T(8,128)(2,1)S(1)}, bf16[928,128]{1,0:T(8,128)(2,1)S(1)}, u32[]{:S(2)}, u32[]{:S(2)}) %collective-permute-start.7) | collective-permute-done | bytes 237600 | tf_op jit(solution)/shard_map/ppermute | solution.py:500
  86.5 1.5 %copy-done.8 = f32[128,3584]{1,0:T(8,128)S(1)} copy-done((f32[128,3584]{1,0:T(8,128)S(1)}, f32[128,3584]{1,0:T(8,128)}, u32[]{:S(2)}) %copy-start.8) | copy-done | bytes 1835032
  89.7 6.4 %back.1 = (bf16[128,3584]{1,0:T(8,128)(2,1)}, f32[128,3584]{1,0:T(8,128)S(1)}, f32[2,128,128]{2,1,0:T(8,128)S(1)}, f32[1,3584]{1,0:T(1,128)S(1)}, f32[8,128]{1,0:T(8,128)S(1)}, /*index=5*/f32[128,128]{1,0:T(8,128)S(1)}) custom-call(s32[1]{0:T(128)} %bitcast.core.role, f32[128,3584]{1,0:T(8,128)S(1)} %copy-done.8, ...), custom_call_target="tpu_custom_call" | custom-call | flops 352321536 | bytes 8458244 | tf_op jit(solution)/shard_map/back/pallas_call | solution.py:481
  96.1 7.1 %close.1 = (bf16[128,3712]{1,0:T(8,128)(2,1)}, bf16[8,3712]{1,0:T(8,128)(2,1)S(1)}, f32[8,3712]{1,0:T(8,128)S(1)}, f32[128,56]{1,0:T(8,128)S(1)}, f32[8,1024]{1,...) custom-call(s32[2]{0:T(128)S(1)} %pad_add_fusion.place, ...), custom_call_target="tpu_custom_call" | custom-call | bytes 8587272 | tf_op jit(solution)/shard_map/close/pallas_call | solution.py:481
  103.3 1.5 %collective-permute-start.10 = (f32[8,1024]{1,0:T(8,128)S(1)}, f32[8,1024]{1,0:T(8,128)S(1)}, u32[]{:S(2)}, u32[]{:S(2)}) collective-permute-start(f32[8,1024]{1,0:T(8,128)S(1)} %get-tuple-element.78), channel_id=1, source_target_pairs={{0,8},{8,16},{16,24},{24,0},{1,9},{9,17},{17,25},{25,1},{2,10},{10... | collective-permute-start | bytes 98312 | tf_op jit(solution)/shard_map/ppermute | solution.py:500
  105.3 2.4 %collective-permute-start.12 = (f32[8,1024]{1,0:T(8,128)S(1)}, f32[8,1024]{1,0:T(8,128)S(1)}, u32[]{:S(2)}, u32[]{:S(2)}) collective-permute-start(f32[8,1024]{1,0:T(8,128)S(1)} %get-tuple-element.80), channel_id=1, source_target_pairs={{0,24},{8,0},{16,8},{24,16},{1,25},{9,1},{17,9},{25,17},{2,26},{10... | collective-permute-start | bytes 98312 | tf_op jit(solution)/shard_map/ppermute | solution.py:500
  109.4 1.3 %collective-permute-start.9 = (bf16[8,3712]{1,0:T(8,128)(2,1)S(1)}, bf16[8,3712]{1,0:T(8,128)(2,1)S(1)}, u32[]{:S(2)}, u32[]{:S(2)}) collective-permute-start(bf16[8,3712]{1,0:T(8,128)(2,1)S(1)} %get-tuple-element.74), channel_id=1, source_target_pairs={{1,0},{2,1},{3,2},{4,3},{5,4},{6,5},{7,6},{9,8},{10,9},{11,10},{12... | collective-permute-start | bytes 178184 | tf_op jit(solution)/shard_map/ppermute | solution.py:500
  110.7 1.8 %collective-permute-start.16 = (f32[8,1024]{1,0:T(8,128)S(1)}, f32[8,1024]{1,0:T(8,128)S(1)}, u32[]{:S(2)}, u32[]{:S(2)}) collective-permute-start(f32[8,1024]{1,0:T(8,128)S(1)} %add.11.refs_0_), channel_id=1, source_target_pairs={{0,6},{1,7},{2,0},{3,1},{4,2},{5,3},{6,4},{7,5},{8,14},{9,15},{10,... | collective-permute-start | bytes 98312 | tf_op jit(solution)/shard_map/ppermute | solution.py:500
  112.5 2.5 %collective-permute-start.15 = (f32[8,1024]{1,0:T(8,128)S(1)}, f32[8,1024]{1,0:T(8,128)S(1)}, u32[]{:S(2)}, u32[]{:S(2)}) collective-permute-start(f32[8,1024]{1,0:T(8,128)S(1)} %add.11.refs_0_), channel_id=1, source_target_pairs={{0,4},{1,5},{2,6},{3,7},{4,0},{5,1},{6,2},{7,3},{8,12},{9,13},{10,... | collective-permute-start | bytes 98312 | tf_op jit(solution)/shard_map/ppermute | solution.py:500
  116.3 1.6 %patch.1 = bf16[128,3712]{1,0:T(8,128)(2,1)} custom-call(bf16[128,3712]{1,0:T(8,128)(2,1)} %get-tuple-element.72.whole, f32[8,3712]{1,0:T(8,128)} %copy-done.15, bf16[8,3712]{1,0:T(8,128)(2,1)} %copy-done.23), custom_call_target="tpu_custom_call", output_to_operand_aliasing={{}: (0, {})} | custom-call | tf_op jit(solution)/shard_map/patch/pallas_call | solution.py:684
  118.3 2.4 %collective-permute-done.14.refs_1_ = f32[8,1024]{1,0:T(8,128)S(1)} collective-permute-done((f32[8,1024]{1,0:T(8,128)S(1)}, f32[8,1024]{1,0:T(8,128)S(1)}, u32[]{:S(2)}, u32[]{:S(2)}) %collective-permute-start.14) | collective-permute-done | bytes 32800 | tf_op jit(solution)/shard_map/ppermute | solution.py:500
  (83 shorter events, 21.6 us)
Async XLA Ops:
  1.5 16.9 %collective-permute-start = (bf16[8,3712]{1,0:T(8,128)(2,1)S(1)}, bf16[8,3712]{1,0:T(8,128)(2,1)S(1)}, u32[]{:S(2)}, u32[]{:S(2)}) collective-permute-start(bf16[8,3712]{1,0:T(8,128)(2,1)S(1)} %slice_bitcast_fusion), channel_id=1, source_target_pairs={{0,1},{1,2},{2,3},{3,4},{4,5},{5,6},{6,7},{8,9},{9,10},{10,11},{11... | collective-permute-start | bytes 178184 | tf_op jit(solution)/shard_map/ppermute | solution.py:500
  19.6 24.3 %copy-start.1 = (bf16[1,128,3712]{2,1,0:T(8,128)(2,1)S(1)}, bf16[1,128,3712]{2,1,0:T(8,128)(2,1)}, u32[]{:S(2)}) copy-start(bf16[1,128,3712]{2,1,0:T(8,128)(2,1)} %param.10) | copy-start | bytes 2850820
  22.8 24.2 %copy-start.9 = (f32[3,128,128]{2,1,0:T(8,128)}, f32[3,128,128]{2,1,0:T(8,128)S(1)}, u32[]{:S(2)}) copy-start(f32[3,128,128]{2,1,0:T(8,128)S(1)} %get-tuple-element.51.rows_ref) | copy-start | bytes 589828
  22.8 24.2 %copy-start.11 = (f32[8,3840]{1,0:T(8,128)}, f32[8,3840]{1,0:T(8,128)S(1)}, u32[]{:S(2)}) copy-start(f32[8,3840]{1,0:T(8,128)S(1)} %get-tuple-element.48.full) | copy-start | bytes 368644
  22.8 25.5 %copy-start.16 = (f32[1,3584]{1,0:T(1,128)}, f32[1,3584]{1,0:T(1,128)S(1)}, u32[]{:S(2)}) copy-start(f32[1,3584]{1,0:T(1,128)S(1)} %get-tuple-element.60.gain) | copy-start | bytes 43012
  22.8 1.6 %collective-permute-start.1 = (bf16[928,128]{1,0:T(8,128)(2,1)S(1)}, bf16[928,128]{1,0:T(8,128)(2,1)S(1)}, u32[]{:S(2)}, u32[]{:S(2)}) collective-permute-start(bf16[928,128]{1,0:T(8,128)(2,1)S(1)} %get-tuple-element.56), channel_id=1, source_target_pairs={{0,1},{1,0},{2,3},{3,2},{4,5},{5,4},{6,7},{7,6},{8,9},{9,8},{10,11... | collective-permute-start | bytes 712712 | tf_op jit(solution)/shard_map/ppermute | solution.py:500
  24.5 8.8 %collective-permute-start.2 = (bf16[928,128]{1,0:T(8,128)(2,1)S(1)}, bf16[928,128]{1,0:T(8,128)(2,1)S(1)}, u32[]{:S(2)}, u32[]{:S(2)}) collective-permute-start(bf16[928,128]{1,0:T(8,128)(2,1)S(1)} %meet.2.second), channel_id=1, source_target_pairs={{0,2},{1,3},{2,4},{3,5},{4,6},{5,7},{8,10},{9,11},{10,12},{11,13},... | collective-permute-start | bytes 712712 | tf_op jit(solution)/shard_map/ppermute | solution.py:500
  33.5 14.8 %copy-start.2 = (bf16[1,128,3584]{2,1,0:T(8,128)(2,1)S(1)}, bf16[1,128,3584]{2,1,0:T(8,128)(2,1)}, u32[]{:S(2)}) copy-start(bf16[1,128,3584]{2,1,0:T(8,128)(2,1)} %param.11) | copy-start | bytes 2752516
  33.5 14.8 %copy-start.3 = (bf16[1,128,3584]{2,1,0:T(8,128)(2,1)S(1)}, bf16[1,128,3584]{2,1,0:T(8,128)(2,1)}, u32[]{:S(2)}) copy-start(bf16[1,128,3584]{2,1,0:T(8,128)(2,1)} %param.13) | copy-start | bytes 2752516
  33.5 10.1 %collective-permute-start.3 = (bf16[928,128]{1,0:T(8,128)(2,1)S(1)}, bf16[928,128]{1,0:T(8,128)(2,1)S(1)}, u32[]{:S(2)}, u32[]{:S(2)}) collective-permute-start(bf16[928,128]{1,0:T(8,128)(2,1)S(1)} %join.4), channel_id=1, source_target_pairs={{0,4},{1,5},{2,6},{3,7},{8,12},{9,13},{10,14},{11,15},{16,20},{17,... | collective-permute-start | bytes 712712 | tf_op jit(solution)/shard_map/ppermute | solution.py:500
  43.8 4.5 %collective-permute-start.4 = (bf16[896,128]{1,0:T(8,128)(2,1)S(1)}, bf16[896,128]{1,0:T(8,128)(2,1)S(1)}, u32[]{:S(2)}, u32[]{:S(2)}) collective-permute-start(bf16[896,128]{1,0:T(8,128)(2,1)S(1)} %get-tuple-element.58), channel_id=1, source_target_pairs={{0,1},{1,0},{2,3},{3,2},{4,5},{5,4},{6,7},{7,6},{8,9},{9,8},{10,11... | collective-permute-start | bytes 688136 | tf_op jit(solution)/shard_map/ppermute | solution.py:500
  51.8 1.6 %collective-permute-start.5 = (bf16[928,128]{1,0:T(8,128)(2,1)S(1)}, bf16[928,128]{1,0:T(8,128)(2,1)S(1)}, u32[]{:S(2)}, u32[]{:S(2)}) collective-permute-start(bf16[928,128]{1,0:T(8,128)(2,1)S(1)} %get-tuple-element.62), channel_id=1, source_target_pairs={{0,1},{1,0},{2,3},{3,2},{4,5},{5,4},{6,7},{7,6},{8,9},{9,8},{10,11... | collective-permute-start | bytes 712712 | tf_op jit(solution)/shard_map/ppermute | solution.py:500
  53.6 14.6 %collective-permute-start.6 = (bf16[928,128]{1,0:T(8,128)(2,1)S(1)}, bf16[928,128]{1,0:T(8,128)(2,1)S(1)}, u32[]{:S(2)}, u32[]{:S(2)}) collective-permute-start(bf16[928,128]{1,0:T(8,128)(2,1)S(1)} %meet.3.second), channel_id=1, source_target_pairs={{2,0},{3,1},{4,2},{5,3},{6,4},{7,5},{10,8},{11,9},{12,10},{13,11},... | collective-permute-start | bytes 712712 | tf_op jit(solution)/shard_map/ppermute | solution.py:500
  68.3 15.4 %collective-permute-start.7 = (bf16[928,128]{1,0:T(8,128)(2,1)S(1)}, bf16[928,128]{1,0:T(8,128)(2,1)S(1)}, u32[]{:S(2)}, u32[]{:S(2)}) collective-permute-start(bf16[928,128]{1,0:T(8,128)(2,1)S(1)} %join.6), channel_id=1, source_target_pairs={{4,0},{5,1},{6,2},{7,3},{12,8},{13,9},{14,10},{15,11},{20,16},{21,... | collective-permute-start | bytes 712712 | tf_op jit(solution)/shard_map/ppermute | solution.py:500
  85.3 10.9 %collective-permute-start.8 = (bf16[896,128]{1,0:T(8,128)(2,1)}, bf16[896,128]{1,0:T(8,128)(2,1)}, u32[]{:S(2)}, u32[]{:S(2)}) collective-permute-start(bf16[896,128]{1,0:T(8,128)(2,1)} %get-tuple-element.64), channel_id=1, source_target_pairs={{0,1},{1,0},{2,3},{3,2},{4,5},{5,4},{6,7},{7,6},{8,9},{9,8},{10,11... | collective-permute-start | bytes 688136 | tf_op jit(solution)/shard_map/ppermute | solution.py:500
  103.3 9.2 %copy-start.15 = (f32[8,3712]{1,0:T(8,128)}, f32[8,3712]{1,0:T(8,128)S(1)}, u32[]{:S(2)}) copy-start(f32[8,3712]{1,0:T(8,128)S(1)} %get-tuple-element.73.ending) | copy-start | bytes 356356
  103.3 4.9 %collective-permute-start.10 = (f32[8,1024]{1,0:T(8,128)S(1)}, f32[8,1024]{1,0:T(8,128)S(1)}, u32[]{:S(2)}, u32[]{:S(2)}) collective-permute-start(f32[8,1024]{1,0:T(8,128)S(1)} %get-tuple-element.78), channel_id=1, source_target_pairs={{0,8},{8,16},{16,24},{24,0},{1,9},{9,17},{17,25},{25,1},{2,10},{10... | collective-permute-start | bytes 98312 | tf_op jit(solution)/shard_map/ppermute | solution.py:500
  104.8 3.9 %collective-permute-start.11 = (f32[8,1024]{1,0:T(8,128)S(1)}, f32[8,1024]{1,0:T(8,128)S(1)}, u32[]{:S(2)}, u32[]{:S(2)}) collective-permute-start(f32[8,1024]{1,0:T(8,128)S(1)} %get-tuple-element.79), channel_id=1, source_target_pairs={{0,16},{8,24},{16,0},{24,8},{1,17},{9,25},{17,1},{25,9},{2,18},{10... | collective-permute-start | bytes 98312 | tf_op jit(solution)/shard_map/ppermute | solution.py:500
  105.3 4.0 %collective-permute-start.12 = (f32[8,1024]{1,0:T(8,128)S(1)}, f32[8,1024]{1,0:T(8,128)S(1)}, u32[]{:S(2)}, u32[]{:S(2)}) collective-permute-start(f32[8,1024]{1,0:T(8,128)S(1)} %get-tuple-element.80), channel_id=1, source_target_pairs={{0,24},{8,0},{16,8},{24,16},{1,25},{9,1},{17,9},{25,17},{2,26},{10... | collective-permute-start | bytes 98312 | tf_op jit(solution)/shard_map/ppermute | solution.py:500
  109.3 1.4 %collective-permute-start.13 = (f32[8,1024]{1,0:T(8,128)S(1)}, f32[8,1024]{1,0:T(8,128)S(1)}, u32[]{:S(2)}, u32[]{:S(2)}) collective-permute-start(f32[8,1024]{1,0:T(8,128)S(1)} %add.10.refs_0_), channel_id=1, source_target_pairs={{0,1},{1,0},{2,3},{3,2},{4,5},{5,4},{6,7},{7,6},{8,9},{9,8},{10,11... | collective-permute-start | bytes 98312 | tf_op jit(solution)/shard_map/ppermute | solution.py:500
  109.4 6.3 %collective-permute-start.9 = (bf16[8,3712]{1,0:T(8,128)(2,1)S(1)}, bf16[8,3712]{1,0:T(8,128)(2,1)S(1)}, u32[]{:S(2)}, u32[]{:S(2)}) collective-permute-start(bf16[8,3712]{1,0:T(8,128)(2,1)S(1)} %get-tuple-element.74), channel_id=1, source_target_pairs={{1,0},{2,1},{3,2},{4,3},{5,4},{6,5},{7,6},{9,8},{10,9},{11,10},{12... | collective-permute-start | bytes 178184 | tf_op jit(solution)/shard_map/ppermute | solution.py:500
  110.7 7.2 %collective-permute-start.16 = (f32[8,1024]{1,0:T(8,128)S(1)}, f32[8,1024]{1,0:T(8,128)S(1)}, u32[]{:S(2)}, u32[]{:S(2)}) collective-permute-start(f32[8,1024]{1,0:T(8,128)S(1)} %add.11.refs_0_), channel_id=1, source_target_pairs={{0,6},{1,7},{2,0},{3,1},{4,2},{5,3},{6,4},{7,5},{8,14},{9,15},{10,... | collective-permute-start | bytes 98312 | tf_op jit(solution)/shard_map/ppermute | solution.py:500
  112.5 5.8 %collective-permute-start.15 = (f32[8,1024]{1,0:T(8,128)S(1)}, f32[8,1024]{1,0:T(8,128)S(1)}, u32[]{:S(2)}, u32[]{:S(2)}) collective-permute-start(f32[8,1024]{1,0:T(8,128)S(1)} %add.11.refs_0_), channel_id=1, source_target_pairs={{0,4},{1,5},{2,6},{3,7},{4,0},{5,1},{6,2},{7,3},{8,12},{9,13},{10,... | collective-permute-start | bytes 98312 | tf_op jit(solution)/shard_map/ppermute | solution.py:500
  115.0 5.7 %collective-permute-start.14 = (f32[8,1024]{1,0:T(8,128)S(1)}, f32[8,1024]{1,0:T(8,128)S(1)}, u32[]{:S(2)}, u32[]{:S(2)}) collective-permute-start(f32[8,1024]{1,0:T(8,128)S(1)} %add.11.refs_0_), channel_id=1, source_target_pairs={{0,2},{1,3},{2,4},{3,5},{4,6},{5,7},{6,0},{7,1},{8,10},{9,11},{10,... | collective-permute-start | bytes 98312 | tf_op jit(solution)/shard_map/ppermute | solution.py:500
  (17 other events, 32.1 us)

commit v2 on v1

v2 whole, which is shorter than its diff:
```python
import functools

import jax
import jax.numpy as jnp
from jax import lax
from jax.experimental import pallas as pl
from jax.experimental.pallas import tpu as pltpu
from jax.sharding import PartitionSpec as P

P_SIZE = 64
N = 64
EPS = 1e-05
LANES = 2 * P_SIZE
HALO = 8
SMALL = 8
STREAMS = 2
FOLDS = 4
BACK_ROWS = 16
CUT = 16
DEC_ROWS = 16
F32, BF16 = jnp.float32, jnp.bfloat16
HIGH = lax.Precision.HIGHEST


def dot(a, b, over=(1, 0), precision=None):
    return lax.dot_general(
        a, b, (((over[0],), (over[1],)), ((), ())), precision=precision, preferred_element_type=F32
    )


def here_at():
    index = lax.axis_index("seq")
    return lax.rem(index, 2), lax.div(index, 2), lax.axis_index("fsdp")


def iota(shape, axis):
    return lax.broadcasted_iota(jnp.int32, shape, axis)


def sigmoid(x):
    return 0.5 * jnp.tanh(0.5 * x) + 0.5


def split(x):
    high = x.astype(BF16)
    return high, (x - high.astype(F32)).astype(BF16)


def block(position):
    return slice(position * LANES, (position + 1) * LANES)


def by_head(columns, pair, shape):
    first = jnp.broadcast_to(columns[:, 2 * pair : 2 * pair + 1], shape)
    second = jnp.broadcast_to(columns[:, 2 * pair + 1 : 2 * pair + 2], shape)
    return jnp.where(iota(shape, 1) < P_SIZE, first, second)


def apart(pair_block):
    first = iota(pair_block.shape, 1) < P_SIZE
    zero = jnp.zeros_like(pair_block)
    return jnp.concatenate(
        [jnp.where(first, pair_block, zero), jnp.where(first, zero, pair_block)], axis=0
    )


def head_sums(product, pair):
    shape = (LANES, LANES)
    pick = (iota(shape, 1) == 2 * pair + (iota(shape, 0) >= P_SIZE).astype(jnp.int32)).astype(BF16)
    high, low = split(product)
    return dot(jnp.concatenate([high, low], axis=1), jnp.concatenate([pick, pick], axis=0))


def before_silu(rows, full, cols, taps, length):
    start = HALO - (taps - 1)
    total = full[taps : taps + 1, cols] + full[0:1, cols] * rows[start : start + length, cols]
    for tap in range(1, taps):
        total = total + full[tap : tap + 1, cols] * rows[start + tap : start + tap + length, cols]
    return total


def open_kernel(x, dt, cw, cb, dtb, al, sk, gain, halo, out, own, late, raw, *rest):
    held, sems = rest[:-1], rest[-1]
    ending = x.at[pl.ds(x.shape[0] - late.shape[0], late.shape[0])]
    copies = [
        pltpu.make_async_copy(source, target, sems.at[number])
        for number, (source, target) in enumerate(
            zip((cw, cb, dtb, al, sk, gain, dt, ending), held + (raw, late))
        )
    ]
    for copy in copies:
        copy.start()
    out[...] = jnp.zeros_like(out)
    for copy in copies:
        copy.wait()
    halo[...] = late[...].astype(F32)[HALO:].astype(BF16)
    cw, cb, dtb, al, sk, gain = held
    taps, width = cw.shape
    out[0:taps, 0:width] = cw[...]
    out[taps : taps + 1, 0:width] = cb[...]
    out[taps + 1 : taps + 2, 0 : gain.shape[0]] = gain[...].reshape(1, -1)
    for number, ref in enumerate((dtb, al, sk)):
        out[taps + 2 : taps + 3, number * LANES : number * LANES + ref.shape[1]] = ref[...]
    own[0:SMALL, :] = out[...]
    own[SMALL:, :] = jnp.zeros((SMALL, own.shape[1]), F32)
    for group in range(raw.shape[0] // SMALL):
        own[SMALL:, block(group)] = raw[group * SMALL : (group + 1) * SMALL, :]


def placement(position, width):
    start = position * width
    base = start // LANES * LANES
    return base, start - base


def state_rows(pair, half):
    pair = pair % half
    return [slice((cut * half + pair) * CUT, (cut * half + pair + 1) * CUT) for cut in range(N // CUT)]


def put_state(states, pair, half, value):
    for cut, rows in enumerate(state_rows(pair, half)):
        states[rows, :] = value[cut * CUT : (cut + 1) * CUT]


def get_state(states, pair, half):
    return jnp.concatenate([states[rows, :] for rows in state_rows(pair, half)], axis=0)


def hand_out(states, decs, core, mine, other):
    end = states.shape[1] - DEC_ROWS
    states[:, end:, :] = decs[...]
    mine[...] = states[core]
    other[...] = states[1 - core]


def pack_decays(decays):
    high, low = split(decays)
    group = iota(decays.shape, 1) // (P_SIZE // 2)
    return jnp.where(lax.rem(group, 2) == 0, high.astype(F32), low.astype(F32)).astype(BF16)


def unpack_decays(packed):
    value = packed.astype(F32)
    group = iota(value.shape, 1) // (P_SIZE // 2)
    ahead = pltpu.roll(value, LANES - P_SIZE // 2, 1)
    behind = pltpu.roll(value, P_SIZE // 2, 1)
    return value + jnp.where(lax.rem(group, 2) == 0, ahead, behind)


def gather_kernel(taps, sizes, parts, length, own, *refs):
    given, refs = refs[: parts - 1], refs[parts - 1 :]
    full, gain, small, cols, rows_out, decs, wide, pieces = refs
    mine_at = here_at()[2]
    piece_width = pieces.shape[2]
    pieces[mine_at] = own[0:SMALL, :]
    for distance in range(1, parts):
        pieces[lax.rem(mine_at + parts - distance, parts)] = given[distance - 1][...]
    width, gain_width, heads_here = sizes
    heads = heads_here * parts
    half = heads // 4
    full[...] = jnp.zeros_like(full)
    small[...] = jnp.zeros_like(small)
    wide[...] = jnp.zeros_like(wide)
    for group in range(heads // SMALL):
        wide[group * SMALL : (group + 1) * SMALL, :] = own[SMALL:, block(group)]
    for part in range(parts):
        base, shift = placement(part, width)
        piece = jnp.concatenate([pieces[part], jnp.zeros((SMALL, LANES), F32)], axis=1)
        if shift:
            piece = pltpu.roll(piece, shift, 1)
        full[:, base : base + piece_width + LANES] += piece
        gain[:, part * gain_width : (part + 1) * gain_width] = pieces[
            part, taps + 1 : taps + 2, 0:gain_width
        ]
        for number in range(3):
            row = pieces[part, taps + 2 : taps + 3, block(number)]
            if part:
                row = pltpu.roll(row, part * heads_here, 1)
            small[number : number + 1, :] += row
    raw = wide[...].T + small[0:1, :]
    step = jnp.maximum(raw, 0.0) + jnp.log1p(jnp.exp(-jnp.abs(raw)))
    logs = -jnp.exp(small[1:2, :]) * step
    square = (length, length)
    lower = (iota(square, 0) >= iota(square, 1)).astype(F32)
    running = dot(lower, logs, precision=HIGH)
    running_t = running.T
    step_t = step.T
    last = jnp.broadcast_to(running_t[:, length - 1 : length], running_t.shape)
    cols[0] = step
    cols[1] = running
    rows_out[0] = step_t
    rows_out[1] = running_t
    rows_out[2] = jnp.exp(last - running_t) * step_t
    wide[...] = jnp.exp(last)[:, 0:LANES]
    first = iota((half, LANES), 1) < P_SIZE
    for side in range(2):
        even = wide[pl.ds(2 * half * side, half, stride=2), :]
        odd = wide[pl.ds(2 * half * side + 1, half, stride=2), :]
        decays = jnp.where(first, even, odd)
        decs[side] = pack_decays(
            jnp.concatenate([decays, jnp.zeros((DEC_ROWS - half, LANES), F32)], axis=0)
        )


def side_block(pair):
    return pl.ds(pl.multiple_of(pair * LANES, LANES), LANES)


def front_side(taps, side, rows, full, tails, decs, write_t, conv, out):
    length = conv.shape[0]
    half = (out.shape[0] - DEC_ROWS) // N
    scale = tails[2, pl.ds(side * 2 * half, 2 * half), :]
    for pair in range(half):
        here = side_block(side * half + pair)
        pre = before_silu(rows, full, here, taps, length)
        value = (pre * sigmoid(pre)).astype(BF16)
        conv[:, here] = value
        scaled = jnp.concatenate(
            [
                (write_t * scale[2 * pair + which : 2 * pair + which + 1, :]).astype(BF16)
                for which in range(2)
            ],
            axis=1,
        )
        put_state(out, pair, half, dot(scaled, apart(value)).astype(BF16))
    out[half * N :, :] = decs[side]


def front_kernel(taps, lifted, halo, full, tails, decs, rows, conv, write_out, other):
    core = here_at()[0]
    length, channels = conv.shape
    rows[0:HALO, :] = halo[...].astype(F32)
    here = block(channels // LANES - 1)
    pre = before_silu(rows, full, here, taps, length)
    vectors = (pre * sigmoid(pre)).astype(BF16)
    conv[:, here] = vectors
    write_t = vectors.astype(F32).T[0:N, :]
    write_out[...] = write_t
    front_side(taps, 1 - core, rows, full, tails, decs, write_t, conv, other)


def front_own_kernel(taps, conv_in, rows, full, tails, decs, write_t, conv, mine):
    front_side(taps, here_at()[0], rows, full, tails, decs, write_t[...], conv, mine)


def head_weights(cols, rows_ref, head, causal, scores):
    gap = cols[1, :, head : head + 1] - rows_ref[1, head : head + 1, :]
    scaled = jnp.exp(jnp.where(causal, gap, -1e30)) * rows_ref[0, head : head + 1, :]
    return scaled, (scaled * scores).astype(BF16)


def intra_kernel(taps, rows, full, conv, cols, rows_ref, small, local, slope):
    length, channels = conv.shape
    features = local.shape[1]
    pairs = features // LANES
    write = conv[:, features : features + N]
    read = conv[:, features + N : features + 2 * N]
    scores = dot(read, write, (1, 1))
    square = (length, length)
    causal = iota(square, 0) >= iota(square, 1)
    for pair in range(pairs):
        weights = jnp.concatenate(
            [head_weights(cols, rows_ref, 2 * pair + which, causal, scores)[1] for which in range(2)],
            axis=1,
        )
        values = conv[:, block(pair)]
        skip = by_head(small[2:3, :], pair, (1, LANES))
        local[:, block(pair)] = dot(weights, apart(values)) + skip * values.astype(F32)
    for position in range(channels // LANES):
        here = block(position)
        pre = before_silu(rows, full, here, taps, length)
        gate = sigmoid(pre)
        slope[:, here] = gate * (1.0 + pre * (1.0 - gate))


def side_columns(columns, side, half):
    return pltpu.roll(columns, lax.rem(LANES - 2 * half * side, LANES), 1)


def mix_side(side, local, conv, cols, gate, grad, gain, entry, mixed, gated, silus):
    length, features = local.shape
    half = features // LANES // 2
    shape = (length, LANES)
    read = conv[:, features + N : features + 2 * N]
    decay = side_columns(jnp.exp(cols[1]), side, half)
    square_sum = jnp.zeros(shape, F32)
    cross_sum = jnp.zeros(shape, F32)
    for pair in range(half):
        here = side_block(side * half + pair)
        carried = dot(read, get_state(entry, pair, half))
        mix = local[:, here] + by_head(decay, pair, shape) * carried
        mixed[:, here] = mix
        z = gate[:, here].astype(F32)
        silu = z * sigmoid(z)
        silus[:, here] = silu
        product = mix * silu
        gated[:, here] = product
        square_sum += product * product
        cross_sum += product * (grad[:, here].astype(F32) * gain[:, here])
    return square_sum, cross_sum


def norm_own_kernel(local, conv, cols, gate, grad, gain, entry, mixed, gated, silus, sums):
    square, cross = mix_side(
        here_at()[0], local, conv, cols, gate, grad, gain, entry, mixed, gated, silus
    )
    sums[0] = square
    sums[1] = cross


def back_state_side(side, stats, conv, cols, grad, gain, gated, silus, decs, out):
    length, features = gated.shape
    half = features // LANES // 2
    shape = (length, LANES)
    read = conv[:, features + N : features + 2 * N]
    decay = side_columns(jnp.exp(cols[1]), side, half)
    scale = jnp.broadcast_to(stats[:, 0:1], shape)
    factor = jnp.broadcast_to(stats[:, 1:2], shape)
    for pair in range(half):
        here = side_block(side * half + pair)
        grad_gated = scale * (grad[:, here].astype(F32) * gain[:, here]) - factor * gated[:, here]
        weighted = by_head(decay, pair, shape) * (grad_gated * silus[:, here])
        put_state(out, pair, half, dot(read, weighted.astype(BF16), (0, 0)).astype(BF16))
    out[half * N :, :] = decs[side]


def norm_kernel(
    mixed_in, gated_in, silus_in, local, conv, cols, gate, grad, gain, entry, sums, decs, mixed, gated, silus, stats, other
):
    length, features = local.shape
    side = 1 - here_at()[0]
    square, cross = mix_side(side, local, conv, cols, gate, grad, gain, entry, mixed, gated, silus)
    square = jnp.sum(square + sums[0], axis=1, keepdims=True)
    cross = jnp.sum(cross + sums[1], axis=1, keepdims=True)
    scale = lax.rsqrt(square * (1.0 / features) + EPS)
    factor = scale * scale * scale * cross * (1.0 / features)
    lane = iota((length, LANES), 1)
    values = jnp.where(lane == 0, scale, jnp.where(lane == 1, factor, 0.0))
    stats[...] = values
    back_state_side(side, values, conv, cols, grad, gain, gated, silus, decs, other)


def norm_last_kernel(stats, conv, cols, grad, gain, gated, silus, decs, mine):
    back_state_side(here_at()[0], stats[...], conv, cols, grad, gain, gated, silus, decs, mine)


def gate_kernel(
    mixed, conv, cols, small, gate, grad, gain, stats, own, got, grad_gate, grad_mixed, sums, grad_gain, grad_small, grad_read, entry
):
    core = here_at()[0]
    length, features = mixed.shape
    pairs = features // LANES
    half = pairs // 2
    shape = (length, LANES)
    entry[core] = own[...]
    entry[1 - core] = got[...]
    scale = jnp.broadcast_to(stats[:, 0:1], shape)
    factor = jnp.broadcast_to(stats[:, 1:2], shape)
    decay = jnp.exp(cols[1])
    read_grad = jnp.zeros((length, N), F32)
    out_sums = jnp.zeros(shape, F32)
    skip_sums = jnp.zeros(shape, F32)
    for pair in range(pairs):
        here = block(pair)
        z = gate[:, here].astype(F32)
        sig = sigmoid(z)
        silu = z * sig
        mix = mixed[:, here]
        product = mix * silu
        grads = grad[:, here].astype(F32)
        grad_gain[:, here] = jnp.sum(grads * (product * scale), axis=0, keepdims=True)
        grad_gated = scale * (grads * gain[:, here]) - factor * product
        grad_mix = grad_gated * silu
        grad_mixed[:, here] = grad_mix
        grad_gate[:, here] = (grad_gated * mix * (sig * (1.0 + z * (1.0 - sig)))).astype(BF16)
        values = conv[:, here].astype(F32)
        skip = by_head(small[2:3, :], pair, (1, LANES))
        rounded = grad_mix.astype(BF16).astype(F32)
        out_sums += head_sums(rounded * (mix - skip * values), pair)
        skip_sums += head_sums(grad_mix * values, pair)
        weighted = (by_head(decay, pair, shape) * grad_mix).astype(BF16)
        read_grad += dot(weighted, get_state(entry.at[pair // half], pair, half), (1, 1))
    sums[...] = out_sums
    grad_read[...] = jnp.concatenate([jnp.zeros_like(read_grad), read_grad], axis=1)
    grad_small[...] = jnp.zeros_like(grad_small)
    grad_small[2:3, :] = jnp.sum(skip_sums, axis=0, keepdims=True)


def back_kernel(grad_mixed, conv, cols, rows_ref, small, grad_read, grad_values, sums, grad_vecs):
    length, features = grad_mixed.shape
    pairs = features // LANES
    shape = (length, LANES)
    write = conv[:, features : features + N]
    read = conv[:, features + N : features + 2 * N]
    scores = dot(read, write, (1, 1))
    square = (length, length)
    causal = iota(square, 0) >= iota(square, 1)
    score_grad = jnp.zeros(square, F32)
    in_sums = jnp.zeros(shape, F32)
    first = iota(shape, 1) < P_SIZE
    for pair in range(pairs):
        here = block(pair)
        grad_mix = grad_mixed[:, here]
        values = conv[:, here]
        rounded = grad_mix.astype(BF16)
        scaled = [head_weights(cols, rows_ref, 2 * pair + which, causal, scores) for which in range(2)]
        weight_grad = dot(rounded, apart(values), (1, 1))
        score_grad += weight_grad[:, 0:length] * scaled[0][0] + weight_grad[:, length:] * scaled[1][0]
        both = dot(jnp.concatenate([scaled[0][1], scaled[1][1]], axis=1), rounded, (0, 0))
        value_grad = jnp.where(first, both[0:length], both[length:])
        in_sums += head_sums(values.astype(F32) * value_grad, pair)
        skip = by_head(small[2:3, :], pair, (1, LANES))
        grad_values[:, here] = value_grad + skip * grad_mix
    sums[...] = in_sums
    high, low = split(score_grad)
    read_grad = dot(high, write) + dot(low, write)
    write_grad = dot(high, read, (0, 0)) + dot(low, read, (0, 0))
    grad_vecs[...] = grad_read[...] + jnp.concatenate([write_grad, read_grad], axis=1)


def through_taps(taps, full, slopes, cols, start, count):
    total = full[0:1, cols] * slopes[start + taps - 1 : start + taps - 1 + count, cols]
    for tap in range(1, taps):
        ahead = start + taps - 1 - tap
        total = total + full[tap : tap + 1, cols] * slopes[ahead : ahead + count, cols]
    return total


def through_conv(taps, here, grad_out, rows, slope, slopes, whole):
    length = grad_out.shape[0]
    grad_pre = grad_out.astype(BF16).astype(F32) * slope[:, here]
    slopes[HALO : HALO + length, here] = grad_pre
    start = HALO - (taps - 1)
    for tap in range(taps):
        whole[tap : tap + 1, here] = jnp.sum(
            grad_pre * rows[start + tap : start + tap + length, here], axis=0, keepdims=True
        )
    whole[taps : taps + 1, here] = jnp.sum(grad_pre, axis=0, keepdims=True)


def close_side(taps, side, rows, conv, slope, cols, entry, leave, grad_values, slopes, whole):
    length, features = grad_values.shape
    half = features // LANES // 2
    shape = (length, LANES)
    write = conv[:, features : features + N]
    running = cols[1]
    tail = side_columns(jnp.exp(running[length - 1 : length, :] - running) * cols[0], side, half)
    state_sums = jnp.zeros(shape, F32)
    end_sums = jnp.zeros((8, LANES), F32)
    write_grad = jnp.zeros((length, N), F32)
    for pair in range(half):
        here = side_block(side * half + pair)
        leaving = get_state(leave, pair, half)
        values = conv[:, here].astype(F32)
        tail_wide = by_head(tail, pair, shape)
        state_grad = tail_wide * dot(write, leaving)
        state_sums += head_sums(values * state_grad, pair)
        write_grad += dot((tail_wide * values).astype(BF16), leaving, (1, 1))
        entering = get_state(entry, pair, half).astype(F32)
        overlap = jnp.sum(leaving.astype(F32) * entering, axis=0, keepdims=True)
        end_sums += head_sums(jnp.broadcast_to(overlap, (8, LANES)), pair)
        through_conv(taps, here, grad_values[:, here] + state_grad, rows, slope, slopes, whole)
    back = 2 * half * side
    return pltpu.roll(state_sums, back, 1), pltpu.roll(end_sums, back, 1), write_grad


def close_own_kernel(
    taps, rows, conv, slope, cols, entry, leave, grad_values, slopes, whole, state_out, end_out, write_out
):
    length, channels = conv.shape
    slopes[0:HALO, :] = jnp.zeros((HALO, channels), F32)
    slopes[HALO + length :, :] = jnp.zeros((HALO, channels), F32)
    whole[...] = jnp.zeros_like(whole)
    state_sums, end_sums, write_grad = close_side(
        taps, here_at()[0], rows, conv, slope, cols, entry, leave, grad_values, slopes, whole
    )
    state_out[...] = state_sums
    end_out[...] = end_sums
    write_out[...] = jnp.concatenate([write_grad, jnp.zeros_like(write_grad)], axis=1)


def close_kernel(
    taps, sizes, slopes_in, whole_in, rows, conv, slope, cols, small, entry, leave, grad_values, grad_vecs, out_sums, in_sums,
    grad_gain, grad_small, state_in, end_in, write_in, slopes, whole, grad_dt, *rest
):
    outs, cut = rest[:-1], rest[-1]
    parts = len(outs)
    core, _, position_here = here_at()
    length, channels = conv.shape
    width, gain_width, heads_here = sizes
    heads = heads_here * parts
    step = cols[0]
    last = cols[1, length - 1 : length, :]
    state_sums, end_sums, write_grad = close_side(
        taps, 1 - core, rows, conv, slope, cols, entry, leave, grad_values, slopes, whole
    )
    state_sums = state_sums + state_in[...]
    end_sums = end_sums + end_in[...]
    vecs = grad_vecs[...] + write_in[...]
    vecs = vecs + jnp.concatenate([write_grad, jnp.zeros_like(write_grad)], axis=1)
    through_conv(taps, block(channels // LANES - 1), vecs, rows, slope, slopes, whole)

    into = in_sums[...] + state_sums
    change = out_sums[...] - into
    end_grad = jnp.sum(state_sums, axis=0, keepdims=True) + jnp.exp(last) * end_sums[0:1, :]
    square = (length, length)
    upper = (iota(square, 0) <= iota(square, 1)).astype(F32)
    log_grad = dot(upper, change, precision=HIGH) + end_grad
    rate = jnp.exp(small[1:2, :])
    raw_grad = (into / step - rate * log_grad) * (1.0 - jnp.exp(-step))
    grad_dt[...] = raw_grad.T[0:heads, :]
    vectors = (
        jnp.sum(raw_grad, axis=0, keepdims=True),
        jnp.sum(-rate * step * log_grad, axis=0, keepdims=True),
        grad_small[2:3, :],
    )
    piece_width = cut.shape[2]
    for part in range(parts):
        base, shift = placement(part, width)
        piece = whole[:, base : base + piece_width + LANES]
        if shift:
            piece = pltpu.roll(piece, piece_width + LANES - shift, 1)
        cut[part] = piece[:, 0:piece_width]
        cut[part, taps + 1 : taps + 2, 0:gain_width] = grad_gain[:, part * gain_width : (part + 1) * gain_width]
        for number, vector in enumerate(vectors):
            row = pltpu.roll(vector, LANES - part * heads_here, 1) if part else vector
            cut[part, taps + 2 : taps + 3, block(number)] = row
    for distance in range(parts):
        outs[distance][...] = cut[lax.rem(position_here + distance, parts)]


def input_kernel(taps, full, slopes, grad_x, ending, back):
    length, channels = grad_x.shape
    folded = back.shape[1] // LANES
    back[...] = jnp.zeros_like(back)
    for position in range(channels // LANES):
        here = block(position)
        total = through_taps(taps, full, slopes, here, HALO, length)
        grad_x[:, here] = total.astype(BF16)
        ending[:, here] = total[length - 2 * HALO :]
        ahead = through_taps(taps, full, slopes, here, 0, HALO)
        for tap in range(taps - 1):
            at = tap * FOLDS + position // folded
            back[at : at + 1, block(position % folded)] = ahead[HALO - taps + 1 + tap : HALO - taps + 2 + tap]


def unpack_kernel(terms, chips, taps, grad_in, ending, from_core, from_chip, *refs):
    given, refs = refs[:terms], refs[terms:]
    core, chip, _ = here_at()
    grad_x, cw, cb, dtb, al, sk, gain, late, sem = refs
    rows = late.shape[0]
    channels = ending.shape[1]
    folded = from_core.shape[1] // LANES
    inside = core == 0
    later = jnp.where(inside, from_core[SMALL:, :], from_chip[SMALL:, :])
    later = jnp.where(jnp.logical_or(inside, chip < chips - 1), later, 0.0)
    padding = jnp.zeros((rows - taps + 1, LANES), F32)
    for position in range(channels // LANES):
        here = block(position)
        lines = [
            later[tap * FOLDS + position // folded : tap * FOLDS + position // folded + 1, block(position % folded)]
            for tap in range(taps - 1)
        ]
        late[:, here] = (ending[:, here] + jnp.concatenate([padding] + lines, axis=0)).astype(BF16)
    copy = pltpu.make_async_copy(late, grad_x.at[pl.ds(grad_x.shape[0] - rows, rows)], sem)
    copy.start()
    total = given[0][0:SMALL, :]
    for ref in given[1:]:
        total = total + ref[0:SMALL, :]
    width = cw.shape[1]
    cw[...] = total[0:taps, 0:width]
    cb[...] = total[taps, 0:width]
    gain[...] = total[taps + 1, 0 : gain.shape[0]]
    for number, ref in enumerate((dtb, al, sk)):
        ref[...] = total[taps + 2 : taps + 3, number * LANES : number * LANES + ref.shape[1]]
    copy.wait()


def add_kernel(*refs):
    *terms, back, out = refs
    total = terms[0][...]
    for ref in terms[1:]:
        total = total + ref[...]
    out[0:SMALL, :] = total
    out[SMALL:, :] = back[...]


def add_pair_kernel(own, other, out, alone):
    total = own[0:SMALL, :] + other[0:SMALL, :]
    out[0:SMALL, :] = total
    out[SMALL:, :] = other[SMALL:, :]
    alone[...] = total


def parts_of(message):
    end = message.shape[0] - DEC_ROWS
    return message[0:end, :].astype(F32), unpack_decays(message[end:, :])


def decayed(state, decay, half):
    cuts = state.shape[0] // (half * CUT)
    split_rows = state.reshape(cuts, half, CUT, LANES)
    return (split_rows * decay[0:half].reshape(1, half, 1, LANES)).reshape(state.shape)


def joined(first, second, half):
    state, decay = second
    return decayed(first[0], decay, half) + state, decay * first[1]


def store(out, value):
    state, decay = value
    end = state.shape[0]
    out[0:end, :] = state.astype(BF16)
    out[end:, :] = pack_decays(decay)


def ordered(later, a, b):
    return jnp.where(later, b, a), jnp.where(later, a, b)


def meet_kernel(half, reverse, mine, got, out):
    later = here_at()[0] == (0 if reverse else 1)
    first, second = ordered(later, mine[...], got[...])
    store(out, joined(parts_of(first), parts_of(second), half))


def join_kernel(half, first, second, out):
    store(out, joined(parts_of(first[...]), parts_of(second[...]), half))


def meet_chain_kernel(half, reverse, mine, got, decay_out, *outs):
    later = here_at()[0] == (0 if reverse else 1)
    rows = outs[0].shape[0]
    end = rows * len(outs)
    early, late = ordered(later, mine[end:, :], got[end:, :])
    early, late = unpack_decays(early), unpack_decays(late)
    decay_out[...] = early * late
    for number, out in enumerate(outs):
        here = slice(number * rows, (number + 1) * rows)
        first, second = ordered(later, mine[here, :], got[here, :])
        out[...] = (decayed(first.astype(F32), late, half) + second.astype(F32)).astype(BF16)


def pass_kernel(half, before, own, decay, out):
    state = decayed(before[...].astype(F32), decay[...], half)
    out[...] = (state + own[...].astype(F32)).astype(BF16)


def enter_chain_kernel(half, reverse, streams, *refs):
    given, (mine, got, own, send) = refs[:-4], refs[-4:]
    later = here_at()[0] == (0 if reverse else 1)
    rows = given[0].shape[0]
    end = rows * streams
    decay = unpack_decays(ordered(later, mine[end:, :], got[end:, :])[0])
    for number in range(streams):
        here = slice(number * rows, (number + 1) * rows)
        start = given[number][...].astype(F32)
        for ref in given[streams + number :: streams]:
            start = start + ref[...].astype(F32)
        first = ordered(later, mine[here, :], got[here, :])[0]
        after = decayed(start, decay, half) + first.astype(F32)
        own[here, :] = jnp.where(later, after, start).astype(BF16)
        send[here, :] = jnp.where(later, start, after).astype(BF16)


def enter_kernel(half, reverse, entering, mine, got, own, send):
    later = here_at()[0] == (0 if reverse else 1)
    end = own.shape[0]
    start = entering[0:end, :].astype(F32)
    first = ordered(later, mine[...], got[...])[0]
    state, decay = parts_of(first)
    after = decayed(start, decay, half) + state
    own[...] = jnp.where(later, after, start).astype(BF16)
    send[...] = jnp.where(later, start, after).astype(BF16)


def call(kernel, outs, args, scratch=(), megabytes=8, flops=0, name=None, fetched=(), aliases=None):
    specs = [
        pl.BlockSpec(
            memory_space=pltpu.HBM if number in fetched else pltpu.VMEM
        )
        for number in range(len(args))
    ]
    fetched_out = [out for given, out in (aliases or {}).items() if given in fetched]
    moved = sum(a.size * a.dtype.itemsize for a in args)
    moved += sum(o.size * o.dtype.itemsize for o in outs)
    return pl.pallas_call(
        kernel,
        out_shape=outs,
        in_specs=specs,
        out_specs=[
            pl.BlockSpec(memory_space=pltpu.HBM if number in fetched_out else pltpu.VMEM)
            for number in range(len(outs))
        ],
        input_output_aliases=aliases or {},
        scratch_shapes=list(scratch),
        compiler_params=pltpu.CompilerParams(vmem_limit_bytes=megabytes << 20),
        cost_estimate=pl.CostEstimate(flops=flops, bytes_accessed=moved, transcendentals=0),
        name=name,
    )(*args)


def like(shape, dtype=F32):
    return jax.ShapeDtypeStruct(shape, dtype)


def shift(value, axis, route):
    count = lax.axis_size(axis)
    pairs = [(i, route(i)) for i in range(count)]
    return lax.ppermute(value, axis, [(i, j) for i, j in pairs if 0 <= j < count])


def between_chips(value, routes):
    return shift(value, "seq", lambda i: 2 * routes[i // 2] + i % 2 if i // 2 in routes else -1)


def entering_states(mine, got, half, reverse, beside):
    chips = lax.axis_size("seq") // 2
    entry = like((mine.shape[0] - DEC_ROWS, LANES), BF16)
    if 1 < chips <= 4:
        order = list(range(chips))[::-1] if reverse else list(range(chips))
        stream = like((entry.shape[0] // STREAMS, LANES), BF16)
        decay, *chip = call(
            functools.partial(meet_chain_kernel, half, reverse),
            [like((DEC_ROWS, LANES))] + [stream] * STREAMS,
            [mine, got],
            name="meet",
        )
        arrived = []
        moving = chip
        for hop in range(chips - 1):
            route = {order[hop]: order[hop + 1]}
            landed = [between_chips(part, route) for part in moving]
            if hop < len(beside):
                landed[0] = beside[hop](moving, landed[0])
            arrived += landed
            if hop < chips - 2:
                moving = [
                    call(functools.partial(pass_kernel, half), [stream], [part, own, decay], name="pass")[0]
                    for part, own in zip(landed, chip)
                ]
        own, send = call(
            functools.partial(enter_chain_kernel, half, reverse, STREAMS),
            [entry, entry],
            arrived + [mine, got],
            name="enter",
        )
        return own, shift(send, "seq", lambda i: i ^ 1)
    sign = -1 if reverse else 1
    message = like(mine.shape, BF16)
    chip = call(functools.partial(meet_kernel, half, reverse), [message], [mine, got], name="meet")[0]
    before = shift(chip, "seq", lambda i: i + 2 * sign)
    before = beside[0]([chip], before)
    join = functools.partial(join_kernel, half)
    window = 1
    while window < chips - 1:
        longer = call(join, [message], [before, chip], name="join")[0]
        distance = window + 1
        far = shift(longer, "seq", lambda i: i + 2 * distance * sign)
        before = call(join, [message], [far, before], name="join")[0]
        window = 2 * window + 1
    before = beside[1]([before], before)
    own, send = call(
        functools.partial(enter_kernel, half, reverse),
        [entry, entry],
        [before, mine, got],
        name="enter",
    )
    return own, shift(send, "seq", lambda i: i ^ 1)


def after(value, *signals):
    return lax.optimization_barrier((value, *signals))[0]


def shards(
    conv_input, gate_input, dt_raw, grad_output, conv_weight, conv_bias, dt_bias, a_log, skip, norm_gain
):
    gate, grad = gate_input[0], grad_output[0]
    dt = dt_raw[0].T
    length, channels = conv_input.shape[1:]
    features = gate.shape[1]
    heads = dt.shape[0]
    half = heads // 4
    taps, width = conv_weight.shape
    gain_width = norm_gain.shape[0]
    heads_here = dt_bias.shape[0]
    parts = lax.axis_size("fsdp")
    devices = lax.axis_size("seq")
    sizes = (width, gain_width, heads_here)
    piece_width = -(-width // LANES) * LANES
    full_width = placement(parts - 1, width)[0] + piece_width + LANES
    piece_like = like((SMALL, piece_width))
    shares = [
        conv_weight,
        conv_bias.reshape(1, -1),
        dt_bias.reshape(1, -1),
        a_log.reshape(1, -1),
        skip.reshape(1, -1),
        norm_gain,
    ]

    x = conv_input[0]
    halo, piece, own = call(
        open_kernel,
        [like((HALO, channels), BF16), piece_like, like((2 * SMALL, piece_width))],
        [x, dt] + shares,
        [pltpu.VMEM((2 * HALO, channels), BF16), pltpu.VMEM(dt.shape, F32)]
        + [pltpu.VMEM(share.shape, F32) for share in shares]
        + [pltpu.SemaphoreType.DMA((len(shares) + 2,))],
        fetched=range(len(shares) + 2),
        megabytes=60,
        name="open",
    )
    pieces = [shift(piece, "fsdp", lambda i: (i + distance) % parts) for distance in range(1, parts)]
    halo = shift(halo, "seq", lambda i: i + 1)
    lifted = jnp.pad(after(x, piece).astype(F32), ((HALO, 0), (0, 0)))

    message = like((half * N + DEC_ROWS, LANES), BF16)
    entry = pltpu.VMEM((2, half * N, LANES), BF16)
    full, gain, small, cols, rows, decs = call(
        functools.partial(gather_kernel, taps, sizes, parts, length),
        [
            like((SMALL, full_width)),
            like((1, features)),
            like((8, LANES)),
            like((2, length, LANES)),
            like((3, LANES, length)),
            like((2, DEC_ROWS, LANES), BF16),
        ],
        [own] + pieces,
        [pltpu.VMEM((LANES, LANES), F32), pltpu.VMEM((parts, SMALL, piece_width), F32)],
        name="gather",
    )
    padded, conv, write_t, other = call(
        functools.partial(front_kernel, taps),
        [like(lifted.shape), like((length, channels), BF16), like((N, length)), message],
        [lifted, halo, full, rows, decs],
        name="front",
        aliases={0: 0},
    )
    got = shift(other, "seq", lambda i: i ^ 1)
    conv, mine = call(
        functools.partial(front_own_kernel, taps),
        [like((length, channels), BF16), message],
        [conv, padded, full, rows, decs, write_t],
        name="own",
        aliases={0: 0},
    )
    work = {}

    def intra(signal, value):
        work["local"], work["slope"] = call(
            functools.partial(intra_kernel, taps),
            [like((length, features)), like((length, channels))],
            [padded, full, after(conv, *signal), cols, rows, small],
            flops=2 * length * length * features,
            name="intra",
        )
        return after(value, work["local"])

    def nothing(signal, value):
        return value

    entry_own, entry_got = entering_states(mine, got, half, False, (intra, nothing))
    wide = like((length, features))
    square = like((length, LANES))
    mixed, gated, silus, sums = call(
        norm_own_kernel,
        [wide, wide, wide, like((2, length, LANES))],
        [work["local"], conv, cols, gate, grad, gain, entry_own],
        name="norm_own",
    )
    mixed, gated, silus, stats, other = call(
        norm_kernel,
        [wide, wide, wide, square, message],
        [mixed, gated, silus, work["local"], conv, cols, gate, grad, gain, entry_got, sums, decs],
        name="norm",
        aliases={0: 0, 1: 1, 2: 2},
    )
    got = shift(other, "seq", lambda i: i ^ 1)
    mine = call(
        norm_last_kernel,
        [message],
        [stats, conv, cols, grad, gain, gated, silus, decs],
        name="norm_last",
    )[0]

    def gates(signal, value):
        work["gates"] = call(
            gate_kernel,
            [
                like((length, features), BF16),
                like((length, features)),
                like((length, LANES)),
                like((1, features)),
                like((8, LANES)),
                like((length, LANES)),
            ],
            [mixed, after(conv, *signal), cols, small, gate, grad, gain, stats, entry_own, entry_got],
            [entry],
                flops=2 * length * length * features,
            name="gates",
        )
        return after(value, work["gates"][0])

    def back(signal, value):
        grad_mixed, grad_read = work["gates"][1], work["gates"][5]
        work["back"] = call(
            back_kernel,
            [like((length, features)), like((length, LANES)), like((length, LANES))],
            [after(grad_mixed, *signal), conv, cols, rows, small, grad_read],
            flops=4 * length * length * features,
            name="back",
        )
        return after(value, work["back"][0])

    leave_own, leave_got = entering_states(mine, got, half, True, (gates, back))
    grad_gate, _, out_sums, grad_gain, grad_small, _ = work["gates"]
    grad_values, in_sums, grad_vecs = work["back"]
    slopes, whole, state_sums, end_sums, write_grad = call(
        functools.partial(close_own_kernel, taps),
        [like((2 * HALO + length, channels)), like((SMALL, full_width)), square, like((8, LANES)), square],
        [padded, conv, work["slope"], cols, entry_own, leave_own, grad_values],
        name="close_own",
    )
    slopes, whole, grad_dt, *shares = call(
        functools.partial(close_kernel, taps, sizes),
        [like(slopes.shape), like(whole.shape), like((heads, length))] + [piece_like] * parts,
        [slopes, whole, padded, conv, work["slope"], cols, small, entry_got, leave_got, grad_values, grad_vecs, out_sums]
        + [in_sums, grad_gain, grad_small, state_sums, end_sums, write_grad],
        [pltpu.VMEM((parts, SMALL, piece_width), F32)],
        name="close",
        aliases={0: 0, 1: 1},
    )
    terms = [shares[0]]
    for distance in range(1, parts):
        terms.append(shift(shares[distance], "fsdp", lambda i: (i + distance) % parts))
    grad_x, ending, earlier = call(
        functools.partial(input_kernel, taps),
        [like((length, channels), BF16), like((2 * HALO, channels)), like((BACK_ROWS, piece_width))],
        [full, slopes],
        flops=length * channels * 16,
        name="inputs",
    )
    terms[1] = after(terms[1], ending)
    bundle = like((SMALL + BACK_ROWS, piece_width))
    total = call(add_kernel, [bundle], terms + [earlier], name="add")[0]
    partner = shift(total, "seq", lambda i: i ^ 1)
    total, alone = call(add_pair_kernel, [bundle, piece_like], [total, partner], name="add")
    chips = devices // 2
    behind = between_chips(total, {i: (i - 1) % chips for i in range(chips)})
    if chips <= 4:
        terms = [alone] + [
            between_chips(alone, {i: (i + distance) % chips for i in range(chips)})
            for distance in range(1, chips - 1)
        ]
        terms += [behind] if chips > 1 else []
    else:
        terms = [lax.psum(alone, "seq") * 0.5]
    grad_x, cw, cb, dtb, al, sk, gn = call(
        functools.partial(unpack_kernel, len(terms), chips, taps),
        [
            like((length, channels), BF16),
            like((taps, width)),
            like((width,)),
            like((1, heads_here)),
            like((1, heads_here)),
            like((1, heads_here)),
            like((gain_width,)),
        ],
        [grad_x, ending, partner, behind] + terms,
        [pltpu.VMEM((2 * HALO, channels), BF16), pltpu.SemaphoreType.DMA],
        fetched=(0,),
        aliases={0: 0},
        name="unpack",
    )
    return (
        grad_x[None],
        grad_gate[None],
        grad_dt.T[None],
        cw,
        cb,
        dtb.reshape(-1),
        al.reshape(-1),
        sk.reshape(-1),
        gn,
    )


def solution(mesh):
    tokens = P("fsdp", "seq", None)
    in_specs = (tokens,) * 4 + (P(None, "fsdp"),) + (P("fsdp"),) * 5
    out_specs = (tokens,) * 3 + (P(None, "fsdp"),) + (P("fsdp"),) * 5
    return jax.shard_map(shards, mesh=mesh, in_specs=in_specs, out_specs=out_specs, check_vma=False)
```

time: 123 us -> 85.3 us (0.69)
  waiting for transfers between devices: 44 us -> 24.6 us
  local copies, waits for them, and re-layouts: 15.8 us -> 0.02 us
  blocking collectives: 9.63 us -> 0 us
  Pallas kernels: 25.9 us -> 31.1 us
  starting transfers between devices: 25 us -> 26.6 us
    ppermute x17 -> x27, waiting for transfers between devices: 44 us -> 24.6 us  [shift(): lax.ppermute(value, axis, [(i, j) for i, j in pairs if 0 <= j < count])]
    unnamed x50 -> x6, local copies, waits for them, and re-layouts: 14.3 us -> 0.02 us
    all_gather x1 -> x0, blocking collectives: 9.63 us -> none  [shards(): pieces = lax.all_gather(piece, 'fsdp')]
    pallas_call x17 -> x28, Pallas kernels: 24.3 us -> 31.1 us  [call(): pl.pallas_call(kernel, out_shape=outs, in_specs=specs, out_specs=[pl.Bloc...]
    ppermute x17 -> x27, starting transfers between devices: 25 us -> 26.6 us  [shift(): lax.ppermute(value, axis, [(i, j) for i, j in pairs if 0 <= j < count])]
    pallas_call x1 -> x0, Pallas kernels: 1.62 us -> none  [shards(): pl.pallas_call(patch_kernel, grid=(1,), out_shape=like((length, channels)...]
    pad x0 -> x1, other arithmetic: none -> 1.32 us  [shards(): lifted = jnp.pad(after(x, piece).astype(F32), ((HALO, 0), (0, 0)))]
  transfers between devices with their start and end apart: 17 -> 27, of which waited for: 11 -> 11; matrix products, arithmetic and copies ran while one was open for 2% -> 2% of each run, Pallas kernels for 9% -> 25%
where the time goes in v2:
time: 85.3 us; the launch traced here: 84.9 us
  Pallas kernels  31.1 us (36%)
  starting transfers between devices  26.6 us (31%)
  waiting for transfers between devices  24.6 us (29%)
  other arithmetic  1.32 us (2%)
  between operations  1.19 us (1%)
    pallas_call x28, Pallas kernels, call(): pl.pallas_call(kernel, out_shape=outs, in_specs=specs, out_specs=[pl.Bloc...  31.1 us
    ppermute x27, starting transfers between devices, shift(): lax.ppermute(value, axis, [(i, j) for i, j in pairs if 0 <= j < count])  26.6 us
    ppermute x27, waiting for transfers between devices, shift(): lax.ppermute(value, axis, [(i, j) for i, j in pairs if 0 <= j < count])  24.6 us
  transfers between devices with their start and end apart: 27, of which 11 were waited for; matrix products, arithmetic and copies ran while one was open for 2% of the time, Pallas kernels for 25%

profile of v2, /device:TPU:0, one launch (start us, length us, event | category | flops | bytes accessed | tf_op | source)
XLA Modules:
  0.0 84.9 jit_solution(6182908694624032003)
XLA Ops:
  0.6 1.8 %open.1 = (bf16[8,3712]{1,0:T(8,128)(2,1)}, f32[8,1024]{1,0:T(8,128)}, f32[16,1024]{1,0:T(8,128)}) custom-call(bf16[128,3712]{1,0:T(8,128)(2,1)} %bitcast.25, f32[56,128]{1,0:T(8,128)} %bitcast.28, f32[4,928]{1,0:T(4,128)} %cw.1, f32[1,928]{1,0:T(1,128)} %bitcast.29, f32[1,14]{1,0:T(1,128)} %bitcast.30, f32[1,14]{1,0:T(1,128)} %bitcast.31, ...), custom_call_target="tpu_custom_call" | custom-call | bytes 1158952 | tf_op jit(solution)/shard_map/open/pallas_call | solution.py:689
  2.4 3.9 %collective-permute-start.2 = (f32[8,1024]{1,0:T(8,128)}, f32[8,1024]{1,0:T(8,128)S(1)}, u32[]{:S(2)}, u32[]{:S(2)}) collective-permute-start(f32[8,1024]{1,0:T(8,128)} %get-tuple-element.86), channel_id=1, source_target_pairs={{0,24},{8,0},{16,8},{24,16},{1,25},{9,1},{17,9},{25,17},{2,26},{10... | collective-permute-start | bytes 98312 | tf_op jit(solution)/shard_map/ppermute | solution.py:712
  8.8 1.3 %pad_convert_fusion.lifted = f32[136,3712]{1,0:T(8,128)S(1)} fusion(bf16[128,3712]{1,0:T(8,128)(2,1)} %bitcast.26), kind=kLoop, calls=%fused_computation | loop fusion | flops 504832 | bytes 2969600 | tf_op jit(solution)/shard_map/jit(_pad)/pad | solution.py:819
  10.6 1.3 %collective-permute-done.refs_0_ = f32[8,1024]{1,0:T(8,128)S(1)} collective-permute-done((f32[8,1024]{1,0:T(8,128)}, f32[8,1024]{1,0:T(8,128)S(1)}, u32[]{:S(2)}, u32[]{:S(2)}) %collective-permute-start) | collective-permute-done | bytes 32800 | tf_op jit(solution)/shard_map/ppermute | solution.py:712
  12.5 1.4 %front.1 = (f32[136,3712]{1,0:T(8,128)S(1)}, bf16[128,3712]{1,0:T(8,128)(2,1)S(1)}, f32[64,128]{1,0:T(8,128)S(1)}, bf16[912,128]{1,0:T(8,128)(2,1)S(1)}) custom-call(f32[136,3712]{1,0:T(8,128)S(1)} %pad_convert_fusion.lifted, bf16[8,3712]{1,0:T(8,128)(2,1)S(1)} %collective-permute-done.3.halo, ...), custom_call_target="tpu_custom_call", output_to_operand_aliasing={{0}: (0, {})} | custom-call | bytes 5642240 | tf_op jit(solution)/shard_map/front/pallas_call | solution.py:689
  14.5 1.3 %own.1 = (bf16[128,3712]{1,0:T(8,128)(2,1)S(1)}, bf16[912,128]{1,0:T(8,128)(2,1)S(1)}) custom-call(bf16[128,3712]{1,0:T(8,128)(2,1)S(1)} %get-tuple-element.93.conv_in, f32[136,3712]{1,0:T(8,128)S(1)} %get-tuple-element.92.rows, f32[8,3840]{1,0:T(8,128)S(1)} %get-tuple-element.87.full, ...), custom_call_target="tpu_custom_call", output_to_operand_aliasing={{0}: (0, {})} | custom-call | bytes 4513792 | tf_op jit(solution)/shard_map/own/pallas_call | solution.py:689
  16.0 3.8 %collective-permute-start.6 = (bf16[448,128]{1,0:T(8,128)(2,1)S(1)}, bf16[448,128]{1,0:T(8,128)(2,1)S(1)}, u32[]{:S(2)}, u32[]{:S(2)}) collective-permute-start(bf16[448,128]{1,0:T(8,128)(2,1)S(1)} %get-tuple-element.99.own), channel_id=1, source_target_pairs={{0,2},{1,3},{8,10},{9,11},{16,18},{17,19},{24,26},{25,27}} | collective-permute-start | bytes 344072 | tf_op jit(solution)/shard_map/ppermute | solution.py:712
  19.9 1.3 %collective-permute-start.5 = (bf16[448,128]{1,0:T(8,128)(2,1)S(1)}, bf16[448,128]{1,0:T(8,128)(2,1)S(1)}, u32[]{:S(2)}, u32[]{:S(2)}) collective-permute-start(bf16[448,128]{1,0:T(8,128)(2,1)S(1)} %get-tuple-element.98.own), channel_id=1, source_target_pairs={{0,2},{1,3},{8,10},{9,11},{16,18},{17,19},{24,26},{25,27}} | collective-permute-start | bytes 344072 | tf_op jit(solution)/shard_map/ppermute | solution.py:712
  21.2 3.1 %intra.1 = (f32[128,3584]{1,0:T(8,128)S(1)}, f32[128,3712]{1,0:T(8,128)S(1)}) custom-call(f32[136,3712]{1,0:T(8,128)S(1)} %get-tuple-element.92.rows, f32[8,3840]{1,0:T(8,128)S(1)} %get-tuple-element.87.full, bf16[128,3712]{1,0:T(8,128)(2,1)S(1)} %get-tuple-element.121.conv, f32[2,128,128]{2,1,0:T(8,128)S(1)} %get-tuple-element.101.cols, ...), custom_call_target="tpu_custom_call" | custom-call | flops 117440512 | bytes 7159808 | tf_op jit(solution)/shard_map/intra/pallas_call | solution.py:689
  29.3 1.8 %norm.1 = (f32[128,3584]{1,0:T(8,128)S(1)}, f32[128,3584]{1,0:T(8,128)S(1)}, f32[128,3584]{1,0:T(8,128)S(1)}, f32[128,128]{1,0:T(8,128)S(1)}, bf16[912,128]{1,0:T(8,128)(2,1)S(1)}) custom-call(f32[128,3584]{1,0:T(8,128)S(1)} %get-tuple-element.109.mixed_in, ...), custom_call_target="tpu_custom_call", output_to_operand_aliasing={{0}: (0, {}), {1}: (1, {}), {2}: (2, {})} | custom-call | bytes 16443392 | tf_op jit(solution)/shard_map/norm/pallas_call | solution.py:689
  34.4 4.0 %gates.1 = (bf16[128,3584]{1,0:T(8,128)(2,1)}, f32[128,3584]{1,0:T(8,128)S(1)}, f32[128,128]{1,0:T(8,128)S(1)}, f32[1,3584]{1,0:T(1,128)S(1)}, f32[8,128]{1,0:T(8,128)S(1)}, /*index=5*/f32[128,128]{1,0:T(8,128)S(1)}) custom-call(f32[128,3584]{1,0:T(8,128)S(1)} %get-tuple-element.119.mixed, bf16[128,3712]{1,0:T(8,128)(2,1)S(1)} %get-tuple-element.121.conv, ...), custom_call_target="tpu_custom_call" | custom-call | flops 117440512 | bytes 8196096 | tf_op jit(solution)/shard_map/gates/pallas_call | solution.py:689
  39.8 5.5 %back.1 = (f32[128,3584]{1,0:T(8,128)S(1)}, f32[128,128]{1,0:T(8,128)S(1)}, f32[128,128]{1,0:T(8,128)S(1)}) custom-call(f32[128,3584]{1,0:T(8,128)S(1)} %get-tuple-element.126.grad_mixed, bf16[128,3712]{1,0:T(8,128)(2,1)S(1)} %get-tuple-element.121.conv, f32[2,128,128]{2,1,0:T(8,128)S(1)} %get-tuple-element.101.cols, ...), custom_call_target="tpu_custom_call" | custom-call | flops 234881024 | bytes 5148672 | tf_op jit(solution)/shard_map/back/pallas_call | solution.py:689
  45.4 1.3 %collective-permute-start.18 = (bf16[448,128]{1,0:T(8,128)(2,1)S(1)}, bf16[448,128]{1,0:T(8,128)(2,1)S(1)}, u32[]{:S(2)}, u32[]{:S(2)}) collective-permute-start(bf16[448,128]{1,0:T(8,128)(2,1)S(1)} %pass.15), channel_id=1, source_target_pairs={{2,0},{3,1},{10,8},{11,9},{18,16},{19,17},{26,24},{27,25}} | collective-permute-start | bytes 344072 | tf_op jit(solution)/shard_map/ppermute | solution.py:712
  46.7 1.3 %collective-permute-start.17 = (bf16[448,128]{1,0:T(8,128)(2,1)S(1)}, bf16[448,128]{1,0:T(8,128)(2,1)S(1)}, u32[]{:S(2)}, u32[]{:S(2)}) collective-permute-start(bf16[448,128]{1,0:T(8,128)(2,1)S(1)} %pass.14), channel_id=1, source_target_pairs={{2,0},{3,1},{10,8},{11,9},{18,16},{19,17},{26,24},{27,25}} | collective-permute-start | bytes 344072 | tf_op jit(solution)/shard_map/ppermute | solution.py:712
  48.0 13.6 %collective-permute-done.18.refs_5_ = bf16[448,128]{1,0:T(8,128)(2,1)S(1)} collective-permute-done((bf16[448,128]{1,0:T(8,128)(2,1)S(1)}, bf16[448,128]{1,0:T(8,128)(2,1)S(1)}, u32[]{:S(2)}, u32[]{:S(2)}) %collective-permute-start.18) | collective-permute-done | bytes 114720 | tf_op jit(solution)/shard_map/ppermute | solution.py:712
  61.7 1.5 %collective-permute-done.17.refs_4_ = bf16[448,128]{1,0:T(8,128)(2,1)S(1)} collective-permute-done((bf16[448,128]{1,0:T(8,128)(2,1)S(1)}, bf16[448,128]{1,0:T(8,128)(2,1)S(1)}, u32[]{:S(2)}, u32[]{:S(2)}) %collective-permute-start.17) | collective-permute-done | bytes 114720 | tf_op jit(solution)/shard_map/ppermute | solution.py:712
  63.6 1.9 %close_own.1 = (f32[144,3712]{1,0:T(8,128)S(1)}, f32[8,3840]{1,0:T(8,128)S(1)}, f32[128,128]{1,0:T(8,128)S(1)}, f32[8,128]{1,0:T(8,128)S(1)}, f32[128,128]{1,0:T(8,128)S(1)}) custom-call(f32[136,3712]{1,0:T(8,128)S(1)} %get-tuple-element.92.rows, bf16[128,3712]{1,0:T(8,128)(2,1)S(1)} %get-tuple-element.121.conv, f32[128,3712]{1,0:T(8,128)S(1)} %get-tuple-element.103.slope, ...), custom_call_target="tpu_custom_call" | custom-call | bytes 9691136 | tf_op jit(solution)/shard_map/close_own/pallas_call | solution.py:689
  65.5 2.9 %close.1 = (f32[144,3712]{1,0:T(8,128)S(1)}, f32[8,3840]{1,0:T(8,128)S(1)}, f32[56,128]{1,0:T(8,128)}, f32[8,1024]{1,0:T(8,128)S(1)}, f32[8,1024]{1,0:T(8,128)S(...) custom-call(f32[144,3712]{1,0:T(8,128)S(1)} %get-tuple-element.131.slopes_in, ...), custom_call_target="tpu_custom_call", output_to_operand_aliasing={{0}: (0, {}), {1}: (1, {})} | custom-call | bytes 12331008 | tf_op jit(solution)/shard_map/close/pallas_call | solution.py:689
  68.4 2.4 %collective-permute-start.20 = (f32[8,1024]{1,0:T(8,128)S(1)}, f32[8,1024]{1,0:T(8,128)S(1)}, u32[]{:S(2)}, u32[]{:S(2)}) collective-permute-start(f32[8,1024]{1,0:T(8,128)S(1)} %get-tuple-element.146), channel_id=1, source_target_pairs={{0,8},{8,16},{16,24},{24,0},{1,9},{9,17},{17,25},{25,1},{2,10},{10... | collective-permute-start | bytes 98312 | tf_op jit(solution)/shard_map/ppermute | solution.py:712
  72.3 2.4 %inputs.1 = (bf16[128,3712]{1,0:T(8,128)(2,1)}, f32[16,3712]{1,0:T(8,128)S(1)}, f32[16,1024]{1,0:T(8,128)S(1)}) custom-call(f32[8,3840]{1,0:T(8,128)S(1)} %get-tuple-element.87.full, f32[144,3712]{1,0:T(8,128)S(1)} %get-tuple-element.142.slopes), custom_call_target="tpu_custom_call" | custom-call | flops 7602176 | bytes 3514368 | tf_op jit(solution)/shard_map/inputs/pallas_call | solution.py:689
  75.3 1.3 %collective-permute-done.23.other.from_core = f32[24,1024]{1,0:T(8,128)S(1)} collective-permute-done((f32[24,1024]{1,0:T(8,128)S(1)}, f32[24,1024]{1,0:T(8,128)S(1)}, u32[]{:S(2)}, u32[]{:S(2)}) %collective-permute-start.23) | collective-permute-done | bytes 98336 | tf_op jit(solution)/shard_map/ppermute | solution.py:712
  78.7 2.9 %collective-permute-done.26.refs_2_ = f32[8,1024]{1,0:T(8,128)S(1)} collective-permute-done((f32[8,1024]{1,0:T(8,128)S(1)}, f32[8,1024]{1,0:T(8,128)S(1)}, u32[]{:S(2)}, u32[]{:S(2)}) %collective-permute-start.26) | collective-permute-done | bytes 32800 | tf_op jit(solution)/shard_map/ppermute | solution.py:712
  81.6 1.8 %collective-permute-done.25.refs_1_ = f32[8,1024]{1,0:T(8,128)S(1)} collective-permute-done((f32[8,1024]{1,0:T(8,128)S(1)}, f32[8,1024]{1,0:T(8,128)S(1)}, u32[]{:S(2)}, u32[]{:S(2)}) %collective-permute-start.25) | collective-permute-done | bytes 32800 | tf_op jit(solution)/shard_map/ppermute | solution.py:712
  83.4 1.3 %unpack.1 = (bf16[128,3712]{1,0:T(8,128)(2,1)}, f32[4,928]{1,0:T(4,128)}, f32[928]{0:T(1024)}, f32[1,14]{1,0:T(1,128)}, f32[1,14]{1,0:T(1,128)}, /*index=5*/f32[1,14]{1,0:T(1,128)}, f32[896]{0:T(1024)}) custom-call(bf16[128,3712]{1,0:T(8,128)(2,1)} %get-tuple-element.143.grad_in, ...), custom_call_target="tpu_custom_call", output_to_operand_aliasing={{0}: (0, {})} | custom-call | bytes 2553640 | tf_op jit(solution)/shard_map/unpack/pallas_call | solution.py:689
  (65 shorter events, 18.5 us)
Async XLA Ops:
  2.4 7.7 %collective-permute-start.2 = (f32[8,1024]{1,0:T(8,128)}, f32[8,1024]{1,0:T(8,128)S(1)}, u32[]{:S(2)}, u32[]{:S(2)}) collective-permute-start(f32[8,1024]{1,0:T(8,128)} %get-tuple-element.86), channel_id=1, source_target_pairs={{0,24},{8,0},{16,8},{24,16},{1,25},{9,1},{17,9},{25,17},{2,26},{10... | collective-permute-start | bytes 98312 | tf_op jit(solution)/shard_map/ppermute | solution.py:712
  6.4 4.2 %collective-permute-start.1 = (f32[8,1024]{1,0:T(8,128)}, f32[8,1024]{1,0:T(8,128)S(1)}, u32[]{:S(2)}, u32[]{:S(2)}) collective-permute-start(f32[8,1024]{1,0:T(8,128)} %get-tuple-element.86), channel_id=1, source_target_pairs={{0,16},{8,24},{16,0},{24,8},{1,17},{9,25},{17,1},{25,9},{2,18},{10... | collective-permute-start | bytes 98312 | tf_op jit(solution)/shard_map/ppermute | solution.py:712
  6.9 5.0 %collective-permute-start = (f32[8,1024]{1,0:T(8,128)}, f32[8,1024]{1,0:T(8,128)S(1)}, u32[]{:S(2)}, u32[]{:S(2)}) collective-permute-start(f32[8,1024]{1,0:T(8,128)} %get-tuple-element.86), channel_id=1, source_target_pairs={{0,8},{8,16},{16,24},{24,0},{1,9},{9,17},{17,25},{25,1},{2,10},{10... | collective-permute-start | bytes 98312 | tf_op jit(solution)/shard_map/ppermute | solution.py:712
  7.5 5.0 %collective-permute-start.3 = (bf16[8,3712]{1,0:T(8,128)(2,1)}, bf16[8,3712]{1,0:T(8,128)(2,1)S(1)}, u32[]{:S(2)}, u32[]{:S(2)}) collective-permute-start(bf16[8,3712]{1,0:T(8,128)(2,1)} %get-tuple-element.89), channel_id=1, source_target_pairs={{0,1},{1,2},{2,3},{3,4},{4,5},{5,6},{6,7},{8,9},{9,10},{10,11},{11... | collective-permute-start | bytes 178184 | tf_op jit(solution)/shard_map/ppermute | solution.py:712
  13.9 1.9 %collective-permute-start.4 = (bf16[912,128]{1,0:T(8,128)(2,1)S(1)}, bf16[912,128]{1,0:T(8,128)(2,1)S(1)}, u32[]{:S(2)}, u32[]{:S(2)}) collective-permute-start(bf16[912,128]{1,0:T(8,128)(2,1)S(1)} %get-tuple-element.97), channel_id=1, source_target_pairs={{0,1},{1,0},{2,3},{3,2},{4,5},{5,4},{6,7},{7,6},{8,9},{9,8},{10,11... | collective-permute-start | bytes 700424 | tf_op jit(solution)/shard_map/ppermute | solution.py:712
  16.0 8.3 %collective-permute-start.6 = (bf16[448,128]{1,0:T(8,128)(2,1)S(1)}, bf16[448,128]{1,0:T(8,128)(2,1)S(1)}, u32[]{:S(2)}, u32[]{:S(2)}) collective-permute-start(bf16[448,128]{1,0:T(8,128)(2,1)S(1)} %get-tuple-element.99.own), channel_id=1, source_target_pairs={{0,2},{1,3},{8,10},{9,11},{16,18},{17,19},{24,26},{25,27}} | collective-permute-start | bytes 344072 | tf_op jit(solution)/shard_map/ppermute | solution.py:712
  19.9 5.4 %collective-permute-start.5 = (bf16[448,128]{1,0:T(8,128)(2,1)S(1)}, bf16[448,128]{1,0:T(8,128)(2,1)S(1)}, u32[]{:S(2)}, u32[]{:S(2)}) collective-permute-start(bf16[448,128]{1,0:T(8,128)(2,1)S(1)} %get-tuple-element.98.own), channel_id=1, source_target_pairs={{0,2},{1,3},{8,10},{9,11},{16,18},{17,19},{24,26},{25,27}} | collective-permute-start | bytes 344072 | tf_op jit(solution)/shard_map/ppermute | solution.py:712
  24.4 1.6 %collective-permute-start.8 = (bf16[448,128]{1,0:T(8,128)(2,1)S(1)}, bf16[448,128]{1,0:T(8,128)(2,1)S(1)}, u32[]{:S(2)}, u32[]{:S(2)}) collective-permute-start(bf16[448,128]{1,0:T(8,128)(2,1)S(1)} %pass.9), channel_id=1, source_target_pairs={{2,4},{3,5},{10,12},{11,13},{18,20},{19,21},{26,28},{27,29}} | collective-permute-start | bytes 344072 | tf_op jit(solution)/shard_map/ppermute | solution.py:712
  25.3 1.4 %collective-permute-start.7 = (bf16[448,128]{1,0:T(8,128)(2,1)S(1)}, bf16[448,128]{1,0:T(8,128)(2,1)S(1)}, u32[]{:S(2)}, u32[]{:S(2)}) collective-permute-start(bf16[448,128]{1,0:T(8,128)(2,1)S(1)} %pass.8), channel_id=1, source_target_pairs={{2,4},{3,5},{10,12},{11,13},{18,20},{19,21},{26,28},{27,29}} | collective-permute-start | bytes 344072 | tf_op jit(solution)/shard_map/ppermute | solution.py:712
  27.7 1.6 %collective-permute-start.11 = (bf16[896,128]{1,0:T(8,128)(2,1)S(1)}, bf16[896,128]{1,0:T(8,128)(2,1)S(1)}, u32[]{:S(2)}, u32[]{:S(2)}) collective-permute-start(bf16[896,128]{1,0:T(8,128)(2,1)S(1)} %get-tuple-element.112), channel_id=1, source_target_pairs={{0,1},{1,0},{2,3},{3,2},{4,5},{5,4},{6,7},{7,6},{8,9},{9,8},{10,11... | collective-permute-start | bytes 688136 | tf_op jit(solution)/shard_map/ppermute | solution.py:712
  31.1 1.6 %collective-permute-start.12 = (bf16[912,128]{1,0:T(8,128)(2,1)S(1)}, bf16[912,128]{1,0:T(8,128)(2,1)S(1)}, u32[]{:S(2)}, u32[]{:S(2)}) collective-permute-start(bf16[912,128]{1,0:T(8,128)(2,1)S(1)} %get-tuple-element.117), channel_id=1, source_target_pairs={{0,1},{1,0},{2,3},{3,2},{4,5},{5,4},{6,7},{7,6},{8,9},{9,8},{10,11... | collective-permute-start | bytes 700424 | tf_op jit(solution)/shard_map/ppermute | solution.py:712
  32.9 5.5 %collective-permute-start.14 = (bf16[448,128]{1,0:T(8,128)(2,1)S(1)}, bf16[448,128]{1,0:T(8,128)(2,1)S(1)}, u32[]{:S(2)}, u32[]{:S(2)}) collective-permute-start(bf16[448,128]{1,0:T(8,128)(2,1)S(1)} %get-tuple-element.120.own), channel_id=1, source_target_pairs={{6,4},{7,5},{14,12},{15,13},{22,20},{23,21},{30,28},{31,29}} | collective-permute-start | bytes 344072 | tf_op jit(solution)/shard_map/ppermute | solution.py:712
  33.6 5.6 %collective-permute-start.13 = (bf16[448,128]{1,0:T(8,128)(2,1)S(1)}, bf16[448,128]{1,0:T(8,128)(2,1)S(1)}, u32[]{:S(2)}, u32[]{:S(2)}) collective-permute-start(bf16[448,128]{1,0:T(8,128)(2,1)S(1)} %get-tuple-element.118.own), channel_id=1, source_target_pairs={{6,4},{7,5},{14,12},{15,13},{22,20},{23,21},{30,28},{31,29}} | collective-permute-start | bytes 344072 | tf_op jit(solution)/shard_map/ppermute | solution.py:712
  38.4 6.9 %collective-permute-start.16 = (bf16[448,128]{1,0:T(8,128)(2,1)S(1)}, bf16[448,128]{1,0:T(8,128)(2,1)S(1)}, u32[]{:S(2)}, u32[]{:S(2)}) collective-permute-start(bf16[448,128]{1,0:T(8,128)(2,1)S(1)} %pass.13), channel_id=1, source_target_pairs={{4,2},{5,3},{12,10},{13,11},{20,18},{21,19},{28,26},{29,27}} | collective-permute-start | bytes 344072 | tf_op jit(solution)/shard_map/ppermute | solution.py:712
  39.2 7.5 %collective-permute-start.15 = (bf16[448,128]{1,0:T(8,128)(2,1)S(1)}, bf16[448,128]{1,0:T(8,128)(2,1)S(1)}, u32[]{:S(2)}, u32[]{:S(2)}) collective-permute-start(bf16[448,128]{1,0:T(8,128)(2,1)S(1)} %pass.12), channel_id=1, source_target_pairs={{4,2},{5,3},{12,10},{13,11},{20,18},{21,19},{28,26},{29,27}} | collective-permute-start | bytes 344072 | tf_op jit(solution)/shard_map/ppermute | solution.py:712
  45.4 16.3 %collective-permute-start.18 = (bf16[448,128]{1,0:T(8,128)(2,1)S(1)}, bf16[448,128]{1,0:T(8,128)(2,1)S(1)}, u32[]{:S(2)}, u32[]{:S(2)}) collective-permute-start(bf16[448,128]{1,0:T(8,128)(2,1)S(1)} %pass.15), channel_id=1, source_target_pairs={{2,0},{3,1},{10,8},{11,9},{18,16},{19,17},{26,24},{27,25}} | collective-permute-start | bytes 344072 | tf_op jit(solution)/shard_map/ppermute | solution.py:712
  46.7 16.5 %collective-permute-start.17 = (bf16[448,128]{1,0:T(8,128)(2,1)S(1)}, bf16[448,128]{1,0:T(8,128)(2,1)S(1)}, u32[]{:S(2)}, u32[]{:S(2)}) collective-permute-start(bf16[448,128]{1,0:T(8,128)(2,1)S(1)} %pass.14), channel_id=1, source_target_pairs={{2,0},{3,1},{10,8},{11,9},{18,16},{19,17},{26,24},{27,25}} | collective-permute-start | bytes 344072 | tf_op jit(solution)/shard_map/ppermute | solution.py:712
  63.5 2.0 %collective-permute-start.19 = (bf16[896,128]{1,0:T(8,128)(2,1)S(1)}, bf16[896,128]{1,0:T(8,128)(2,1)S(1)}, u32[]{:S(2)}, u32[]{:S(2)}) collective-permute-start(bf16[896,128]{1,0:T(8,128)(2,1)S(1)} %get-tuple-element.133), channel_id=1, source_target_pairs={{0,1},{1,0},{2,3},{3,2},{4,5},{5,4},{6,7},{7,6},{8,9},{9,8},{10,11... | collective-permute-start | bytes 688136 | tf_op jit(solution)/shard_map/ppermute | solution.py:712
  68.4 6.2 %collective-permute-start.20 = (f32[8,1024]{1,0:T(8,128)S(1)}, f32[8,1024]{1,0:T(8,128)S(1)}, u32[]{:S(2)}, u32[]{:S(2)}) collective-permute-start(f32[8,1024]{1,0:T(8,128)S(1)} %get-tuple-element.146), channel_id=1, source_target_pairs={{0,8},{8,16},{16,24},{24,0},{1,9},{9,17},{17,25},{25,1},{2,10},{10... | collective-permute-start | bytes 98312 | tf_op jit(solution)/shard_map/ppermute | solution.py:712
  70.8 3.9 %collective-permute-start.21 = (f32[8,1024]{1,0:T(8,128)S(1)}, f32[8,1024]{1,0:T(8,128)S(1)}, u32[]{:S(2)}, u32[]{:S(2)}) collective-permute-start(f32[8,1024]{1,0:T(8,128)S(1)} %get-tuple-element.148), channel_id=1, source_target_pairs={{0,16},{8,24},{16,0},{24,8},{1,17},{9,25},{17,1},{25,9},{2,18},{10... | collective-permute-start | bytes 98312 | tf_op jit(solution)/shard_map/ppermute | solution.py:712
  71.3 3.9 %collective-permute-start.22 = (f32[8,1024]{1,0:T(8,128)S(1)}, f32[8,1024]{1,0:T(8,128)S(1)}, u32[]{:S(2)}, u32[]{:S(2)}) collective-permute-start(f32[8,1024]{1,0:T(8,128)S(1)} %get-tuple-element.149), channel_id=1, source_target_pairs={{0,24},{8,0},{16,8},{24,16},{1,25},{9,1},{17,9},{25,17},{2,26},{10... | collective-permute-start | bytes 98312 | tf_op jit(solution)/shard_map/ppermute | solution.py:712
  76.6 6.8 %collective-permute-start.24 = (f32[24,1024]{1,0:T(8,128)S(1)}, f32[24,1024]{1,0:T(8,128)S(1)}, u32[]{:S(2)}, u32[]{:S(2)}) collective-permute-start(f32[24,1024]{1,0:T(8,128)S(1)} %get-tuple-element.151), channel_id=1, source_target_pairs={{0,6},{1,7},{2,0},{3,1},{4,2},{5,3},{6,4},{7,5},{8,14},{9,15},{10,... | collective-permute-start | bytes 294920 | tf_op jit(solution)/shard_map/ppermute | solution.py:712
  76.7 4.9 %collective-permute-start.26 = (f32[8,1024]{1,0:T(8,128)S(1)}, f32[8,1024]{1,0:T(8,128)S(1)}, u32[]{:S(2)}, u32[]{:S(2)}) collective-permute-start(f32[8,1024]{1,0:T(8,128)S(1)} %get-tuple-element.152.refs_0_), channel_id=1, source_target_pairs={{0,4},{1,5},{2,6},{3,7},{4,0},{5,1},{6,2},{7,3},{8,12},{9,13},{10,... | collective-permute-start | bytes 98312 | tf_op jit(solution)/shard_map/ppermute | solution.py:712
  77.7 5.7 %collective-permute-start.25 = (f32[8,1024]{1,0:T(8,128)S(1)}, f32[8,1024]{1,0:T(8,128)S(1)}, u32[]{:S(2)}, u32[]{:S(2)}) collective-permute-start(f32[8,1024]{1,0:T(8,128)S(1)} %get-tuple-element.152.refs_0_), channel_id=1, source_target_pairs={{0,2},{1,3},{2,4},{3,5},{4,6},{5,7},{6,0},{7,1},{8,10},{9,11},{10,... | collective-permute-start | bytes 98312 | tf_op jit(solution)/shard_map/ppermute | solution.py:712
  (6 other events, 20.1 us)

commit v3 on v2

--- a/solution.py
+++ b/solution.py
@@ -16,15 +16,13 @@
 STREAMS = 2
 FOLDS = 4
 BACK_ROWS = 16
-CUT = 16
 DEC_ROWS = 16
 F32, BF16 = jnp.float32, jnp.bfloat16
-HIGH = lax.Precision.HIGHEST
-
-
-def dot(a, b, over=(1, 0), precision=None):
+
+
+def dot(a, b, over=(1, 0)):
     return lax.dot_general(
-        a, b, (((over[0],), (over[1],)), ((), ())), precision=precision, preferred_element_type=F32
+        a, b, (((over[0],), (over[1],)), ((), ())), preferred_element_type=F32
     )
 
 
@@ -44,6 +42,16 @@
 def split(x):
     high = x.astype(BF16)
     return high, (x - high.astype(F32)).astype(BF16)
+
+
+def dot_parts(ones, value, parts):
+    pieces = []
+    for _ in range(parts):
+        piece = value.astype(BF16)
+        pieces.append(piece)
+        value = value - piece.astype(F32)
+    ones = ones.astype(BF16)
+    return dot(jnp.concatenate([ones] * parts, axis=1), jnp.concatenate(pieces, axis=0))
 
 
 def block(position):
@@ -64,9 +72,11 @@
     )
 
 
-def head_sums(product, pair):
+def head_sums(product, pair, parts=2):
     shape = (LANES, LANES)
     pick = (iota(shape, 1) == 2 * pair + (iota(shape, 0) >= P_SIZE).astype(jnp.int32)).astype(BF16)
+    if parts == 1:
+        return dot(product.astype(BF16), pick)
     high, low = split(product)
     return dot(jnp.concatenate([high, low], axis=1), jnp.concatenate([pick, pick], axis=0))
 
@@ -107,31 +117,30 @@
         own[SMALL:, block(group)] = raw[group * SMALL : (group + 1) * SMALL, :]
 
 
+def peer(position, distance, parts):
+    if parts & (parts - 1) == 0:
+        return position ^ distance
+    return (position + distance) % parts
+
+
+def peer_back(position, distance, parts):
+    if parts & (parts - 1) == 0:
+        return position ^ distance
+    return lax.rem(position + parts - distance, parts)
+
+
 def placement(position, width):
     start = position * width
     base = start // LANES * LANES
     return base, start - base
 
 
-def state_rows(pair, half):
-    pair = pair % half
-    return [slice((cut * half + pair) * CUT, (cut * half + pair + 1) * CUT) for cut in range(N // CUT)]
-
-
-def put_state(states, pair, half, value):
-    for cut, rows in enumerate(state_rows(pair, half)):
-        states[rows, :] = value[cut * CUT : (cut + 1) * CUT]
-
-
-def get_state(states, pair, half):
-    return jnp.concatenate([states[rows, :] for rows in state_rows(pair, half)], axis=0)
-
-
-def hand_out(states, decs, core, mine, other):
-    end = states.shape[1] - DEC_ROWS
-    states[:, end:, :] = decs[...]
-    mine[...] = states[core]
-    other[...] = states[1 - core]
+def put_state(states, pair, value):
+    states[pair * N : (pair + 1) * N, :] = value
+
+
+def get_state(states, pair):
+    return states[pair * N : (pair + 1) * N, :]
 
 
 def pack_decays(decays):
@@ -155,7 +164,7 @@
     piece_width = pieces.shape[2]
     pieces[mine_at] = own[0:SMALL, :]
     for distance in range(1, parts):
-        pieces[lax.rem(mine_at + parts - distance, parts)] = given[distance - 1][...]
+        pieces[peer_back(mine_at, distance, parts)] = given[distance - 1][...]
     width, gain_width, heads_here = sizes
     heads = heads_here * parts
     half = heads // 4
@@ -182,8 +191,8 @@
     step = jnp.maximum(raw, 0.0) + jnp.log1p(jnp.exp(-jnp.abs(raw)))
     logs = -jnp.exp(small[1:2, :]) * step
     square = (length, length)
-    lower = (iota(square, 0) >= iota(square, 1)).astype(F32)
-    running = dot(lower, logs, precision=HIGH)
+    lower = iota(square, 0) >= iota(square, 1)
+    running = dot_parts(lower, logs, 3)
     running_t = running.T
     step_t = step.T
     last = jnp.broadcast_to(running_t[:, length - 1 : length], running_t.shape)
@@ -193,13 +202,14 @@
     rows_out[1] = running_t
     rows_out[2] = jnp.exp(last - running_t) * step_t
     wide[...] = jnp.exp(last)[:, 0:LANES]
-    first = iota((half, LANES), 1) < P_SIZE
-    for side in range(2):
-        even = wide[pl.ds(2 * half * side, half, stride=2), :]
-        odd = wide[pl.ds(2 * half * side + 1, half, stride=2), :]
+    group = half // STREAMS
+    first = iota((group, LANES), 1) < P_SIZE
+    for number in range(2 * STREAMS):
+        even = wide[pl.ds(2 * group * number, group, stride=2), :]
+        odd = wide[pl.ds(2 * group * number + 1, group, stride=2), :]
         decays = jnp.where(first, even, odd)
-        decs[side] = pack_decays(
-            jnp.concatenate([decays, jnp.zeros((DEC_ROWS - half, LANES), F32)], axis=0)
+        decs[number] = pack_decays(
+            jnp.concatenate([decays, jnp.zeros((DEC_ROWS - group, LANES), F32)], axis=0)
         )
 
 
@@ -207,12 +217,12 @@
     return pl.ds(pl.multiple_of(pair * LANES, LANES), LANES)
 
 
-def front_side(taps, side, rows, full, tails, decs, write_t, conv, out):
+def front_group(taps, number, rows, full, tails, decs, write_t, conv, out):
     length = conv.shape[0]
-    half = (out.shape[0] - DEC_ROWS) // N
-    scale = tails[2, pl.ds(side * 2 * half, 2 * half), :]
-    for pair in range(half):
-        here = side_block(side * half + pair)
+    group = (out.shape[0] - DEC_ROWS) // N
+    scale = tails[2, pl.ds(number * 2 * group, 2 * group), :]
+    for pair in range(group):
+        here = side_block(number * group + pair)
         pre = before_silu(rows, full, here, taps, length)
         value = (pre * sigmoid(pre)).astype(BF16)
         conv[:, here] = value
@@ -223,12 +233,11 @@
             ],
             axis=1,
         )
-        put_state(out, pair, half, dot(scaled, apart(value)).astype(BF16))
-    out[half * N :, :] = decs[side]
-
-
-def front_kernel(taps, lifted, halo, full, tails, decs, rows, conv, write_out, other):
-    core = here_at()[0]
+        put_state(out, pair, dot(scaled, apart(value)).astype(BF16))
+    out[group * N :, :] = decs[number]
+
+
+def front_kernel(taps, lifted, halo, full, tails, decs, rows, conv, write_out, out):
     length, channels = conv.shape
     rows[0:HALO, :] = halo[...].astype(F32)
     here = block(channels // LANES - 1)
@@ -237,17 +246,34 @@
     conv[:, here] = vectors
     write_t = vectors.astype(F32).T[0:N, :]
     write_out[...] = write_t
-    front_side(taps, 1 - core, rows, full, tails, decs, write_t, conv, other)
-
-
-def front_own_kernel(taps, conv_in, rows, full, tails, decs, write_t, conv, mine):
-    front_side(taps, here_at()[0], rows, full, tails, decs, write_t[...], conv, mine)
+    front_group(taps, group_at(False, 0), rows, full, tails, decs, write_t, conv, out)
+
+
+def group_at(own, stream):
+    core = here_at()[0]
+    return (core if own else 1 - core) * STREAMS + stream
+
+
+def front_next_kernel(taps, own, streams, conv_in, rows, full, tails, decs, write_t, conv, *outs):
+    for stream, out in zip(streams, outs):
+        front_group(taps, group_at(own, stream), rows, full, tails, decs, write_t[...], conv, out)
 
 
 def head_weights(cols, rows_ref, head, causal, scores):
     gap = cols[1, :, head : head + 1] - rows_ref[1, head : head + 1, :]
     scaled = jnp.exp(jnp.where(causal, gap, -1e30)) * rows_ref[0, head : head + 1, :]
     return scaled, (scaled * scores).astype(BF16)
+
+
+def factor_kernel(cols, gate, grad, gain, silus, grown, decays):
+    length, features = gate.shape
+    decay = jnp.exp(cols[1])
+    for pair in range(features // LANES):
+        here = block(pair)
+        z = gate[:, here].astype(F32)
+        silus[:, here] = z * sigmoid(z)
+        grown[:, here] = grad[:, here].astype(F32) * gain[:, here]
+        decays[:, here] = by_head(decay, pair, (length, LANES))
 
 
 def intra_kernel(taps, rows, full, conv, cols, rows_ref, small, local, slope):
@@ -266,7 +292,8 @@
         )
         values = conv[:, block(pair)]
         skip = by_head(small[2:3, :], pair, (1, LANES))
-        local[:, block(pair)] = dot(weights, apart(values)) + skip * values.astype(F32)
+        here = block(pair)
+        local[:, here] = dot(weights, apart(values)) + skip * values.astype(F32)
     for position in range(channels // LANES):
         here = block(position)
         pre = before_silu(rows, full, here, taps, length)
@@ -274,63 +301,53 @@
         slope[:, here] = gate * (1.0 + pre * (1.0 - gate))
 
 
-def side_columns(columns, side, half):
-    return pltpu.roll(columns, lax.rem(LANES - 2 * half * side, LANES), 1)
-
-
-def mix_side(side, local, conv, cols, gate, grad, gain, entry, mixed, gated, silus):
+def mix_side(own, local, conv, silus, grown, decays, entries, mixed, gated):
     length, features = local.shape
-    half = features // LANES // 2
     shape = (length, LANES)
     read = conv[:, features + N : features + 2 * N]
-    decay = side_columns(jnp.exp(cols[1]), side, half)
     square_sum = jnp.zeros(shape, F32)
     cross_sum = jnp.zeros(shape, F32)
-    for pair in range(half):
-        here = side_block(side * half + pair)
-        carried = dot(read, get_state(entry, pair, half))
-        mix = local[:, here] + by_head(decay, pair, shape) * carried
-        mixed[:, here] = mix
-        z = gate[:, here].astype(F32)
-        silu = z * sigmoid(z)
-        silus[:, here] = silu
-        product = mix * silu
-        gated[:, here] = product
-        square_sum += product * product
-        cross_sum += product * (grad[:, here].astype(F32) * gain[:, here])
+    for stream, entry in enumerate(entries):
+        number = group_at(own, stream)
+        group = entry.shape[0] // N
+        for pair in range(group):
+            here = side_block(number * group + pair)
+            carried = dot(read, get_state(entry, pair))
+            mix = local[:, here] + decays[:, here] * carried
+            mixed[:, here] = mix
+            product = mix * silus[:, here]
+            gated[:, here] = product
+            square_sum += product * product
+            cross_sum += product * grown[:, here]
     return square_sum, cross_sum
 
 
-def norm_own_kernel(local, conv, cols, gate, grad, gain, entry, mixed, gated, silus, sums):
-    square, cross = mix_side(
-        here_at()[0], local, conv, cols, gate, grad, gain, entry, mixed, gated, silus
-    )
+def mix_kernel(local, conv, silus, grown, decays, *refs):
+    entries, (mixed, gated, sums) = refs[:STREAMS], refs[STREAMS:]
+    square, cross = mix_side(True, local, conv, silus, grown, decays, entries, mixed, gated)
     sums[0] = square
     sums[1] = cross
 
 
-def back_state_side(side, stats, conv, cols, grad, gain, gated, silus, decs, out):
+def back_state(number, stats, conv, silus, grown, decays, gated, decs, out):
     length, features = gated.shape
-    half = features // LANES // 2
+    group = (out.shape[0] - DEC_ROWS) // N
     shape = (length, LANES)
     read = conv[:, features + N : features + 2 * N]
-    decay = side_columns(jnp.exp(cols[1]), side, half)
     scale = jnp.broadcast_to(stats[:, 0:1], shape)
     factor = jnp.broadcast_to(stats[:, 1:2], shape)
-    for pair in range(half):
-        here = side_block(side * half + pair)
-        grad_gated = scale * (grad[:, here].astype(F32) * gain[:, here]) - factor * gated[:, here]
-        weighted = by_head(decay, pair, shape) * (grad_gated * silus[:, here])
-        put_state(out, pair, half, dot(read, weighted.astype(BF16), (0, 0)).astype(BF16))
-    out[half * N :, :] = decs[side]
-
-
-def norm_kernel(
-    mixed_in, gated_in, silus_in, local, conv, cols, gate, grad, gain, entry, sums, decs, mixed, gated, silus, stats, other
-):
+    for pair in range(group):
+        here = side_block(number * group + pair)
+        grad_gated = scale * grown[:, here] - factor * gated[:, here]
+        weighted = decays[:, here] * (grad_gated * silus[:, here])
+        put_state(out, pair, dot(read, weighted.astype(BF16), (0, 0)).astype(BF16))
+    out[group * N :, :] = decs[number]
+
+
+def norm_kernel(mixed_in, gated_in, local, conv, silus, grown, decays, sums, decs, *refs):
+    entries, (mixed, gated, stats, out) = refs[:STREAMS], refs[STREAMS:]
     length, features = local.shape
-    side = 1 - here_at()[0]
-    square, cross = mix_side(side, local, conv, cols, gate, grad, gain, entry, mixed, gated, silus)
+    square, cross = mix_side(False, local, conv, silus, grown, decays, entries, mixed, gated)
     square = jnp.sum(square + sums[0], axis=1, keepdims=True)
     cross = jnp.sum(cross + sums[1], axis=1, keepdims=True)
     scale = lax.rsqrt(square * (1.0 / features) + EPS)
@@ -338,23 +355,25 @@
     lane = iota((length, LANES), 1)
     values = jnp.where(lane == 0, scale, jnp.where(lane == 1, factor, 0.0))
     stats[...] = values
-    back_state_side(side, values, conv, cols, grad, gain, gated, silus, decs, other)
-
-
-def norm_last_kernel(stats, conv, cols, grad, gain, gated, silus, decs, mine):
-    back_state_side(here_at()[0], stats[...], conv, cols, grad, gain, gated, silus, decs, mine)
+    back_state(group_at(False, 0), values, conv, silus, grown, decays, gated, decs, out)
+
+
+def norm_next_kernel(own, streams, stats, conv, silus, grown, decays, gated, decs, *outs):
+    for stream, out in zip(streams, outs):
+        back_state(group_at(own, stream), stats[...], conv, silus, grown, decays, gated, decs, out)
 
 
 def gate_kernel(
-    mixed, conv, cols, small, gate, grad, gain, stats, own, got, grad_gate, grad_mixed, sums, grad_gain, grad_small, grad_read, entry
+    mixed, conv, cols, small, gate, grad, gain, stats, *refs
 ):
-    core = here_at()[0]
+    given, refs = refs[: 2 * STREAMS], refs[2 * STREAMS :]
+    grad_gate, grad_mixed, sums, grad_gain, grad_small, grad_read, entry = refs
     length, features = mixed.shape
     pairs = features // LANES
-    half = pairs // 2
+    group = pairs // (2 * STREAMS)
     shape = (length, LANES)
-    entry[core] = own[...]
-    entry[1 - core] = got[...]
+    for number, ref in enumerate(given):
+        entry[group_at(number < STREAMS, number % STREAMS)] = ref[...]
     scale = jnp.broadcast_to(stats[:, 0:1], shape)
     factor = jnp.broadcast_to(stats[:, 1:2], shape)
     decay = jnp.exp(cols[1])
@@ -380,7 +399,7 @@
         out_sums += head_sums(rounded * (mix - skip * values), pair)
         skip_sums += head_sums(grad_mix * values, pair)
         weighted = (by_head(decay, pair, shape) * grad_mix).astype(BF16)
-        read_grad += dot(weighted, get_state(entry.at[pair // half], pair, half), (1, 1))
+        read_grad += dot(weighted, get_state(entry.at[pair // group], pair % group), (1, 1))
     sums[...] = out_sums
     grad_read[...] = jnp.concatenate([jnp.zeros_like(read_grad), read_grad], axis=1)
     grad_small[...] = jnp.zeros_like(grad_small)
@@ -439,74 +458,81 @@
     whole[taps : taps + 1, here] = jnp.sum(grad_pre, axis=0, keepdims=True)
 
 
-def close_side(taps, side, rows, conv, slope, cols, entry, leave, grad_values, slopes, whole):
+def close_group(taps, number, rows, conv, slope, cols, entry, leave, grad_values, slopes, whole):
     length, features = grad_values.shape
-    half = features // LANES // 2
+    group = leave.shape[0] // N
     shape = (length, LANES)
     write = conv[:, features : features + N]
     running = cols[1]
-    tail = side_columns(jnp.exp(running[length - 1 : length, :] - running) * cols[0], side, half)
+    tail = jnp.exp(running[length - 1 : length, :] - running) * cols[0]
+    tail = pltpu.roll(tail, lax.rem(LANES - 2 * group * number, LANES), 1)
     state_sums = jnp.zeros(shape, F32)
     end_sums = jnp.zeros((8, LANES), F32)
     write_grad = jnp.zeros((length, N), F32)
-    for pair in range(half):
-        here = side_block(side * half + pair)
-        leaving = get_state(leave, pair, half)
+    for pair in range(group):
+        here = side_block(number * group + pair)
+        leaving = get_state(leave, pair)
         values = conv[:, here].astype(F32)
         tail_wide = by_head(tail, pair, shape)
         state_grad = tail_wide * dot(write, leaving)
         state_sums += head_sums(values * state_grad, pair)
         write_grad += dot((tail_wide * values).astype(BF16), leaving, (1, 1))
-        entering = get_state(entry, pair, half).astype(F32)
+        entering = get_state(entry, pair).astype(F32)
         overlap = jnp.sum(leaving.astype(F32) * entering, axis=0, keepdims=True)
         end_sums += head_sums(jnp.broadcast_to(overlap, (8, LANES)), pair)
         through_conv(taps, here, grad_values[:, here] + state_grad, rows, slope, slopes, whole)
-    back = 2 * half * side
+    back = 2 * group * number
+    write_grad = jnp.concatenate([write_grad, jnp.zeros_like(write_grad)], axis=1)
     return pltpu.roll(state_sums, back, 1), pltpu.roll(end_sums, back, 1), write_grad
 
 
-def close_own_kernel(
-    taps, rows, conv, slope, cols, entry, leave, grad_values, slopes, whole, state_out, end_out, write_out
-):
+def close_side(taps, own, rows, conv, slope, cols, entries, leaves, grad_values, slopes, whole):
+    totals = None
+    for stream, (entry, leave) in enumerate(zip(entries, leaves)):
+        sums = close_group(
+            taps, group_at(own, stream), rows, conv, slope, cols, entry, leave, grad_values, slopes, whole
+        )
+        totals = sums if totals is None else [a + b for a, b in zip(totals, sums)]
+    return totals
+
+
+def close_own_kernel(taps, rows, conv, slope, cols, grad_values, *refs):
+    given, (slopes, whole, state_out, end_out, write_out) = refs[: 2 * STREAMS], refs[2 * STREAMS :]
     length, channels = conv.shape
     slopes[0:HALO, :] = jnp.zeros((HALO, channels), F32)
     slopes[HALO + length :, :] = jnp.zeros((HALO, channels), F32)
     whole[...] = jnp.zeros_like(whole)
-    state_sums, end_sums, write_grad = close_side(
-        taps, here_at()[0], rows, conv, slope, cols, entry, leave, grad_values, slopes, whole
-    )
-    state_out[...] = state_sums
-    end_out[...] = end_sums
-    write_out[...] = jnp.concatenate([write_grad, jnp.zeros_like(write_grad)], axis=1)
+    state_out[...], end_out[...], write_out[...] = close_side(
+        taps, True, rows, conv, slope, cols, given[:STREAMS], given[STREAMS:], grad_values, slopes, whole
+    )
 
 
 def close_kernel(
-    taps, sizes, slopes_in, whole_in, rows, conv, slope, cols, small, entry, leave, grad_values, grad_vecs, out_sums, in_sums,
-    grad_gain, grad_small, state_in, end_in, write_in, slopes, whole, grad_dt, *rest
+    taps, sizes, slopes_in, whole_in, rows, conv, slope, cols, small, grad_values, grad_vecs, out_sums, in_sums,
+    grad_gain, grad_small, state_in, end_in, write_in, *rest
 ):
-    outs, cut = rest[:-1], rest[-1]
+    given, (slopes, whole, grad_dt, *outs, cut) = rest[: 2 * STREAMS], rest[2 * STREAMS :]
     parts = len(outs)
-    core, _, position_here = here_at()
+    position_here = here_at()[2]
     length, channels = conv.shape
     width, gain_width, heads_here = sizes
     heads = heads_here * parts
     step = cols[0]
     last = cols[1, length - 1 : length, :]
     state_sums, end_sums, write_grad = close_side(
-        taps, 1 - core, rows, conv, slope, cols, entry, leave, grad_values, slopes, whole
+        taps, False, rows, conv, slope, cols, given[:STREAMS], given[STREAMS:], grad_values, slopes, whole
     )
     state_sums = state_sums + state_in[...]
     end_sums = end_sums + end_in[...]
-    vecs = grad_vecs[...] + write_in[...]
-    vecs = vecs + jnp.concatenate([write_grad, jnp.zeros_like(write_grad)], axis=1)
+    vecs = grad_vecs[...] + (write_in[...] + write_grad)
     through_conv(taps, block(channels // LANES - 1), vecs, rows, slope, slopes, whole)
 
     into = in_sums[...] + state_sums
     change = out_sums[...] - into
     end_grad = jnp.sum(state_sums, axis=0, keepdims=True) + jnp.exp(last) * end_sums[0:1, :]
     square = (length, length)
-    upper = (iota(square, 0) <= iota(square, 1)).astype(F32)
-    log_grad = dot(upper, change, precision=HIGH) + end_grad
+    upper = iota(square, 0) <= iota(square, 1)
+    log_grad = dot_parts(upper, change, 3) + end_grad
     rate = jnp.exp(small[1:2, :])
     raw_grad = (into / step - rate * log_grad) * (1.0 - jnp.exp(-step))
     grad_dt[...] = raw_grad.T[0:heads, :]
@@ -530,15 +556,21 @@
         outs[distance][...] = cut[lax.rem(position_here + distance, parts)]
 
 
-def input_kernel(taps, full, slopes, grad_x, ending, back):
+def input_kernel(taps, full, slopes, grad_x, ending):
     length, channels = grad_x.shape
-    folded = back.shape[1] // LANES
-    back[...] = jnp.zeros_like(back)
     for position in range(channels // LANES):
         here = block(position)
         total = through_taps(taps, full, slopes, here, HALO, length)
         grad_x[:, here] = total.astype(BF16)
         ending[:, here] = total[length - 2 * HALO :]
+
+
+def before_kernel(taps, full, slopes, back):
+    channels = slopes.shape[1]
+    folded = back.shape[1] // LANES
+    back[...] = jnp.zeros_like(back)
+    for position in range(channels // LANES):
+        here = block(position)
         ahead = through_taps(taps, full, slopes, here, 0, HALO)
         for tap in range(taps - 1):
             at = tap * FOLDS + position // folded
@@ -598,15 +630,15 @@
     return message[0:end, :].astype(F32), unpack_decays(message[end:, :])
 
 
-def decayed(state, decay, half):
-    cuts = state.shape[0] // (half * CUT)
-    split_rows = state.reshape(cuts, half, CUT, LANES)
-    return (split_rows * decay[0:half].reshape(1, half, 1, LANES)).reshape(state.shape)
-
-
-def joined(first, second, half):
+def decayed(state, decay):
+    group = state.shape[0] // N
+    split_rows = state.reshape(group, N, LANES)
+    return (split_rows * decay[0:group].reshape(group, 1, LANES)).reshape(state.shape)
+
+
+def joined(first, second):
     state, decay = second
-    return decayed(first[0], decay, half) + state, decay * first[1]
+    return decayed(first[0], decay) + state, decay * first[1]
 
 
 def store(out, value):
@@ -620,58 +652,33 @@
     return jnp.where(later, b, a), jnp.where(later, a, b)
 
 
-def meet_kernel(half, reverse, mine, got, out):
+def meet_kernel(reverse, mine, got, out, decay):
     later = here_at()[0] == (0 if reverse else 1)
     first, second = ordered(later, mine[...], got[...])
-    store(out, joined(parts_of(first), parts_of(second), half))
-
-
-def join_kernel(half, first, second, out):
-    store(out, joined(parts_of(first[...]), parts_of(second[...]), half))
-
-
-def meet_chain_kernel(half, reverse, mine, got, decay_out, *outs):
-    later = here_at()[0] == (0 if reverse else 1)
-    rows = outs[0].shape[0]
-    end = rows * len(outs)
-    early, late = ordered(later, mine[end:, :], got[end:, :])
-    early, late = unpack_decays(early), unpack_decays(late)
-    decay_out[...] = early * late
-    for number, out in enumerate(outs):
-        here = slice(number * rows, (number + 1) * rows)
-        first, second = ordered(later, mine[here, :], got[here, :])
-        out[...] = (decayed(first.astype(F32), late, half) + second.astype(F32)).astype(BF16)
-
-
-def pass_kernel(half, before, own, decay, out):
-    state = decayed(before[...].astype(F32), decay[...], half)
-    out[...] = (state + own[...].astype(F32)).astype(BF16)
-
-
-def enter_chain_kernel(half, reverse, streams, *refs):
+    whole = joined(parts_of(first), parts_of(second))
+    store(out, whole)
+    decay[...] = whole[1]
+
+
+def join_kernel(first, second, out):
+    store(out, joined(parts_of(first[...]), parts_of(second[...])))
+
+
+def pass_kernel(before, own, decay, out):
+    end = out.shape[0]
+    state = decayed(before[0:end, :].astype(F32), decay[...])
+    out[...] = (state + own[0:end, :].astype(F32)).astype(BF16)
+
+
+def enter_kernel(reverse, *refs):
     given, (mine, got, own, send) = refs[:-4], refs[-4:]
     later = here_at()[0] == (0 if reverse else 1)
-    rows = given[0].shape[0]
-    end = rows * streams
-    decay = unpack_decays(ordered(later, mine[end:, :], got[end:, :])[0])
-    for number in range(streams):
-        here = slice(number * rows, (number + 1) * rows)
-        start = given[number][...].astype(F32)
-        for ref in given[streams + number :: streams]:
-            start = start + ref[...].astype(F32)
-        first = ordered(later, mine[here, :], got[here, :])[0]
-        after = decayed(start, decay, half) + first.astype(F32)
-        own[here, :] = jnp.where(later, after, start).astype(BF16)
-        send[here, :] = jnp.where(later, start, after).astype(BF16)
-
-
-def enter_kernel(half, reverse, entering, mine, got, own, send):
-    later = here_at()[0] == (0 if reverse else 1)
     end = own.shape[0]
-    start = entering[0:end, :].astype(F32)
-    first = ordered(later, mine[...], got[...])[0]
-    state, decay = parts_of(first)
-    after = decayed(start, decay, half) + state
+    start = given[0][0:end, :].astype(F32)
+    for ref in given[1:]:
+        start = start + ref[0:end, :].astype(F32)
+    state, decay = parts_of(ordered(later, mine[...], got[...])[0])
+    after = decayed(start, decay) + state
     own[...] = jnp.where(later, after, start).astype(BF16)
     send[...] = jnp.where(later, start, after).astype(BF16)
 
@@ -716,59 +723,54 @@
     return shift(value, "seq", lambda i: 2 * routes[i // 2] + i % 2 if i // 2 in routes else -1)
 
 
-def entering_states(mine, got, half, reverse, beside):
+def entering_states(own_states, got, reverse, beside):
     chips = lax.axis_size("seq") // 2
-    entry = like((mine.shape[0] - DEC_ROWS, LANES), BF16)
+    message = like(got[0].shape, BF16)
+    entry = like((got[0].shape[0] - DEC_ROWS, LANES), BF16)
+    chip, decays, mine = [], [], []
+    for stream, other in enumerate(got):
+        mine.append(own_states(stream, chip))
+        whole, decay = call(
+            functools.partial(meet_kernel, reverse),
+            [message, like((DEC_ROWS, LANES))],
+            [mine[-1], other],
+            name="meet",
+        )
+        chip.append(whole)
+        decays.append(decay)
     if 1 < chips <= 4:
         order = list(range(chips))[::-1] if reverse else list(range(chips))
-        stream = like((entry.shape[0] // STREAMS, LANES), BF16)
-        decay, *chip = call(
-            functools.partial(meet_chain_kernel, half, reverse),
-            [like((DEC_ROWS, LANES))] + [stream] * STREAMS,
-            [mine, got],
-            name="meet",
-        )
-        arrived = []
+        arrived = [[] for _ in chip]
         moving = chip
         for hop in range(chips - 1):
             route = {order[hop]: order[hop + 1]}
             landed = [between_chips(part, route) for part in moving]
             if hop < len(beside):
-                landed[0] = beside[hop](moving, landed[0])
-            arrived += landed
+                landed = beside[hop](moving, landed)
+            for stream, part in zip(arrived, landed):
+                stream.append(part)
             if hop < chips - 2:
                 moving = [
-                    call(functools.partial(pass_kernel, half), [stream], [part, own, decay], name="pass")[0]
-                    for part, own in zip(landed, chip)
+                    call(pass_kernel, [entry], list(parts), name="pass")[0] for parts in zip(landed, chip, decays)
                 ]
-        own, send = call(
-            functools.partial(enter_chain_kernel, half, reverse, STREAMS),
-            [entry, entry],
-            arrived + [mine, got],
-            name="enter",
-        )
-        return own, shift(send, "seq", lambda i: i ^ 1)
-    sign = -1 if reverse else 1
-    message = like(mine.shape, BF16)
-    chip = call(functools.partial(meet_kernel, half, reverse), [message], [mine, got], name="meet")[0]
-    before = shift(chip, "seq", lambda i: i + 2 * sign)
-    before = beside[0]([chip], before)
-    join = functools.partial(join_kernel, half)
-    window = 1
-    while window < chips - 1:
-        longer = call(join, [message], [before, chip], name="join")[0]
-        distance = window + 1
-        far = shift(longer, "seq", lambda i: i + 2 * distance * sign)
-        before = call(join, [message], [far, before], name="join")[0]
-        window = 2 * window + 1
-    before = beside[1]([before], before)
-    own, send = call(
-        functools.partial(enter_kernel, half, reverse),
-        [entry, entry],
-        [before, mine, got],
-        name="enter",
-    )
-    return own, shift(send, "seq", lambda i: i ^ 1)
+    else:
+        sign = -1 if reverse else 1
+        before = [shift(part, "seq", lambda i: i + 2 * sign) for part in chip]
+        before = beside[1](chip, beside[0](chip, before))
+        window = 1
+        while window < chips - 1:
+            distance = window + 1
+            longer = [call(join_kernel, [message], pair, name="join")[0] for pair in zip(before, chip)]
+            far = [shift(part, "seq", lambda i: i + 2 * distance * sign) for part in longer]
+            before = [call(join_kernel, [message], pair, name="join")[0] for pair in zip(far, before)]
+            window = 2 * window + 1
+        arrived = [[part] for part in before]
+    owns, others = [], []
+    for parts, a, b in zip(arrived, mine, got):
+        own, send = call(functools.partial(enter_kernel, reverse), [entry, entry], parts + [a, b], name="enter")
+        owns.append(own)
+        others.append(shift(send, "seq", lambda i: i ^ 1))
+    return owns, others
 
 
 def after(value, *signals):
@@ -814,12 +816,15 @@
         megabytes=60,
         name="open",
     )
-    pieces = [shift(piece, "fsdp", lambda i: (i + distance) % parts) for distance in range(1, parts)]
+    pieces = [shift(piece, "fsdp", lambda i: peer(i, distance, parts)) for distance in range(1, parts)]
     halo = shift(halo, "seq", lambda i: i + 1)
     lifted = jnp.pad(after(x, piece).astype(F32), ((HALO, 0), (0, 0)))
 
-    message = like((half * N + DEC_ROWS, LANES), BF16)
-    entry = pltpu.VMEM((2, half * N, LANES), BF16)
+    group = half // STREAMS
+    message = like((group * N + DEC_ROWS, LANES), BF16)
+    entry = pltpu.VMEM((2 * STREAMS, group * N, LANES), BF16)
+    wide = like((length, features))
+    square = like((length, LANES))
     full, gain, small, cols, rows, decs = call(
         functools.partial(gather_kernel, taps, sizes, parts, length),
         [
@@ -828,65 +833,91 @@
             like((8, LANES)),
             like((2, length, LANES)),
             like((3, LANES, length)),
-            like((2, DEC_ROWS, LANES), BF16),
+            like((2 * STREAMS, DEC_ROWS, LANES), BF16),
         ],
         [own] + pieces,
         [pltpu.VMEM((LANES, LANES), F32), pltpu.VMEM((parts, SMALL, piece_width), F32)],
         name="gather",
     )
+    conv_like = like((length, channels), BF16)
     padded, conv, write_t, other = call(
         functools.partial(front_kernel, taps),
-        [like(lifted.shape), like((length, channels), BF16), like((N, length)), message],
+        [like(lifted.shape), conv_like, like((N, length)), message],
         [lifted, halo, full, rows, decs],
         name="front",
         aliases={0: 0},
     )
-    got = shift(other, "seq", lambda i: i ^ 1)
-    conv, mine = call(
-        functools.partial(front_own_kernel, taps),
-        [like((length, channels), BF16), message],
-        [conv, padded, full, rows, decs, write_t],
-        name="own",
-        aliases={0: 0},
-    )
+    got = [shift(other, "seq", lambda i: i ^ 1)]
+    for stream in range(1, STREAMS):
+        conv, other = call(
+            functools.partial(front_next_kernel, taps, False, (stream,)),
+            [conv_like, message],
+            [conv, padded, full, rows, decs, write_t],
+            name="front",
+            aliases={0: 0},
+        )
+        got.append(shift(other, "seq", lambda i: i ^ 1))
+    held = [conv]
+
+    def own_first(stream, signals):
+        held[0], mine = call(
+            functools.partial(front_next_kernel, taps, True, (stream,)),
+            [conv_like, message],
+            [after(held[0], *signals), padded, full, rows, decs, write_t],
+            name="own",
+            aliases={0: 0},
+        )
+        return mine
+
     work = {}
 
     def intra(signal, value):
         work["local"], work["slope"] = call(
             functools.partial(intra_kernel, taps),
-            [like((length, features)), like((length, channels))],
-            [padded, full, after(conv, *signal), cols, rows, small],
+            [wide, like((length, channels))],
+            [padded, full, after(held[0], *signal), cols, rows, small],
             flops=2 * length * length * features,
             name="intra",
         )
-        return after(value, work["local"])
-
-    def nothing(signal, value):
-        return value
-
-    entry_own, entry_got = entering_states(mine, got, half, False, (intra, nothing))
-    wide = like((length, features))
-    square = like((length, LANES))
-    mixed, gated, silus, sums = call(
-        norm_own_kernel,
-        [wide, wide, wide, like((2, length, LANES))],
-        [work["local"], conv, cols, gate, grad, gain, entry_own],
-        name="norm_own",
-    )
-    mixed, gated, silus, stats, other = call(
+        return [after(part, work["local"]) for part in value]
+
+    def factors(signal, value):
+        work["factors"] = call(
+            factor_kernel,
+            [wide] * 3,
+            [after(cols, *signal), gate, grad, gain],
+            flops=length * features * 16,
+            name="factors",
+        )
+        return [after(part, work["factors"][0]) for part in value]
+
+    sums_like = like((2, length, LANES))
+
+    entry_own, entry_got = entering_states(own_first, got, False, (intra, factors))
+    conv = held[0]
+    silus, grown, decays = work["factors"]
+    given = [work["local"], conv, silus, grown, decays]
+    mixed, gated, sums = call(mix_kernel, [wide, wide, sums_like], given + entry_own, name="mix")
+    mixed, gated, stats, other = call(
         norm_kernel,
-        [wide, wide, wide, square, message],
-        [mixed, gated, silus, work["local"], conv, cols, gate, grad, gain, entry_got, sums, decs],
+        [wide, wide, square, message],
+        [mixed, gated] + given + [sums, decs] + entry_got,
         name="norm",
-        aliases={0: 0, 1: 1, 2: 2},
-    )
-    got = shift(other, "seq", lambda i: i ^ 1)
-    mine = call(
-        norm_last_kernel,
-        [message],
-        [stats, conv, cols, grad, gain, gated, silus, decs],
-        name="norm_last",
-    )[0]
+        aliases={0: 0, 1: 1},
+    )
+    got = [shift(other, "seq", lambda i: i ^ 1)]
+    given = [conv, silus, grown, decays, gated, decs]
+
+    def norm_next(own, stream, signals):
+        return call(
+            functools.partial(norm_next_kernel, own, (stream,)),
+            [message],
+            [after(stats, *signals)] + given,
+            name="norm_next",
+        )[0]
+
+    for stream in range(1, STREAMS):
+        got.append(shift(norm_next(False, stream, []), "seq", lambda i: i ^ 1))
 
     def gates(signal, value):
         work["gates"] = call(
@@ -899,12 +930,12 @@
                 like((8, LANES)),
                 like((length, LANES)),
             ],
-            [mixed, after(conv, *signal), cols, small, gate, grad, gain, stats, entry_own, entry_got],
+            [mixed, after(conv, *signal), cols, small, gate, grad, gain, stats] + entry_own + entry_got,
             [entry],
                 flops=2 * length * length * features,
             name="gates",
         )
-        return after(value, work["gates"][0])
+        return [after(part, work["gates"][0]) for part in value]
 
     def back(signal, value):
         grad_mixed, grad_read = work["gates"][1], work["gates"][5]
@@ -915,22 +946,25 @@
             flops=4 * length * length * features,
             name="back",
         )
-        return after(value, work["back"][0])
-
-    leave_own, leave_got = entering_states(mine, got, half, True, (gates, back))
+        return [after(part, work["back"][0]) for part in value]
+
+    shapes = [like((2 * HALO + length, channels)), like((SMALL, full_width)), square, like((8, LANES)), square]
+    fixed = [padded, conv, work["slope"], cols]
+
+    leave_own, leave_got = entering_states(functools.partial(norm_next, True), got, True, (gates, back))
     grad_gate, _, out_sums, grad_gain, grad_small, _ = work["gates"]
     grad_values, in_sums, grad_vecs = work["back"]
-    slopes, whole, state_sums, end_sums, write_grad = call(
+    slopes, whole, *sums = call(
         functools.partial(close_own_kernel, taps),
-        [like((2 * HALO + length, channels)), like((SMALL, full_width)), square, like((8, LANES)), square],
-        [padded, conv, work["slope"], cols, entry_own, leave_own, grad_values],
+        shapes,
+        fixed + [grad_values] + entry_own + leave_own,
         name="close_own",
     )
     slopes, whole, grad_dt, *shares = call(
         functools.partial(close_kernel, taps, sizes),
-        [like(slopes.shape), like(whole.shape), like((heads, length))] + [piece_like] * parts,
-        [slopes, whole, padded, conv, work["slope"], cols, small, entry_got, leave_got, grad_values, grad_vecs, out_sums]
-        + [in_sums, grad_gain, grad_small, state_sums, end_sums, write_grad],
+        shapes[:2] + [like((heads, length))] + [piece_like] * parts,
+        [slopes, whole] + fixed + [small, grad_values, grad_vecs, out_sums, in_sums, grad_gain, grad_small]
+        + sums + entry_got + leave_got,
         [pltpu.VMEM((parts, SMALL, piece_width), F32)],
         name="close",
         aliases={0: 0, 1: 1},
@@ -938,14 +972,9 @@
     terms = [shares[0]]
     for distance in range(1, parts):
         terms.append(shift(shares[distance], "fsdp", lambda i: (i + distance) % parts))
-    grad_x, ending, earlier = call(
-        functools.partial(input_kernel, taps),
-        [like((length, channels), BF16), like((2 * HALO, channels)), like((BACK_ROWS, piece_width))],
-        [full, slopes],
-        flops=length * channels * 16,
-        name="inputs",
-    )
-    terms[1] = after(terms[1], ending)
+    earlier = call(
+        functools.partial(before_kernel, taps), [like((BACK_ROWS, piece_width))], [full, slopes], name="before"
+    )[0]
     bundle = like((SMALL + BACK_ROWS, piece_width))
     total = call(add_kernel, [bundle], terms + [earlier], name="add")[0]
     partner = shift(total, "seq", lambda i: i ^ 1)
@@ -960,6 +989,13 @@
         terms += [behind] if chips > 1 else []
     else:
         terms = [lax.psum(alone, "seq") * 0.5]
+    grad_x, ending = call(
+        functools.partial(input_kernel, taps),
+        [like((length, channels), BF16), like((2 * HALO, channels))],
+        [full, after(slopes, alone)],
+        flops=length * channels * 16,
+        name="inputs",
+    )
     grad_x, cw, cb, dtb, al, sk, gn = call(
         functools.partial(unpack_kernel, len(terms), chips, taps),
         [

time: 85.3 us -> 84 us (0.985)
  waiting for transfers between devices: 24.6 us -> 19.2 us
  starting transfers between devices: 26.6 us -> 29.2 us
  Pallas kernels: 31.1 us -> 32.6 us
    ppermute x27 -> x31, waiting for transfers between devices: 24.6 us -> 19.2 us  [shift(): lax.ppermute(value, axis, [(i, j) for i, j in pairs if 0 <= j < count])]
    ppermute x27 -> x31, starting transfers between devices: 26.6 us -> 29.2 us  [shift(): lax.ppermute(value, axis, [(i, j) for i, j in pairs if 0 <= j < count])]
    pallas_call x28 -> x38, Pallas kernels: 31.1 us -> 32.6 us  [call(): pl.pallas_call(kernel, out_shape=outs, in_specs=specs, out_specs=[pl.Bloc...]
  transfers between devices with their start and end apart: 27 -> 31, of which waited for: 11 -> 12; matrix products, arithmetic and copies ran while one was open for 2% -> 2% of each run, Pallas kernels for 25% -> 29%
where the time goes in v3:
time: 84 us; the launch traced here: 83.6 us
  Pallas kernels  32.6 us (39%)
  starting transfers between devices  29.2 us (35%)
  waiting for transfers between devices  19.2 us (23%)
  other arithmetic  1.32 us (2%)
  between operations  1.29 us (2%)
    pallas_call x38, Pallas kernels, call(): pl.pallas_call(kernel, out_shape=outs, in_specs=specs, out_specs=[pl.Bloc...  32.6 us
    ppermute x31, starting transfers between devices, shift(): lax.ppermute(value, axis, [(i, j) for i, j in pairs if 0 <= j < count])  29.2 us
    ppermute x31, waiting for transfers between devices, shift(): lax.ppermute(value, axis, [(i, j) for i, j in pairs if 0 <= j < count])  19.2 us
  transfers between devices with their start and end apart: 31, of which 12 were waited for; matrix products, arithmetic and copies ran while one was open for 2% of the time, Pallas kernels for 29%

profile of v3, /device:TPU:0, one launch (start us, length us, event | category | flops | bytes accessed | tf_op | source)
XLA Modules:
  0.0 83.6 jit_solution(16612513169108706092)
XLA Ops:
  0.6 1.8 %open.1 = (bf16[8,3712]{1,0:T(8,128)(2,1)}, f32[8,1024]{1,0:T(8,128)}, f32[16,1024]{1,0:T(8,128)}) custom-call(bf16[128,3712]{1,0:T(8,128)(2,1)} %bitcast.22, f32[56,128]{1,0:T(8,128)} %bitcast.25, f32[4,928]{1,0:T(4,128)} %cw.1, f32[1,928]{1,0:T(1,128)} %bitcast.26, f32[1,14]{1,0:T(1,128)} %bitcast.27, f32[1,14]{1,0:T(1,128)} %bitcast.28, ...), custom_call_target="tpu_custom_call" | custom-call | bytes 1158952 | tf_op jit(solution)/shard_map/open/pallas_call | solution.py:696
  2.4 4.0 %collective-permute-start.2 = (f32[8,1024]{1,0:T(8,128)}, f32[8,1024]{1,0:T(8,128)S(1)}, u32[]{:S(2)}, u32[]{:S(2)}) collective-permute-start(f32[8,1024]{1,0:T(8,128)} %get-tuple-element.104), channel_id=1, source_target_pairs={{0,24},{8,16},{16,8},{24,0},{1,25},{9,17},{17,9},{25,1},{2,26},{10... | collective-permute-start | bytes 98312 | tf_op jit(solution)/shard_map/ppermute | solution.py:719
  8.3 1.3 %pad_convert_fusion.lifted = f32[136,3712]{1,0:T(8,128)S(1)} fusion(bf16[128,3712]{1,0:T(8,128)(2,1)} %bitcast.23), kind=kLoop, calls=%fused_computation | loop fusion | flops 504832 | bytes 2969600 | tf_op jit(solution)/shard_map/jit(_pad)/pad | solution.py:821
  12.4 1.4 %collective-permute-start.4 = (bf16[464,128]{1,0:T(8,128)(2,1)S(1)}, bf16[464,128]{1,0:T(8,128)(2,1)S(1)}, u32[]{:S(2)}, u32[]{:S(2)}) collective-permute-start(bf16[464,128]{1,0:T(8,128)(2,1)S(1)} %get-tuple-element.116), channel_id=1, source_target_pairs={{0,1},{1,0},{2,3},{3,2},{4,5},{5,4},{6,7},{7,6},{8,9},{9,8},{10,11... | collective-permute-start | bytes 356360 | tf_op jit(solution)/shard_map/ppermute | solution.py:719
  15.4 4.2 %collective-permute-start.6 = (bf16[464,128]{1,0:T(8,128)(2,1)S(1)}, bf16[464,128]{1,0:T(8,128)(2,1)S(1)}, u32[]{:S(2)}, u32[]{:S(2)}) collective-permute-start(bf16[464,128]{1,0:T(8,128)(2,1)S(1)} %get-tuple-element.117.own), channel_id=1, source_target_pairs={{0,2},{1,3},{8,10},{9,11},{16,18},{17,19},{24,26},{25,27}} | collective-permute-start | bytes 356360 | tf_op jit(solution)/shard_map/ppermute | solution.py:719
  20.5 1.3 %collective-permute-start.7 = (bf16[464,128]{1,0:T(8,128)(2,1)S(1)}, bf16[464,128]{1,0:T(8,128)(2,1)S(1)}, u32[]{:S(2)}, u32[]{:S(2)}) collective-permute-start(bf16[464,128]{1,0:T(8,128)(2,1)S(1)} %get-tuple-element.122.own), channel_id=1, source_target_pairs={{0,2},{1,3},{8,10},{9,11},{16,18},{17,19},{24,26},{25,27}} | collective-permute-start | bytes 356360 | tf_op jit(solution)/shard_map/ppermute | solution.py:719
  21.8 3.0 %intra.1 = (f32[128,3584]{1,0:T(8,128)S(1)}, f32[128,3712]{1,0:T(8,128)S(1)}) custom-call(f32[136,3712]{1,0:T(8,128)S(1)} %get-tuple-element.110.rows, f32[8,3840]{1,0:T(8,128)S(1)} %get-tuple-element.105.full, bf16[128,3712]{1,0:T(8,128)(2,1)S(1)} %get-tuple-element.153.conv, f32[2,128,128]{2,1,0:T(8,128)S(1)} %get-tuple-element.132.cols, ...), custom_call_target="tpu_custom_call" | custom-call | flops 117440512 | bytes 7159808 | tf_op jit(solution)/shard_map/intra/pallas_call | solution.py:696
  26.3 1.6 %factors.1 = (f32[128,3584]{1,0:T(8,128)S(1)}, f32[128,3584]{1,0:T(8,128)S(1)}, f32[128,3584]{1,0:T(8,128)S(1)}) custom-call(f32[2,128,128]{2,1,0:T(8,128)S(1)} %get-tuple-element.132.cols, bf16[128,3584]{1,0:T(8,128)(2,1)S(1)} %bitcast.18, bf16[128,3584]{1,0:T(8,128)(2,1)S(1)} %bitcast.20, f32[1,3584]{1,0:T(1,128)S(1)} %get-tuple-element.133.gain), custom_call_target="tpu_custom_call" | custom-call | flops 7340032 | bytes 7485440 | tf_op jit(solution)/shard_map/factors/pallas_call | solution.py:696
  36.6 4.0 %gates.1 = (bf16[128,3584]{1,0:T(8,128)(2,1)}, f32[128,3584]{1,0:T(8,128)S(1)}, f32[128,128]{1,0:T(8,128)S(1)}, f32[1,3584]{1,0:T(1,128)S(1)}, f32[8,128]{1,0:T(8,128)S(1)}, /*index=5*/f32[128,128]{1,0:T(8,128)S(1)}) custom-call(f32[128,3584]{1,0:T(8,128)S(1)} %get-tuple-element.146.mixed, bf16[128,3712]{1,0:T(8,128)(2,1)S(1)} %get-tuple-element.153.conv, ...), custom_call_target="tpu_custom_call" | custom-call | flops 117440512 | bytes 8196096 | tf_op jit(solution)/shard_map/gates/pallas_call | solution.py:696
  42.0 5.5 %back.1 = (f32[128,3584]{1,0:T(8,128)S(1)}, f32[128,128]{1,0:T(8,128)S(1)}, f32[128,128]{1,0:T(8,128)S(1)}) custom-call(f32[128,3584]{1,0:T(8,128)S(1)} %get-tuple-element.160.grad_mixed, bf16[128,3712]{1,0:T(8,128)(2,1)S(1)} %get-tuple-element.153.conv, f32[2,128,128]{2,1,0:T(8,128)S(1)} %get-tuple-element.132.cols, ...), custom_call_target="tpu_custom_call" | custom-call | flops 234881024 | bytes 5148672 | tf_op jit(solution)/shard_map/back/pallas_call | solution.py:696
  47.5 1.3 %collective-permute-start.21 = (bf16[448,128]{1,0:T(8,128)(2,1)S(1)}, bf16[448,128]{1,0:T(8,128)(2,1)S(1)}, u32[]{:S(2)}, u32[]{:S(2)}) collective-permute-start(bf16[448,128]{1,0:T(8,128)(2,1)S(1)} %pass.15), channel_id=1, source_target_pairs={{2,0},{3,1},{10,8},{11,9},{18,16},{19,17},{26,24},{27,25}} | collective-permute-start | bytes 344072 | tf_op jit(solution)/shard_map/ppermute | solution.py:719
  48.9 1.5 %collective-permute-start.19 = (bf16[448,128]{1,0:T(8,128)(2,1)S(1)}, bf16[448,128]{1,0:T(8,128)(2,1)S(1)}, u32[]{:S(2)}, u32[]{:S(2)}) collective-permute-start(bf16[448,128]{1,0:T(8,128)(2,1)S(1)} %pass.14), channel_id=1, source_target_pairs={{2,0},{3,1},{10,8},{11,9},{18,16},{19,17},{26,24},{27,25}} | collective-permute-start | bytes 344072 | tf_op jit(solution)/shard_map/ppermute | solution.py:719
  50.4 9.4 %collective-permute-done.21.refs_2_ = bf16[448,128]{1,0:T(8,128)(2,1)S(1)} collective-permute-done((bf16[448,128]{1,0:T(8,128)(2,1)S(1)}, bf16[448,128]{1,0:T(8,128)(2,1)S(1)}, u32[]{:S(2)}, u32[]{:S(2)}) %collective-permute-start.21) | collective-permute-done | bytes 114720 | tf_op jit(solution)/shard_map/ppermute | solution.py:719
  60.0 1.9 %collective-permute-done.19.refs_2_ = bf16[448,128]{1,0:T(8,128)(2,1)S(1)} collective-permute-done((bf16[448,128]{1,0:T(8,128)(2,1)S(1)}, bf16[448,128]{1,0:T(8,128)(2,1)S(1)}, u32[]{:S(2)}, u32[]{:S(2)}) %collective-permute-start.19) | collective-permute-done | bytes 114720 | tf_op jit(solution)/shard_map/ppermute | solution.py:719
  62.1 2.0 %close_own.1 = (f32[144,3712]{1,0:T(8,128)S(1)}, f32[8,3840]{1,0:T(8,128)S(1)}, f32[128,128]{1,0:T(8,128)S(1)}, f32[8,128]{1,0:T(8,128)S(1)}, f32[128,128]{1,0:T(8,128)S(1)}) custom-call(f32[136,3712]{1,0:T(8,128)S(1)} %get-tuple-element.110.rows, bf16[128,3712]{1,0:T(8,128)(2,1)S(1)} %get-tuple-element.153.conv, f32[128,3712]{1,0:T(8,128)S(1)} %get-tuple-element.126.slope, ...), custom_call_target="tpu_custom_call" | custom-call | bytes 9691136 | tf_op jit(solution)/shard_map/close_own/pallas_call | solution.py:696
  64.1 2.8 %close.1 = (f32[144,3712]{1,0:T(8,128)S(1)}, f32[8,3840]{1,0:T(8,128)S(1)}, f32[56,128]{1,0:T(8,128)}, f32[8,1024]{1,0:T(8,128)S(1)}, f32[8,1024]{1,0:T(8,128)S(...) custom-call(f32[144,3712]{1,0:T(8,128)S(1)} %get-tuple-element.167.slopes_in, ...), custom_call_target="tpu_custom_call", output_to_operand_aliasing={{0}: (0, {}), {1}: (1, {})} | custom-call | bytes 12331008 | tf_op jit(solution)/shard_map/close/pallas_call | solution.py:696
  67.0 1.5 %collective-permute-start.24 = (f32[8,1024]{1,0:T(8,128)S(1)}, f32[8,1024]{1,0:T(8,128)S(1)}, u32[]{:S(2)}, u32[]{:S(2)}) collective-permute-start(f32[8,1024]{1,0:T(8,128)S(1)} %get-tuple-element.181), channel_id=1, source_target_pairs={{0,8},{8,16},{16,24},{24,0},{1,9},{9,17},{17,25},{25,1},{2,10},{10... | collective-permute-start | bytes 98312 | tf_op jit(solution)/shard_map/ppermute | solution.py:719
  68.5 1.5 %collective-permute-start.25 = (f32[8,1024]{1,0:T(8,128)S(1)}, f32[8,1024]{1,0:T(8,128)S(1)}, u32[]{:S(2)}, u32[]{:S(2)}) collective-permute-start(f32[8,1024]{1,0:T(8,128)S(1)} %get-tuple-element.182), channel_id=1, source_target_pairs={{0,16},{8,24},{16,0},{24,8},{1,17},{9,25},{17,1},{25,9},{2,18},{10... | collective-permute-start | bytes 98312 | tf_op jit(solution)/shard_map/ppermute | solution.py:719
  70.0 1.4 %collective-permute-start.26 = (f32[8,1024]{1,0:T(8,128)S(1)}, f32[8,1024]{1,0:T(8,128)S(1)}, u32[]{:S(2)}, u32[]{:S(2)}) collective-permute-start(f32[8,1024]{1,0:T(8,128)S(1)} %get-tuple-element.183), channel_id=1, source_target_pairs={{0,24},{8,0},{16,8},{24,16},{1,25},{9,1},{17,9},{25,17},{2,26},{10... | collective-permute-start | bytes 98312 | tf_op jit(solution)/shard_map/ppermute | solution.py:719
  72.4 1.5 %collective-permute-done.26.refs_3_ = f32[8,1024]{1,0:T(8,128)S(1)} collective-permute-done((f32[8,1024]{1,0:T(8,128)S(1)}, f32[8,1024]{1,0:T(8,128)S(1)}, u32[]{:S(2)}, u32[]{:S(2)}) %collective-permute-start.26) | collective-permute-done | bytes 32800 | tf_op jit(solution)/shard_map/ppermute | solution.py:719
  74.0 1.3 %collective-permute-done.27.other.from_core = f32[24,1024]{1,0:T(8,128)S(1)} collective-permute-done((f32[24,1024]{1,0:T(8,128)S(1)}, f32[24,1024]{1,0:T(8,128)S(1)}, u32[]{:S(2)}, u32[]{:S(2)}) %collective-permute-start.27) | collective-permute-done | bytes 98336 | tf_op jit(solution)/shard_map/ppermute | solution.py:719
  77.4 2.3 %inputs.1 = (bf16[128,3712]{1,0:T(8,128)(2,1)}, f32[16,3712]{1,0:T(8,128)S(1)}) custom-call(f32[8,3840]{1,0:T(8,128)S(1)} %get-tuple-element.105.full, f32[144,3712]{1,0:T(8,128)S(1)} %get-tuple-element.185.slopes), custom_call_target="tpu_custom_call" | custom-call | flops 7602176 | bytes 3448832 | tf_op jit(solution)/shard_map/inputs/pallas_call | solution.py:696
  80.3 1.8 %collective-permute-done.29.refs_1_ = f32[8,1024]{1,0:T(8,128)S(1)} collective-permute-done((f32[8,1024]{1,0:T(8,128)S(1)}, f32[8,1024]{1,0:T(8,128)S(1)}, u32[]{:S(2)}, u32[]{:S(2)}) %collective-permute-start.29) | collective-permute-done | bytes 32800 | tf_op jit(solution)/shard_map/ppermute | solution.py:719
  82.1 1.3 %unpack.1 = (bf16[128,3712]{1,0:T(8,128)(2,1)}, f32[4,928]{1,0:T(4,128)}, f32[928]{0:T(1024)}, f32[1,14]{1,0:T(1,128)}, f32[1,14]{1,0:T(1,128)}, /*index=5*/f32[1,14]{1,0:T(1,128)}, f32[896]{0:T(1024)}) custom-call(bf16[128,3712]{1,0:T(8,128)(2,1)} %get-tuple-element.186.grad_in, ...), custom_call_target="tpu_custom_call", output_to_operand_aliasing={{0}: (0, {})} | custom-call | bytes 2553640 | tf_op jit(solution)/shard_map/unpack/pallas_call | solution.py:696
  (83 shorter events, 22.7 us)
Async XLA Ops:
  2.4 7.2 %collective-permute-start.2 = (f32[8,1024]{1,0:T(8,128)}, f32[8,1024]{1,0:T(8,128)S(1)}, u32[]{:S(2)}, u32[]{:S(2)}) collective-permute-start(f32[8,1024]{1,0:T(8,128)} %get-tuple-element.104), channel_id=1, source_target_pairs={{0,24},{8,16},{16,8},{24,0},{1,25},{9,17},{17,9},{25,1},{2,26},{10... | collective-permute-start | bytes 98312 | tf_op jit(solution)/shard_map/ppermute | solution.py:719
  6.4 4.1 %collective-permute-start.1 = (f32[8,1024]{1,0:T(8,128)}, f32[8,1024]{1,0:T(8,128)S(1)}, u32[]{:S(2)}, u32[]{:S(2)}) collective-permute-start(f32[8,1024]{1,0:T(8,128)} %get-tuple-element.104), channel_id=1, source_target_pairs={{0,16},{8,24},{16,0},{24,8},{1,17},{9,25},{17,1},{25,9},{2,18},{10... | collective-permute-start | bytes 98312 | tf_op jit(solution)/shard_map/ppermute | solution.py:719
  6.9 4.1 %collective-permute-start = (f32[8,1024]{1,0:T(8,128)}, f32[8,1024]{1,0:T(8,128)S(1)}, u32[]{:S(2)}, u32[]{:S(2)}) collective-permute-start(f32[8,1024]{1,0:T(8,128)} %get-tuple-element.104), channel_id=1, source_target_pairs={{0,8},{8,0},{16,24},{24,16},{1,9},{9,1},{17,25},{25,17},{2,10},{10... | collective-permute-start | bytes 98312 | tf_op jit(solution)/shard_map/ppermute | solution.py:719
  7.0 4.5 %collective-permute-start.3 = (bf16[8,3712]{1,0:T(8,128)(2,1)}, bf16[8,3712]{1,0:T(8,128)(2,1)S(1)}, u32[]{:S(2)}, u32[]{:S(2)}) collective-permute-start(bf16[8,3712]{1,0:T(8,128)(2,1)} %get-tuple-element.107), channel_id=1, source_target_pairs={{0,1},{1,2},{2,3},{3,4},{4,5},{5,6},{6,7},{8,9},{9,10},{10,11},{11... | collective-permute-start | bytes 178184 | tf_op jit(solution)/shard_map/ppermute | solution.py:719
  12.4 2.9 %collective-permute-start.4 = (bf16[464,128]{1,0:T(8,128)(2,1)S(1)}, bf16[464,128]{1,0:T(8,128)(2,1)S(1)}, u32[]{:S(2)}, u32[]{:S(2)}) collective-permute-start(bf16[464,128]{1,0:T(8,128)(2,1)S(1)} %get-tuple-element.116), channel_id=1, source_target_pairs={{0,1},{1,0},{2,3},{3,2},{4,5},{5,4},{6,7},{7,6},{8,9},{9,8},{10,11... | collective-permute-start | bytes 356360 | tf_op jit(solution)/shard_map/ppermute | solution.py:719
  14.5 5.9 %collective-permute-start.5 = (bf16[464,128]{1,0:T(8,128)(2,1)S(1)}, bf16[464,128]{1,0:T(8,128)(2,1)S(1)}, u32[]{:S(2)}, u32[]{:S(2)}) collective-permute-start(bf16[464,128]{1,0:T(8,128)(2,1)S(1)} %get-tuple-element.121), channel_id=1, source_target_pairs={{0,1},{1,0},{2,3},{3,2},{4,5},{5,4},{6,7},{7,6},{8,9},{9,8},{10,11... | collective-permute-start | bytes 356360 | tf_op jit(solution)/shard_map/ppermute | solution.py:719
  15.4 9.4 %collective-permute-start.6 = (bf16[464,128]{1,0:T(8,128)(2,1)S(1)}, bf16[464,128]{1,0:T(8,128)(2,1)S(1)}, u32[]{:S(2)}, u32[]{:S(2)}) collective-permute-start(bf16[464,128]{1,0:T(8,128)(2,1)S(1)} %get-tuple-element.117.own), channel_id=1, source_target_pairs={{0,2},{1,3},{8,10},{9,11},{16,18},{17,19},{24,26},{25,27}} | collective-permute-start | bytes 356360 | tf_op jit(solution)/shard_map/ppermute | solution.py:719
  20.5 5.1 %collective-permute-start.7 = (bf16[464,128]{1,0:T(8,128)(2,1)S(1)}, bf16[464,128]{1,0:T(8,128)(2,1)S(1)}, u32[]{:S(2)}, u32[]{:S(2)}) collective-permute-start(bf16[464,128]{1,0:T(8,128)(2,1)S(1)} %get-tuple-element.122.own), channel_id=1, source_target_pairs={{0,2},{1,3},{8,10},{9,11},{16,18},{17,19},{24,26},{25,27}} | collective-permute-start | bytes 356360 | tf_op jit(solution)/shard_map/ppermute | solution.py:719
  24.9 3.1 %collective-permute-start.8 = (bf16[448,128]{1,0:T(8,128)(2,1)S(1)}, bf16[448,128]{1,0:T(8,128)(2,1)S(1)}, u32[]{:S(2)}, u32[]{:S(2)}) collective-permute-start(bf16[448,128]{1,0:T(8,128)(2,1)S(1)} %pass.8), channel_id=1, source_target_pairs={{2,4},{3,5},{10,12},{11,13},{18,20},{19,21},{26,28},{27,29}} | collective-permute-start | bytes 344072 | tf_op jit(solution)/shard_map/ppermute | solution.py:719
  25.7 3.1 %collective-permute-start.10 = (bf16[448,128]{1,0:T(8,128)(2,1)S(1)}, bf16[448,128]{1,0:T(8,128)(2,1)S(1)}, u32[]{:S(2)}, u32[]{:S(2)}) collective-permute-start(bf16[448,128]{1,0:T(8,128)(2,1)S(1)} %pass.9), channel_id=1, source_target_pairs={{2,4},{3,5},{10,12},{11,13},{18,20},{19,21},{26,28},{27,29}} | collective-permute-start | bytes 344072 | tf_op jit(solution)/shard_map/ppermute | solution.py:719
  35.2 5.3 %collective-permute-start.17 = (bf16[464,128]{1,0:T(8,128)(2,1)S(1)}, bf16[464,128]{1,0:T(8,128)(2,1)S(1)}, u32[]{:S(2)}, u32[]{:S(2)}) collective-permute-start(bf16[464,128]{1,0:T(8,128)(2,1)S(1)} %get-tuple-element.152.own), channel_id=1, source_target_pairs={{6,4},{7,5},{14,12},{15,13},{22,20},{23,21},{30,28},{31,29}} | collective-permute-start | bytes 356360 | tf_op jit(solution)/shard_map/ppermute | solution.py:719
  35.9 5.4 %collective-permute-start.16 = (bf16[464,128]{1,0:T(8,128)(2,1)S(1)}, bf16[464,128]{1,0:T(8,128)(2,1)S(1)}, u32[]{:S(2)}, u32[]{:S(2)}) collective-permute-start(bf16[464,128]{1,0:T(8,128)(2,1)S(1)} %get-tuple-element.150.own), channel_id=1, source_target_pairs={{6,4},{7,5},{14,12},{15,13},{22,20},{23,21},{30,28},{31,29}} | collective-permute-start | bytes 356360 | tf_op jit(solution)/shard_map/ppermute | solution.py:719
  40.6 6.9 %collective-permute-start.20 = (bf16[448,128]{1,0:T(8,128)(2,1)S(1)}, bf16[448,128]{1,0:T(8,128)(2,1)S(1)}, u32[]{:S(2)}, u32[]{:S(2)}) collective-permute-start(bf16[448,128]{1,0:T(8,128)(2,1)S(1)} %pass.13), channel_id=1, source_target_pairs={{4,2},{5,3},{12,10},{13,11},{20,18},{21,19},{28,26},{29,27}} | collective-permute-start | bytes 344072 | tf_op jit(solution)/shard_map/ppermute | solution.py:719
  41.3 7.5 %collective-permute-start.18 = (bf16[448,128]{1,0:T(8,128)(2,1)S(1)}, bf16[448,128]{1,0:T(8,128)(2,1)S(1)}, u32[]{:S(2)}, u32[]{:S(2)}) collective-permute-start(bf16[448,128]{1,0:T(8,128)(2,1)S(1)} %pass.12), channel_id=1, source_target_pairs={{4,2},{5,3},{12,10},{13,11},{20,18},{21,19},{28,26},{29,27}} | collective-permute-start | bytes 344072 | tf_op jit(solution)/shard_map/ppermute | solution.py:719
  47.5 12.3 %collective-permute-start.21 = (bf16[448,128]{1,0:T(8,128)(2,1)S(1)}, bf16[448,128]{1,0:T(8,128)(2,1)S(1)}, u32[]{:S(2)}, u32[]{:S(2)}) collective-permute-start(bf16[448,128]{1,0:T(8,128)(2,1)S(1)} %pass.15), channel_id=1, source_target_pairs={{2,0},{3,1},{10,8},{11,9},{18,16},{19,17},{26,24},{27,25}} | collective-permute-start | bytes 344072 | tf_op jit(solution)/shard_map/ppermute | solution.py:719
  48.9 13.0 %collective-permute-start.19 = (bf16[448,128]{1,0:T(8,128)(2,1)S(1)}, bf16[448,128]{1,0:T(8,128)(2,1)S(1)}, u32[]{:S(2)}, u32[]{:S(2)}) collective-permute-start(bf16[448,128]{1,0:T(8,128)(2,1)S(1)} %pass.14), channel_id=1, source_target_pairs={{2,0},{3,1},{10,8},{11,9},{18,16},{19,17},{26,24},{27,25}} | collective-permute-start | bytes 344072 | tf_op jit(solution)/shard_map/ppermute | solution.py:719
  60.0 4.1 %collective-permute-start.23 = (bf16[448,128]{1,0:T(8,128)(2,1)S(1)}, bf16[448,128]{1,0:T(8,128)(2,1)S(1)}, u32[]{:S(2)}, u32[]{:S(2)}) collective-permute-start(bf16[448,128]{1,0:T(8,128)(2,1)S(1)} %get-tuple-element.178), channel_id=1, source_target_pairs={{0,1},{1,0},{2,3},{3,2},{4,5},{5,4},{6,7},{7,6},{8,9},{9,8},{10,11... | collective-permute-start | bytes 344072 | tf_op jit(solution)/shard_map/ppermute | solution.py:719
  62.1 2.1 %collective-permute-start.22 = (bf16[448,128]{1,0:T(8,128)(2,1)S(1)}, bf16[448,128]{1,0:T(8,128)(2,1)S(1)}, u32[]{:S(2)}, u32[]{:S(2)}) collective-permute-start(bf16[448,128]{1,0:T(8,128)(2,1)S(1)} %get-tuple-element.177), channel_id=1, source_target_pairs={{0,1},{1,0},{2,3},{3,2},{4,5},{5,4},{6,7},{7,6},{8,9},{9,8},{10,11... | collective-permute-start | bytes 344072 | tf_op jit(solution)/shard_map/ppermute | solution.py:719
  67.0 4.9 %collective-permute-start.24 = (f32[8,1024]{1,0:T(8,128)S(1)}, f32[8,1024]{1,0:T(8,128)S(1)}, u32[]{:S(2)}, u32[]{:S(2)}) collective-permute-start(f32[8,1024]{1,0:T(8,128)S(1)} %get-tuple-element.181), channel_id=1, source_target_pairs={{0,8},{8,16},{16,24},{24,0},{1,9},{9,17},{17,25},{25,1},{2,10},{10... | collective-permute-start | bytes 98312 | tf_op jit(solution)/shard_map/ppermute | solution.py:719
  68.5 3.9 %collective-permute-start.25 = (f32[8,1024]{1,0:T(8,128)S(1)}, f32[8,1024]{1,0:T(8,128)S(1)}, u32[]{:S(2)}, u32[]{:S(2)}) collective-permute-start(f32[8,1024]{1,0:T(8,128)S(1)} %get-tuple-element.182), channel_id=1, source_target_pairs={{0,16},{8,24},{16,0},{24,8},{1,17},{9,25},{17,1},{25,9},{2,18},{10... | collective-permute-start | bytes 98312 | tf_op jit(solution)/shard_map/ppermute | solution.py:719
  70.0 3.9 %collective-permute-start.26 = (f32[8,1024]{1,0:T(8,128)S(1)}, f32[8,1024]{1,0:T(8,128)S(1)}, u32[]{:S(2)}, u32[]{:S(2)}) collective-permute-start(f32[8,1024]{1,0:T(8,128)S(1)} %get-tuple-element.183), channel_id=1, source_target_pairs={{0,24},{8,0},{16,8},{24,16},{1,25},{9,1},{17,9},{25,17},{2,26},{10... | collective-permute-start | bytes 98312 | tf_op jit(solution)/shard_map/ppermute | solution.py:719
  75.3 6.8 %collective-permute-start.28 = (f32[24,1024]{1,0:T(8,128)S(1)}, f32[24,1024]{1,0:T(8,128)S(1)}, u32[]{:S(2)}, u32[]{:S(2)}) collective-permute-start(f32[24,1024]{1,0:T(8,128)S(1)} %get-tuple-element.188), channel_id=1, source_target_pairs={{0,6},{1,7},{2,0},{3,1},{4,2},{5,3},{6,4},{7,5},{8,14},{9,15},{10,... | collective-permute-start | bytes 294920 | tf_op jit(solution)/shard_map/ppermute | solution.py:719
  75.4 4.9 %collective-permute-start.30 = (f32[8,1024]{1,0:T(8,128)S(1)}, f32[8,1024]{1,0:T(8,128)S(1)}, u32[]{:S(2)}, u32[]{:S(2)}) collective-permute-start(f32[8,1024]{1,0:T(8,128)S(1)} %get-tuple-element.184.refs_0_), channel_id=1, source_target_pairs={{0,4},{1,5},{2,6},{3,7},{4,0},{5,1},{6,2},{7,3},{8,12},{9,13},{10,... | collective-permute-start | bytes 98312 | tf_op jit(solution)/shard_map/ppermute | solution.py:719
  76.4 5.7 %collective-permute-start.29 = (f32[8,1024]{1,0:T(8,128)S(1)}, f32[8,1024]{1,0:T(8,128)S(1)}, u32[]{:S(2)}, u32[]{:S(2)}) collective-permute-start(f32[8,1024]{1,0:T(8,128)S(1)} %get-tuple-element.184.refs_0_), channel_id=1, source_target_pairs={{0,2},{1,3},{2,4},{3,5},{4,6},{5,7},{6,0},{7,1},{8,10},{9,11},{10,... | collective-permute-start | bytes 98312 | tf_op jit(solution)/shard_map/ppermute | solution.py:719
  (10 other events, 27.6 us)

commit v4 on v3

--- a/solution.py
+++ b/solution.py
@@ -265,9 +265,14 @@
     return scaled, (scaled * scores).astype(BF16)
 
 
-def factor_kernel(cols, gate, grad, gain, silus, grown, decays):
+def factor_kernel(cols, gate, grad, gain, rows, silus, grown, decays, picks, shifted):
     length, features = gate.shape
+    taps = shifted.shape[0] + 1
+    for tap in range(taps - 1):
+        start = HALO - taps + 1 + tap
+        shifted[tap] = rows[start : start + length, :]
     decay = jnp.exp(cols[1])
+    picks[...] = (iota(picks.shape, 1) == iota(picks.shape, 0) // P_SIZE).astype(BF16)
     for pair in range(features // LANES):
         here = block(pair)
         z = gate[:, here].astype(F32)
@@ -446,72 +451,68 @@
     return total
 
 
-def through_conv(taps, here, grad_out, rows, slope, slopes, whole):
+def through_conv(taps, here, grad_out, rows, shifted, slope, slopes, whole):
     length = grad_out.shape[0]
     grad_pre = grad_out.astype(BF16).astype(F32) * slope[:, here]
     slopes[HALO : HALO + length, here] = grad_pre
-    start = HALO - (taps - 1)
     for tap in range(taps):
-        whole[tap : tap + 1, here] = jnp.sum(
-            grad_pre * rows[start + tap : start + tap + length, here], axis=0, keepdims=True
-        )
+        given = shifted[tap, :, here] if tap < taps - 1 else rows[HALO : HALO + length, here]
+        whole[tap : tap + 1, here] = jnp.sum(grad_pre * given, axis=0, keepdims=True)
     whole[taps : taps + 1, here] = jnp.sum(grad_pre, axis=0, keepdims=True)
 
 
-def close_group(taps, number, rows, conv, slope, cols, entry, leave, grad_values, slopes, whole):
+def close_side(taps, own, rows, shifted, conv, slope, cols, picks, entries, leaves, grad_values, slopes, whole, scratch):
+    products, holds, leavings, overlaps = scratch
     length, features = grad_values.shape
-    group = leave.shape[0] // N
+    half = features // LANES // 2
+    group = half // STREAMS
     shape = (length, LANES)
+    side = here_at()[0] if own else 1 - here_at()[0]
     write = conv[:, features : features + N]
     running = cols[1]
     tail = jnp.exp(running[length - 1 : length, :] - running) * cols[0]
-    tail = pltpu.roll(tail, lax.rem(LANES - 2 * group * number, LANES), 1)
-    state_sums = jnp.zeros(shape, F32)
-    end_sums = jnp.zeros((8, LANES), F32)
-    write_grad = jnp.zeros((length, N), F32)
-    for pair in range(group):
-        here = side_block(number * group + pair)
-        leaving = get_state(leave, pair)
+    tail = pltpu.roll(tail, lax.rem(LANES - 2 * half * side, LANES), 1)
+    for pair in range(half):
+        here = side_block(side * half + pair)
+        local = block(pair)
+        leaving = get_state(leaves[pair // group], pair % group)
         values = conv[:, here].astype(F32)
         tail_wide = by_head(tail, pair, shape)
         state_grad = tail_wide * dot(write, leaving)
-        state_sums += head_sums(values * state_grad, pair)
-        write_grad += dot((tail_wide * values).astype(BF16), leaving, (1, 1))
-        entering = get_state(entry, pair).astype(F32)
+        products[:, local] = (values * state_grad).astype(BF16)
+        holds[:, local] = (tail_wide * values).astype(BF16)
+        leavings[:, local] = leaving
+        entering = get_state(entries[pair // group], pair % group).astype(F32)
         overlap = jnp.sum(leaving.astype(F32) * entering, axis=0, keepdims=True)
-        end_sums += head_sums(jnp.broadcast_to(overlap, (8, LANES)), pair)
-        through_conv(taps, here, grad_values[:, here] + state_grad, rows, slope, slopes, whole)
-    back = 2 * group * number
+        overlaps[:, local] = jnp.broadcast_to(overlap, (8, LANES))
+        through_conv(taps, here, grad_values[:, here] + state_grad, rows, shifted, slope, slopes, whole)
+    back = 2 * half * side
+    choose = picks[...]
+    state_sums = dot(products[...], choose)
+    high, low = split(overlaps[...])
+    end_sums = dot(high, choose) + dot(low, choose)
+    write_grad = dot(holds[...], leavings[...], (1, 1))
     write_grad = jnp.concatenate([write_grad, jnp.zeros_like(write_grad)], axis=1)
     return pltpu.roll(state_sums, back, 1), pltpu.roll(end_sums, back, 1), write_grad
 
 
-def close_side(taps, own, rows, conv, slope, cols, entries, leaves, grad_values, slopes, whole):
-    totals = None
-    for stream, (entry, leave) in enumerate(zip(entries, leaves)):
-        sums = close_group(
-            taps, group_at(own, stream), rows, conv, slope, cols, entry, leave, grad_values, slopes, whole
-        )
-        totals = sums if totals is None else [a + b for a, b in zip(totals, sums)]
-    return totals
-
-
-def close_own_kernel(taps, rows, conv, slope, cols, grad_values, *refs):
-    given, (slopes, whole, state_out, end_out, write_out) = refs[: 2 * STREAMS], refs[2 * STREAMS :]
+def close_own_kernel(taps, rows, shifted, conv, slope, cols, picks, grad_values, *refs):
+    given, (slopes, whole, state_out, end_out, write_out, *scratch) = refs[: 2 * STREAMS], refs[2 * STREAMS :]
     length, channels = conv.shape
     slopes[0:HALO, :] = jnp.zeros((HALO, channels), F32)
     slopes[HALO + length :, :] = jnp.zeros((HALO, channels), F32)
     whole[...] = jnp.zeros_like(whole)
     state_out[...], end_out[...], write_out[...] = close_side(
-        taps, True, rows, conv, slope, cols, given[:STREAMS], given[STREAMS:], grad_values, slopes, whole
+        taps, True, rows, shifted, conv, slope, cols, picks, given[:STREAMS], given[STREAMS:], grad_values, slopes, whole, scratch
     )
 
 
 def close_kernel(
-    taps, sizes, slopes_in, whole_in, rows, conv, slope, cols, small, grad_values, grad_vecs, out_sums, in_sums,
+    taps, sizes, slopes_in, whole_in, rows, shifted, conv, slope, cols, picks, small, grad_values, grad_vecs, out_sums, in_sums,
     grad_gain, grad_small, state_in, end_in, write_in, *rest
 ):
-    given, (slopes, whole, grad_dt, *outs, cut) = rest[: 2 * STREAMS], rest[2 * STREAMS :]
+    given, rest, scratch = rest[: 2 * STREAMS], rest[2 * STREAMS : -4], rest[-4:]
+    slopes, whole, grad_dt, *outs, cut = rest
     parts = len(outs)
     position_here = here_at()[2]
     length, channels = conv.shape
@@ -520,19 +521,19 @@
     step = cols[0]
     last = cols[1, length - 1 : length, :]
     state_sums, end_sums, write_grad = close_side(
-        taps, False, rows, conv, slope, cols, given[:STREAMS], given[STREAMS:], grad_values, slopes, whole
+        taps, False, rows, shifted, conv, slope, cols, picks, given[:STREAMS], given[STREAMS:], grad_values, slopes, whole, scratch
     )
     state_sums = state_sums + state_in[...]
     end_sums = end_sums + end_in[...]
     vecs = grad_vecs[...] + (write_in[...] + write_grad)
-    through_conv(taps, block(channels // LANES - 1), vecs, rows, slope, slopes, whole)
+    through_conv(taps, block(channels // LANES - 1), vecs, rows, shifted, slope, slopes, whole)
 
     into = in_sums[...] + state_sums
     change = out_sums[...] - into
     end_grad = jnp.sum(state_sums, axis=0, keepdims=True) + jnp.exp(last) * end_sums[0:1, :]
     square = (length, length)
     upper = iota(square, 0) <= iota(square, 1)
-    log_grad = dot_parts(upper, change, 3) + end_grad
+    log_grad = dot_parts(upper, change, 2) + end_grad
     rate = jnp.exp(small[1:2, :])
     raw_grad = (into / step - rate * log_grad) * (1.0 - jnp.exp(-step))
     grad_dt[...] = raw_grad.T[0:heads, :]
@@ -882,10 +883,10 @@
         return [after(part, work["local"]) for part in value]
 
     def factors(signal, value):
-        work["factors"] = call(
+        *work["factors"], work["picks"], work["shifted"] = call(
             factor_kernel,
-            [wide] * 3,
-            [after(cols, *signal), gate, grad, gain],
+            [wide] * 3 + [like((half * LANES, LANES), BF16), like((taps - 1, length, channels))],
+            [after(cols, *signal), gate, grad, gain, padded],
             flops=length * features * 16,
             name="factors",
         )
@@ -949,7 +950,9 @@
         return [after(part, work["back"][0]) for part in value]
 
     shapes = [like((2 * HALO + length, channels)), like((SMALL, full_width)), square, like((8, LANES)), square]
-    fixed = [padded, conv, work["slope"], cols]
+    fixed = [padded, work["shifted"], conv, work["slope"], cols, work["picks"]]
+    side = half * LANES
+    scratch = [pltpu.VMEM((length, side), BF16)] * 2 + [pltpu.VMEM((N, side), BF16), pltpu.VMEM((8, side), F32)]
 
     leave_own, leave_got = entering_states(functools.partial(norm_next, True), got, True, (gates, back))
     grad_gate, _, out_sums, grad_gain, grad_small, _ = work["gates"]
@@ -958,6 +961,7 @@
         functools.partial(close_own_kernel, taps),
         shapes,
         fixed + [grad_values] + entry_own + leave_own,
+        scratch,
         name="close_own",
     )
     slopes, whole, grad_dt, *shares = call(
@@ -965,7 +969,7 @@
         shapes[:2] + [like((heads, length))] + [piece_like] * parts,
         [slopes, whole] + fixed + [small, grad_values, grad_vecs, out_sums, in_sums, grad_gain, grad_small]
         + sums + entry_got + leave_got,
-        [pltpu.VMEM((parts, SMALL, piece_width), F32)],
+        [pltpu.VMEM((parts, SMALL, piece_width), F32)] + scratch,
         name="close",
         aliases={0: 0, 1: 1},
     )

time: 84 us -> 82.9 us (0.987)
  transfers between devices with their start and end apart: 31 -> 31, of which waited for: 12 -> 12; matrix products, arithmetic and copies ran while one was open for 2% -> 2% of each run, Pallas kernels for 29% -> 30%
where the time goes in v4:
time: 82.9 us; the launch traced here: 82.5 us
  Pallas kernels  32.3 us (39%)
  starting transfers between devices  29.2 us (35%)
  waiting for transfers between devices  18.4 us (22%)
  other arithmetic  1.32 us (2%)
  between operations  1.27 us (2%)
    pallas_call x38, Pallas kernels, call(): pl.pallas_call(kernel, out_shape=outs, in_specs=specs, out_specs=[pl.Bloc...  32.3 us
    ppermute x31, starting transfers between devices, shift(): lax.ppermute(value, axis, [(i, j) for i, j in pairs if 0 <= j < count])  29.2 us
    ppermute x31, waiting for transfers between devices, shift(): lax.ppermute(value, axis, [(i, j) for i, j in pairs if 0 <= j < count])  18.4 us
  transfers between devices with their start and end apart: 31, of which 12 were waited for; matrix products, arithmetic and copies ran while one was open for 2% of the time, Pallas kernels for 30%

profile of v4, /device:TPU:0, one launch (start us, length us, event | category | flops | bytes accessed | tf_op | source)
XLA Modules:
  0.0 82.5 jit_solution(13079804780842609376)
XLA Ops:
  0.6 1.8 %open.1 = (bf16[8,3712]{1,0:T(8,128)(2,1)}, f32[8,1024]{1,0:T(8,128)}, f32[16,1024]{1,0:T(8,128)}) custom-call(bf16[128,3712]{1,0:T(8,128)(2,1)} %bitcast.22, f32[56,128]{1,0:T(8,128)} %bitcast.25, f32[4,928]{1,0:T(4,128)} %cw.1, f32[1,928]{1,0:T(1,128)} %bitcast.26, f32[1,14]{1,0:T(1,128)} %bitcast.27, f32[1,14]{1,0:T(1,128)} %bitcast.28, ...), custom_call_target="tpu_custom_call" | custom-call | bytes 1158952 | tf_op jit(solution)/shard_map/open/pallas_call | solution.py:697
  2.4 4.0 %collective-permute-start.2 = (f32[8,1024]{1,0:T(8,128)}, f32[8,1024]{1,0:T(8,128)S(1)}, u32[]{:S(2)}, u32[]{:S(2)}) collective-permute-start(f32[8,1024]{1,0:T(8,128)} %get-tuple-element.106), channel_id=1, source_target_pairs={{0,24},{8,16},{16,8},{24,0},{1,25},{9,17},{17,9},{25,1},{2,26},{10... | collective-permute-start | bytes 98312 | tf_op jit(solution)/shard_map/ppermute | solution.py:720
  8.3 1.3 %pad_convert_fusion.lifted = f32[136,3712]{1,0:T(8,128)S(1)} fusion(bf16[128,3712]{1,0:T(8,128)(2,1)} %bitcast.23), kind=kLoop, calls=%fused_computation | loop fusion | flops 504832 | bytes 2969600 | tf_op jit(solution)/shard_map/jit(_pad)/pad | solution.py:822
  12.4 1.4 %collective-permute-start.4 = (bf16[464,128]{1,0:T(8,128)(2,1)S(1)}, bf16[464,128]{1,0:T(8,128)(2,1)S(1)}, u32[]{:S(2)}, u32[]{:S(2)}) collective-permute-start(bf16[464,128]{1,0:T(8,128)(2,1)S(1)} %get-tuple-element.118), channel_id=1, source_target_pairs={{0,1},{1,0},{2,3},{3,2},{4,5},{5,4},{6,7},{7,6},{8,9},{9,8},{10,11... | collective-permute-start | bytes 356360 | tf_op jit(solution)/shard_map/ppermute | solution.py:720
  15.4 4.2 %collective-permute-start.5 = (bf16[464,128]{1,0:T(8,128)(2,1)S(1)}, bf16[464,128]{1,0:T(8,128)(2,1)S(1)}, u32[]{:S(2)}, u32[]{:S(2)}) collective-permute-start(bf16[464,128]{1,0:T(8,128)(2,1)S(1)} %get-tuple-element.119.own), channel_id=1, source_target_pairs={{0,2},{1,3},{8,10},{9,11},{16,18},{17,19},{24,26},{25,27}} | collective-permute-start | bytes 356360 | tf_op jit(solution)/shard_map/ppermute | solution.py:720
  20.5 1.3 %collective-permute-start.7 = (bf16[464,128]{1,0:T(8,128)(2,1)S(1)}, bf16[464,128]{1,0:T(8,128)(2,1)S(1)}, u32[]{:S(2)}, u32[]{:S(2)}) collective-permute-start(bf16[464,128]{1,0:T(8,128)(2,1)S(1)} %get-tuple-element.125.own), channel_id=1, source_target_pairs={{0,2},{1,3},{8,10},{9,11},{16,18},{17,19},{24,26},{25,27}} | collective-permute-start | bytes 356360 | tf_op jit(solution)/shard_map/ppermute | solution.py:720
  21.8 3.1 %intra.1 = (f32[128,3584]{1,0:T(8,128)S(1)}, f32[128,3712]{1,0:T(8,128)S(1)}) custom-call(f32[136,3712]{1,0:T(8,128)S(1)} %get-tuple-element.112.rows, f32[8,3840]{1,0:T(8,128)S(1)} %get-tuple-element.107.full, bf16[128,3712]{1,0:T(8,128)(2,1)S(1)} %get-tuple-element.157.conv, f32[2,128,128]{2,1,0:T(8,128)S(1)} %get-tuple-element.133.cols, ...), custom_call_target="tpu_custom_call" | custom-call | flops 117440512 | bytes 7159808 | tf_op jit(solution)/shard_map/intra/pallas_call | solution.py:697
  26.4 2.4 %factors.1 = (f32[128,3584]{1,0:T(8,128)S(1)}, f32[128,3584]{1,0:T(8,128)S(1)}, f32[128,3584]{1,0:T(8,128)S(1)}, bf16[1792,128]{1,0:T(8,128)(2,1)S(1)}, f32[3,128,3712]{2,1,0:T(8,128)S(1)}) custom-call(f32[2,128,128]{2,1,0:T(8,128)S(1)} %get-tuple-element.133.cols, bf16[128,3584]{1,0:T(8,128)(2,1)S(1)} %bitcast.18, bf16[128,3584]{1,0:T(8,128)(2,1)S(1)} %bitcast.20, ...), custom_call_target="tpu_custom_call" | custom-call | flops 7340032 | bytes 15665152 | tf_op jit(solution)/shard_map/factors/pallas_call | solution.py:697
  37.3 4.0 %gates.1 = (bf16[128,3584]{1,0:T(8,128)(2,1)}, f32[128,3584]{1,0:T(8,128)S(1)}, f32[128,128]{1,0:T(8,128)S(1)}, f32[1,3584]{1,0:T(1,128)S(1)}, f32[8,128]{1,0:T(8,128)S(1)}, /*index=5*/f32[128,128]{1,0:T(8,128)S(1)}) custom-call(f32[128,3584]{1,0:T(8,128)S(1)} %get-tuple-element.150.mixed, bf16[128,3712]{1,0:T(8,128)(2,1)S(1)} %get-tuple-element.157.conv, ...), custom_call_target="tpu_custom_call" | custom-call | flops 117440512 | bytes 8196096 | tf_op jit(solution)/shard_map/gates/pallas_call | solution.py:697
  42.8 5.4 %back.1 = (f32[128,3584]{1,0:T(8,128)S(1)}, f32[128,128]{1,0:T(8,128)S(1)}, f32[128,128]{1,0:T(8,128)S(1)}) custom-call(f32[128,3584]{1,0:T(8,128)S(1)} %get-tuple-element.164.grad_mixed, bf16[128,3712]{1,0:T(8,128)(2,1)S(1)} %get-tuple-element.157.conv, f32[2,128,128]{2,1,0:T(8,128)S(1)} %get-tuple-element.133.cols, ...), custom_call_target="tpu_custom_call" | custom-call | flops 234881024 | bytes 5148672 | tf_op jit(solution)/shard_map/back/pallas_call | solution.py:697
  48.3 1.3 %collective-permute-start.21 = (bf16[448,128]{1,0:T(8,128)(2,1)S(1)}, bf16[448,128]{1,0:T(8,128)(2,1)S(1)}, u32[]{:S(2)}, u32[]{:S(2)}) collective-permute-start(bf16[448,128]{1,0:T(8,128)(2,1)S(1)} %pass.15), channel_id=1, source_target_pairs={{2,0},{3,1},{10,8},{11,9},{18,16},{19,17},{26,24},{27,25}} | collective-permute-start | bytes 344072 | tf_op jit(solution)/shard_map/ppermute | solution.py:720
  49.7 1.5 %collective-permute-start.19 = (bf16[448,128]{1,0:T(8,128)(2,1)S(1)}, bf16[448,128]{1,0:T(8,128)(2,1)S(1)}, u32[]{:S(2)}, u32[]{:S(2)}) collective-permute-start(bf16[448,128]{1,0:T(8,128)(2,1)S(1)} %pass.14), channel_id=1, source_target_pairs={{2,0},{3,1},{10,8},{11,9},{18,16},{19,17},{26,24},{27,25}} | collective-permute-start | bytes 344072 | tf_op jit(solution)/shard_map/ppermute | solution.py:720
  51.2 8.7 %collective-permute-done.21.refs_2_ = bf16[448,128]{1,0:T(8,128)(2,1)S(1)} collective-permute-done((bf16[448,128]{1,0:T(8,128)(2,1)S(1)}, bf16[448,128]{1,0:T(8,128)(2,1)S(1)}, u32[]{:S(2)}, u32[]{:S(2)}) %collective-permute-start.21) | collective-permute-done | bytes 114720 | tf_op jit(solution)/shard_map/ppermute | solution.py:720
  60.1 1.8 %collective-permute-done.19.refs_2_ = bf16[448,128]{1,0:T(8,128)(2,1)S(1)} collective-permute-done((bf16[448,128]{1,0:T(8,128)(2,1)S(1)}, bf16[448,128]{1,0:T(8,128)(2,1)S(1)}, u32[]{:S(2)}, u32[]{:S(2)}) %collective-permute-start.19) | collective-permute-done | bytes 114720 | tf_op jit(solution)/shard_map/ppermute | solution.py:720
  62.2 1.5 %close_own.1 = (f32[144,3712]{1,0:T(8,128)S(1)}, f32[8,3840]{1,0:T(8,128)S(1)}, f32[128,128]{1,0:T(8,128)S(1)}, f32[8,128]{1,0:T(8,128)S(1)}, f32[128,128]{1,0:T(8,128)S(1)}) custom-call(f32[136,3712]{1,0:T(8,128)S(1)} %get-tuple-element.112.rows, f32[3,128,3712]{2,1,0:T(8,128)S(1)} %get-tuple-element.135.shifted, ...), custom_call_target="tpu_custom_call" | custom-call | bytes 15851520 | tf_op jit(solution)/shard_map/close_own/pallas_call | solution.py:697
  63.7 2.2 %close.1 = (f32[144,3712]{1,0:T(8,128)S(1)}, f32[8,3840]{1,0:T(8,128)S(1)}, f32[56,128]{1,0:T(8,128)}, f32[8,1024]{1,0:T(8,128)S(1)}, f32[8,1024]{1,0:T(8,128)S(...) custom-call(f32[144,3712]{1,0:T(8,128)S(1)} %get-tuple-element.171.slopes_in, ...), custom_call_target="tpu_custom_call", output_to_operand_aliasing={{0}: (0, {}), {1}: (1, {})} | custom-call | bytes 18491392 | tf_op jit(solution)/shard_map/close/pallas_call | solution.py:697
  65.9 1.5 %collective-permute-start.24 = (f32[8,1024]{1,0:T(8,128)S(1)}, f32[8,1024]{1,0:T(8,128)S(1)}, u32[]{:S(2)}, u32[]{:S(2)}) collective-permute-start(f32[8,1024]{1,0:T(8,128)S(1)} %get-tuple-element.185), channel_id=1, source_target_pairs={{0,8},{8,16},{16,24},{24,0},{1,9},{9,17},{17,25},{25,1},{2,10},{10... | collective-permute-start | bytes 98312 | tf_op jit(solution)/shard_map/ppermute | solution.py:720
  67.4 1.5 %collective-permute-start.25 = (f32[8,1024]{1,0:T(8,128)S(1)}, f32[8,1024]{1,0:T(8,128)S(1)}, u32[]{:S(2)}, u32[]{:S(2)}) collective-permute-start(f32[8,1024]{1,0:T(8,128)S(1)} %get-tuple-element.186), channel_id=1, source_target_pairs={{0,16},{8,24},{16,0},{24,8},{1,17},{9,25},{17,1},{25,9},{2,18},{10... | collective-permute-start | bytes 98312 | tf_op jit(solution)/shard_map/ppermute | solution.py:720
  68.9 1.4 %collective-permute-start.26 = (f32[8,1024]{1,0:T(8,128)S(1)}, f32[8,1024]{1,0:T(8,128)S(1)}, u32[]{:S(2)}, u32[]{:S(2)}) collective-permute-start(f32[8,1024]{1,0:T(8,128)S(1)} %get-tuple-element.187), channel_id=1, source_target_pairs={{0,24},{8,0},{16,8},{24,16},{1,25},{9,1},{17,9},{25,17},{2,26},{10... | collective-permute-start | bytes 98312 | tf_op jit(solution)/shard_map/ppermute | solution.py:720
  71.3 1.5 %collective-permute-done.26.refs_3_ = f32[8,1024]{1,0:T(8,128)S(1)} collective-permute-done((f32[8,1024]{1,0:T(8,128)S(1)}, f32[8,1024]{1,0:T(8,128)S(1)}, u32[]{:S(2)}, u32[]{:S(2)}) %collective-permute-start.26) | collective-permute-done | bytes 32800 | tf_op jit(solution)/shard_map/ppermute | solution.py:720
  72.9 1.3 %collective-permute-done.27.other.from_core = f32[24,1024]{1,0:T(8,128)S(1)} collective-permute-done((f32[24,1024]{1,0:T(8,128)S(1)}, f32[24,1024]{1,0:T(8,128)S(1)}, u32[]{:S(2)}, u32[]{:S(2)}) %collective-permute-start.27) | collective-permute-done | bytes 98336 | tf_op jit(solution)/shard_map/ppermute | solution.py:720
  76.3 2.3 %inputs.1 = (bf16[128,3712]{1,0:T(8,128)(2,1)}, f32[16,3712]{1,0:T(8,128)S(1)}) custom-call(f32[8,3840]{1,0:T(8,128)S(1)} %get-tuple-element.107.full, f32[144,3712]{1,0:T(8,128)S(1)} %get-tuple-element.189.slopes), custom_call_target="tpu_custom_call" | custom-call | flops 7602176 | bytes 3448832 | tf_op jit(solution)/shard_map/inputs/pallas_call | solution.py:697
  79.2 1.8 %collective-permute-done.29.refs_1_ = f32[8,1024]{1,0:T(8,128)S(1)} collective-permute-done((f32[8,1024]{1,0:T(8,128)S(1)}, f32[8,1024]{1,0:T(8,128)S(1)}, u32[]{:S(2)}, u32[]{:S(2)}) %collective-permute-start.29) | collective-permute-done | bytes 32800 | tf_op jit(solution)/shard_map/ppermute | solution.py:720
  81.0 1.3 %unpack.1 = (bf16[128,3712]{1,0:T(8,128)(2,1)}, f32[4,928]{1,0:T(4,128)}, f32[928]{0:T(1024)}, f32[1,14]{1,0:T(1,128)}, f32[1,14]{1,0:T(1,128)}, /*index=5*/f32[1,14]{1,0:T(1,128)}, f32[896]{0:T(1024)}) custom-call(bf16[128,3712]{1,0:T(8,128)(2,1)} %get-tuple-element.190.grad_in, ...), custom_call_target="tpu_custom_call", output_to_operand_aliasing={{0}: (0, {})} | custom-call | bytes 2553640 | tf_op jit(solution)/shard_map/unpack/pallas_call | solution.py:697
  (83 shorter events, 22.7 us)
Async XLA Ops:
  2.4 7.2 %collective-permute-start.2 = (f32[8,1024]{1,0:T(8,128)}, f32[8,1024]{1,0:T(8,128)S(1)}, u32[]{:S(2)}, u32[]{:S(2)}) collective-permute-start(f32[8,1024]{1,0:T(8,128)} %get-tuple-element.106), channel_id=1, source_target_pairs={{0,24},{8,16},{16,8},{24,0},{1,25},{9,17},{17,9},{25,1},{2,26},{10... | collective-permute-start | bytes 98312 | tf_op jit(solution)/shard_map/ppermute | solution.py:720
  6.4 4.1 %collective-permute-start.1 = (f32[8,1024]{1,0:T(8,128)}, f32[8,1024]{1,0:T(8,128)S(1)}, u32[]{:S(2)}, u32[]{:S(2)}) collective-permute-start(f32[8,1024]{1,0:T(8,128)} %get-tuple-element.106), channel_id=1, source_target_pairs={{0,16},{8,24},{16,0},{24,8},{1,17},{9,25},{17,1},{25,9},{2,18},{10... | collective-permute-start | bytes 98312 | tf_op jit(solution)/shard_map/ppermute | solution.py:720
  6.9 4.1 %collective-permute-start = (f32[8,1024]{1,0:T(8,128)}, f32[8,1024]{1,0:T(8,128)S(1)}, u32[]{:S(2)}, u32[]{:S(2)}) collective-permute-start(f32[8,1024]{1,0:T(8,128)} %get-tuple-element.106), channel_id=1, source_target_pairs={{0,8},{8,0},{16,24},{24,16},{1,9},{9,1},{17,25},{25,17},{2,10},{10... | collective-permute-start | bytes 98312 | tf_op jit(solution)/shard_map/ppermute | solution.py:720
  7.0 4.5 %collective-permute-start.3 = (bf16[8,3712]{1,0:T(8,128)(2,1)}, bf16[8,3712]{1,0:T(8,128)(2,1)S(1)}, u32[]{:S(2)}, u32[]{:S(2)}) collective-permute-start(bf16[8,3712]{1,0:T(8,128)(2,1)} %get-tuple-element.109), channel_id=1, source_target_pairs={{0,1},{1,2},{2,3},{3,4},{4,5},{5,6},{6,7},{8,9},{9,10},{10,11},{11... | collective-permute-start | bytes 178184 | tf_op jit(solution)/shard_map/ppermute | solution.py:720
  12.4 2.9 %collective-permute-start.4 = (bf16[464,128]{1,0:T(8,128)(2,1)S(1)}, bf16[464,128]{1,0:T(8,128)(2,1)S(1)}, u32[]{:S(2)}, u32[]{:S(2)}) collective-permute-start(bf16[464,128]{1,0:T(8,128)(2,1)S(1)} %get-tuple-element.118), channel_id=1, source_target_pairs={{0,1},{1,0},{2,3},{3,2},{4,5},{5,4},{6,7},{7,6},{8,9},{9,8},{10,11... | collective-permute-start | bytes 356360 | tf_op jit(solution)/shard_map/ppermute | solution.py:720
  14.5 5.9 %collective-permute-start.6 = (bf16[464,128]{1,0:T(8,128)(2,1)S(1)}, bf16[464,128]{1,0:T(8,128)(2,1)S(1)}, u32[]{:S(2)}, u32[]{:S(2)}) collective-permute-start(bf16[464,128]{1,0:T(8,128)(2,1)S(1)} %get-tuple-element.124), channel_id=1, source_target_pairs={{0,1},{1,0},{2,3},{3,2},{4,5},{5,4},{6,7},{7,6},{8,9},{9,8},{10,11... | collective-permute-start | bytes 356360 | tf_op jit(solution)/shard_map/ppermute | solution.py:720
  15.4 9.5 %collective-permute-start.5 = (bf16[464,128]{1,0:T(8,128)(2,1)S(1)}, bf16[464,128]{1,0:T(8,128)(2,1)S(1)}, u32[]{:S(2)}, u32[]{:S(2)}) collective-permute-start(bf16[464,128]{1,0:T(8,128)(2,1)S(1)} %get-tuple-element.119.own), channel_id=1, source_target_pairs={{0,2},{1,3},{8,10},{9,11},{16,18},{17,19},{24,26},{25,27}} | collective-permute-start | bytes 356360 | tf_op jit(solution)/shard_map/ppermute | solution.py:720
  20.5 5.1 %collective-permute-start.7 = (bf16[464,128]{1,0:T(8,128)(2,1)S(1)}, bf16[464,128]{1,0:T(8,128)(2,1)S(1)}, u32[]{:S(2)}, u32[]{:S(2)}) collective-permute-start(bf16[464,128]{1,0:T(8,128)(2,1)S(1)} %get-tuple-element.125.own), channel_id=1, source_target_pairs={{0,2},{1,3},{8,10},{9,11},{16,18},{17,19},{24,26},{25,27}} | collective-permute-start | bytes 356360 | tf_op jit(solution)/shard_map/ppermute | solution.py:720
  24.9 3.8 %collective-permute-start.8 = (bf16[448,128]{1,0:T(8,128)(2,1)S(1)}, bf16[448,128]{1,0:T(8,128)(2,1)S(1)}, u32[]{:S(2)}, u32[]{:S(2)}) collective-permute-start(bf16[448,128]{1,0:T(8,128)(2,1)S(1)} %pass.8), channel_id=1, source_target_pairs={{2,4},{3,5},{10,12},{11,13},{18,20},{19,21},{26,28},{27,29}} | collective-permute-start | bytes 344072 | tf_op jit(solution)/shard_map/ppermute | solution.py:720
  25.7 3.8 %collective-permute-start.10 = (bf16[448,128]{1,0:T(8,128)(2,1)S(1)}, bf16[448,128]{1,0:T(8,128)(2,1)S(1)}, u32[]{:S(2)}, u32[]{:S(2)}) collective-permute-start(bf16[448,128]{1,0:T(8,128)(2,1)S(1)} %pass.9), channel_id=1, source_target_pairs={{2,4},{3,5},{10,12},{11,13},{18,20},{19,21},{26,28},{27,29}} | collective-permute-start | bytes 344072 | tf_op jit(solution)/shard_map/ppermute | solution.py:720
  28.8 1.6 %collective-permute-start.9 = (bf16[448,128]{1,0:T(8,128)(2,1)S(1)}, bf16[448,128]{1,0:T(8,128)(2,1)S(1)}, u32[]{:S(2)}, u32[]{:S(2)}) collective-permute-start(bf16[448,128]{1,0:T(8,128)(2,1)S(1)} %pass.10), channel_id=1, source_target_pairs={{4,6},{5,7},{12,14},{13,15},{20,22},{21,23},{28,30},{29,31}} | collective-permute-start | bytes 344072 | tf_op jit(solution)/shard_map/ppermute | solution.py:720
  36.0 5.4 %collective-permute-start.17 = (bf16[464,128]{1,0:T(8,128)(2,1)S(1)}, bf16[464,128]{1,0:T(8,128)(2,1)S(1)}, u32[]{:S(2)}, u32[]{:S(2)}) collective-permute-start(bf16[464,128]{1,0:T(8,128)(2,1)S(1)} %get-tuple-element.156.own), channel_id=1, source_target_pairs={{6,4},{7,5},{14,12},{15,13},{22,20},{23,21},{30,28},{31,29}} | collective-permute-start | bytes 356360 | tf_op jit(solution)/shard_map/ppermute | solution.py:720
  36.6 5.4 %collective-permute-start.16 = (bf16[464,128]{1,0:T(8,128)(2,1)S(1)}, bf16[464,128]{1,0:T(8,128)(2,1)S(1)}, u32[]{:S(2)}, u32[]{:S(2)}) collective-permute-start(bf16[464,128]{1,0:T(8,128)(2,1)S(1)} %get-tuple-element.154.own), channel_id=1, source_target_pairs={{6,4},{7,5},{14,12},{15,13},{22,20},{23,21},{30,28},{31,29}} | collective-permute-start | bytes 356360 | tf_op jit(solution)/shard_map/ppermute | solution.py:720
  41.4 6.9 %collective-permute-start.20 = (bf16[448,128]{1,0:T(8,128)(2,1)S(1)}, bf16[448,128]{1,0:T(8,128)(2,1)S(1)}, u32[]{:S(2)}, u32[]{:S(2)}) collective-permute-start(bf16[448,128]{1,0:T(8,128)(2,1)S(1)} %pass.13), channel_id=1, source_target_pairs={{4,2},{5,3},{12,10},{13,11},{20,18},{21,19},{28,26},{29,27}} | collective-permute-start | bytes 344072 | tf_op jit(solution)/shard_map/ppermute | solution.py:720
  42.1 7.5 %collective-permute-start.18 = (bf16[448,128]{1,0:T(8,128)(2,1)S(1)}, bf16[448,128]{1,0:T(8,128)(2,1)S(1)}, u32[]{:S(2)}, u32[]{:S(2)}) collective-permute-start(bf16[448,128]{1,0:T(8,128)(2,1)S(1)} %pass.12), channel_id=1, source_target_pairs={{4,2},{5,3},{12,10},{13,11},{20,18},{21,19},{28,26},{29,27}} | collective-permute-start | bytes 344072 | tf_op jit(solution)/shard_map/ppermute | solution.py:720
  48.3 11.5 %collective-permute-start.21 = (bf16[448,128]{1,0:T(8,128)(2,1)S(1)}, bf16[448,128]{1,0:T(8,128)(2,1)S(1)}, u32[]{:S(2)}, u32[]{:S(2)}) collective-permute-start(bf16[448,128]{1,0:T(8,128)(2,1)S(1)} %pass.15), channel_id=1, source_target_pairs={{2,0},{3,1},{10,8},{11,9},{18,16},{19,17},{26,24},{27,25}} | collective-permute-start | bytes 344072 | tf_op jit(solution)/shard_map/ppermute | solution.py:720
  49.7 12.3 %collective-permute-start.19 = (bf16[448,128]{1,0:T(8,128)(2,1)S(1)}, bf16[448,128]{1,0:T(8,128)(2,1)S(1)}, u32[]{:S(2)}, u32[]{:S(2)}) collective-permute-start(bf16[448,128]{1,0:T(8,128)(2,1)S(1)} %pass.14), channel_id=1, source_target_pairs={{2,0},{3,1},{10,8},{11,9},{18,16},{19,17},{26,24},{27,25}} | collective-permute-start | bytes 344072 | tf_op jit(solution)/shard_map/ppermute | solution.py:720
  60.0 3.6 %collective-permute-start.23 = (bf16[448,128]{1,0:T(8,128)(2,1)S(1)}, bf16[448,128]{1,0:T(8,128)(2,1)S(1)}, u32[]{:S(2)}, u32[]{:S(2)}) collective-permute-start(bf16[448,128]{1,0:T(8,128)(2,1)S(1)} %get-tuple-element.182), channel_id=1, source_target_pairs={{0,1},{1,0},{2,3},{3,2},{4,5},{5,4},{6,7},{7,6},{8,9},{9,8},{10,11... | collective-permute-start | bytes 344072 | tf_op jit(solution)/shard_map/ppermute | solution.py:720
  65.9 4.9 %collective-permute-start.24 = (f32[8,1024]{1,0:T(8,128)S(1)}, f32[8,1024]{1,0:T(8,128)S(1)}, u32[]{:S(2)}, u32[]{:S(2)}) collective-permute-start(f32[8,1024]{1,0:T(8,128)S(1)} %get-tuple-element.185), channel_id=1, source_target_pairs={{0,8},{8,16},{16,24},{24,0},{1,9},{9,17},{17,25},{25,1},{2,10},{10... | collective-permute-start | bytes 98312 | tf_op jit(solution)/shard_map/ppermute | solution.py:720
  67.4 3.9 %collective-permute-start.25 = (f32[8,1024]{1,0:T(8,128)S(1)}, f32[8,1024]{1,0:T(8,128)S(1)}, u32[]{:S(2)}, u32[]{:S(2)}) collective-permute-start(f32[8,1024]{1,0:T(8,128)S(1)} %get-tuple-element.186), channel_id=1, source_target_pairs={{0,16},{8,24},{16,0},{24,8},{1,17},{9,25},{17,1},{25,9},{2,18},{10... | collective-permute-start | bytes 98312 | tf_op jit(solution)/shard_map/ppermute | solution.py:720
  68.9 3.9 %collective-permute-start.26 = (f32[8,1024]{1,0:T(8,128)S(1)}, f32[8,1024]{1,0:T(8,128)S(1)}, u32[]{:S(2)}, u32[]{:S(2)}) collective-permute-start(f32[8,1024]{1,0:T(8,128)S(1)} %get-tuple-element.187), channel_id=1, source_target_pairs={{0,24},{8,0},{16,8},{24,16},{1,25},{9,1},{17,9},{25,17},{2,26},{10... | collective-permute-start | bytes 98312 | tf_op jit(solution)/shard_map/ppermute | solution.py:720
  74.2 6.8 %collective-permute-start.28 = (f32[24,1024]{1,0:T(8,128)S(1)}, f32[24,1024]{1,0:T(8,128)S(1)}, u32[]{:S(2)}, u32[]{:S(2)}) collective-permute-start(f32[24,1024]{1,0:T(8,128)S(1)} %get-tuple-element.192), channel_id=1, source_target_pairs={{0,6},{1,7},{2,0},{3,1},{4,2},{5,3},{6,4},{7,5},{8,14},{9,15},{10,... | collective-permute-start | bytes 294920 | tf_op jit(solution)/shard_map/ppermute | solution.py:720
  74.3 4.9 %collective-permute-start.30 = (f32[8,1024]{1,0:T(8,128)S(1)}, f32[8,1024]{1,0:T(8,128)S(1)}, u32[]{:S(2)}, u32[]{:S(2)}) collective-permute-start(f32[8,1024]{1,0:T(8,128)S(1)} %get-tuple-element.188.refs_0_), channel_id=1, source_target_pairs={{0,4},{1,5},{2,6},{3,7},{4,0},{5,1},{6,2},{7,3},{8,12},{9,13},{10,... | collective-permute-start | bytes 98312 | tf_op jit(solution)/shard_map/ppermute | solution.py:720
  75.3 5.7 %collective-permute-start.29 = (f32[8,1024]{1,0:T(8,128)S(1)}, f32[8,1024]{1,0:T(8,128)S(1)}, u32[]{:S(2)}, u32[]{:S(2)}) collective-permute-start(f32[8,1024]{1,0:T(8,128)S(1)} %get-tuple-element.188.refs_0_), channel_id=1, source_target_pairs={{0,2},{1,3},{2,4},{3,5},{4,6},{5,7},{6,0},{7,1},{8,10},{9,11},{10,... | collective-permute-start | bytes 98312 | tf_op jit(solution)/shard_map/ppermute | solution.py:720
  (10 other events, 27.6 us)

commit v5 on v4

--- a/solution.py
+++ b/solution.py
@@ -512,12 +512,11 @@
     grad_gain, grad_small, state_in, end_in, write_in, *rest
 ):
     given, rest, scratch = rest[: 2 * STREAMS], rest[2 * STREAMS : -4], rest[-4:]
-    slopes, whole, grad_dt, *outs, cut = rest
+    slopes, whole, grad_raw, *outs, cut = rest
     parts = len(outs)
     position_here = here_at()[2]
     length, channels = conv.shape
     width, gain_width, heads_here = sizes
-    heads = heads_here * parts
     step = cols[0]
     last = cols[1, length - 1 : length, :]
     state_sums, end_sums, write_grad = close_side(
@@ -536,7 +535,7 @@
     log_grad = dot_parts(upper, change, 2) + end_grad
     rate = jnp.exp(small[1:2, :])
     raw_grad = (into / step - rate * log_grad) * (1.0 - jnp.exp(-step))
-    grad_dt[...] = raw_grad.T[0:heads, :]
+    grad_raw[...] = raw_grad
     vectors = (
         jnp.sum(raw_grad, axis=0, keepdims=True),
         jnp.sum(-rate * step * log_grad, axis=0, keepdims=True),
@@ -557,7 +556,8 @@
         outs[distance][...] = cut[lax.rem(position_here + distance, parts)]
 
 
-def input_kernel(taps, full, slopes, grad_x, ending):
+def input_kernel(taps, full, slopes, grad_raw, grad_x, ending, grad_dt):
+    grad_dt[...] = grad_raw[...].T[0 : grad_dt.shape[0], :]
     length, channels = grad_x.shape
     for position in range(channels // LANES):
         here = block(position)
@@ -578,10 +578,8 @@
             back[at : at + 1, block(position % folded)] = ahead[HALO - taps + 1 + tap : HALO - taps + 2 + tap]
 
 
-def unpack_kernel(terms, chips, taps, grad_in, ending, from_core, from_chip, *refs):
-    given, refs = refs[:terms], refs[terms:]
+def patch_kernel(chips, taps, grad_in, ending, from_core, from_chip, grad_x, late, sem):
     core, chip, _ = here_at()
-    grad_x, cw, cb, dtb, al, sk, gain, late, sem = refs
     rows = late.shape[0]
     channels = ending.shape[1]
     folded = from_core.shape[1] // LANES
@@ -598,6 +596,11 @@
         late[:, here] = (ending[:, here] + jnp.concatenate([padding] + lines, axis=0)).astype(BF16)
     copy = pltpu.make_async_copy(late, grad_x.at[pl.ds(grad_x.shape[0] - rows, rows)], sem)
     copy.start()
+    copy.wait()
+
+
+def unpack_kernel(terms, taps, *refs):
+    given, (cw, cb, dtb, al, sk, gain) = refs[:terms], refs[terms:]
     total = given[0][0:SMALL, :]
     for ref in given[1:]:
         total = total + ref[0:SMALL, :]
@@ -607,7 +610,6 @@
     gain[...] = total[taps + 1, 0 : gain.shape[0]]
     for number, ref in enumerate((dtb, al, sk)):
         ref[...] = total[taps + 2 : taps + 3, number * LANES : number * LANES + ref.shape[1]]
-    copy.wait()
 
 
 def add_kernel(*refs):
@@ -964,9 +966,9 @@
         scratch,
         name="close_own",
     )
-    slopes, whole, grad_dt, *shares = call(
+    slopes, whole, grad_raw, *shares = call(
         functools.partial(close_kernel, taps, sizes),
-        shapes[:2] + [like((heads, length))] + [piece_like] * parts,
+        shapes[:2] + [square] + [piece_like] * parts,
         [slopes, whole] + fixed + [small, grad_values, grad_vecs, out_sums, in_sums, grad_gain, grad_small]
         + sums + entry_got + leave_got,
         [pltpu.VMEM((parts, SMALL, piece_width), F32)] + scratch,
@@ -993,17 +995,26 @@
         terms += [behind] if chips > 1 else []
     else:
         terms = [lax.psum(alone, "seq") * 0.5]
-    grad_x, ending = call(
+    grad_x, ending, grad_dt = call(
         functools.partial(input_kernel, taps),
-        [like((length, channels), BF16), like((2 * HALO, channels))],
-        [full, after(slopes, alone)],
+        [like((length, channels), BF16), like((2 * HALO, channels)), like((heads, length))],
+        [full, after(slopes, alone), grad_raw],
         flops=length * channels * 16,
         name="inputs",
     )
-    grad_x, cw, cb, dtb, al, sk, gn = call(
-        functools.partial(unpack_kernel, len(terms), chips, taps),
+    grad_x = call(
+        functools.partial(patch_kernel, chips, taps),
+        [like((length, channels), BF16)],
+        [grad_x, ending, partner, behind],
+        [pltpu.VMEM((2 * HALO, channels), BF16), pltpu.SemaphoreType.DMA],
+        fetched=(0,),
+        aliases={0: 0},
+        flops=length * channels * 8,
+        name="patch",
+    )[0]
+    cw, cb, dtb, al, sk, gn = call(
+        functools.partial(unpack_kernel, len(terms), taps),
         [
-            like((length, channels), BF16),
             like((taps, width)),
             like((width,)),
             like((1, heads_here)),
@@ -1011,10 +1022,7 @@
             like((1, heads_here)),
             like((gain_width,)),
         ],
-        [grad_x, ending, partner, behind] + terms,
-        [pltpu.VMEM((2 * HALO, channels), BF16), pltpu.SemaphoreType.DMA],
-        fetched=(0,),
-        aliases={0: 0},
+        terms,
         name="unpack",
     )
     return (

time: 82.9 us -> 81.5 us (0.983)
    pallas_call x38 -> x39, Pallas kernels: 32.3 us -> 31.8 us  [call(): pl.pallas_call(kernel, out_shape=outs, in_specs=specs, out_specs=[pl.Bloc...]
  transfers between devices with their start and end apart: 31 -> 31, of which waited for: 12 -> 12; matrix products, arithmetic and copies ran while one was open for 2% -> 2% of each run, Pallas kernels for 30% -> 31%
where the time goes in v5:
time: 81.5 us; the launch traced here: 81.1 us
  Pallas kernels  31.8 us (39%)
  starting transfers between devices  29.2 us (36%)
  waiting for transfers between devices  17.7 us (22%)
  other arithmetic  1.32 us (2%)
  between operations  1.11 us (1%)
    pallas_call x39, Pallas kernels, call(): pl.pallas_call(kernel, out_shape=outs, in_specs=specs, out_specs=[pl.Bloc...  31.8 us
    ppermute x31, starting transfers between devices, shift(): lax.ppermute(value, axis, [(i, j) for i, j in pairs if 0 <= j < count])  29.2 us
    ppermute x31, waiting for transfers between devices, shift(): lax.ppermute(value, axis, [(i, j) for i, j in pairs if 0 <= j < count])  17.7 us
  transfers between devices with their start and end apart: 31, of which 12 were waited for; matrix products, arithmetic and copies ran while one was open for 2% of the time, Pallas kernels for 31%

profile of v5, /device:TPU:0, one launch (start us, length us, event | category | flops | bytes accessed | tf_op | source)
XLA Modules:
  0.0 81.1 jit_solution(14782836478803104614)
XLA Ops:
  0.6 1.8 %open.1 = (bf16[8,3712]{1,0:T(8,128)(2,1)}, f32[8,1024]{1,0:T(8,128)}, f32[16,1024]{1,0:T(8,128)}) custom-call(bf16[128,3712]{1,0:T(8,128)(2,1)} %bitcast.22, f32[56,128]{1,0:T(8,128)} %bitcast.25, f32[4,928]{1,0:T(4,128)} %cw.1, f32[1,928]{1,0:T(1,128)} %bitcast.26, f32[1,14]{1,0:T(1,128)} %bitcast.27, f32[1,14]{1,0:T(1,128)} %bitcast.28, ...), custom_call_target="tpu_custom_call" | custom-call | bytes 1158952 | tf_op jit(solution)/shard_map/open/pallas_call | solution.py:699
  2.4 4.0 %collective-permute-start.2 = (f32[8,1024]{1,0:T(8,128)}, f32[8,1024]{1,0:T(8,128)S(1)}, u32[]{:S(2)}, u32[]{:S(2)}) collective-permute-start(f32[8,1024]{1,0:T(8,128)} %get-tuple-element.106), channel_id=1, source_target_pairs={{0,24},{8,16},{16,8},{24,0},{1,25},{9,17},{17,9},{25,1},{2,26},{10... | collective-permute-start | bytes 98312 | tf_op jit(solution)/shard_map/ppermute | solution.py:722
  7.0 1.3 %collective-permute-start.3 = (bf16[8,3712]{1,0:T(8,128)(2,1)}, bf16[8,3712]{1,0:T(8,128)(2,1)S(1)}, u32[]{:S(2)}, u32[]{:S(2)}) collective-permute-start(bf16[8,3712]{1,0:T(8,128)(2,1)} %get-tuple-element.109), channel_id=1, source_target_pairs={{0,1},{1,2},{2,3},{3,4},{4,5},{5,6},{6,7},{8,9},{9,10},{10,11},{11... | collective-permute-start | bytes 178184 | tf_op jit(solution)/shard_map/ppermute | solution.py:722
  8.3 1.3 %pad_convert_fusion.lifted = f32[136,3712]{1,0:T(8,128)S(1)} fusion(bf16[128,3712]{1,0:T(8,128)(2,1)} %bitcast.23), kind=kLoop, calls=%fused_computation | loop fusion | flops 504832 | bytes 2969600 | tf_op jit(solution)/shard_map/jit(_pad)/pad | solution.py:824
  12.4 1.4 %collective-permute-start.4 = (bf16[464,128]{1,0:T(8,128)(2,1)S(1)}, bf16[464,128]{1,0:T(8,128)(2,1)S(1)}, u32[]{:S(2)}, u32[]{:S(2)}) collective-permute-start(bf16[464,128]{1,0:T(8,128)(2,1)S(1)} %get-tuple-element.118), channel_id=1, source_target_pairs={{0,1},{1,0},{2,3},{3,2},{4,5},{5,4},{6,7},{7,6},{8,9},{9,8},{10,11... | collective-permute-start | bytes 356360 | tf_op jit(solution)/shard_map/ppermute | solution.py:722
  15.4 4.2 %collective-permute-start.5 = (bf16[464,128]{1,0:T(8,128)(2,1)S(1)}, bf16[464,128]{1,0:T(8,128)(2,1)S(1)}, u32[]{:S(2)}, u32[]{:S(2)}) collective-permute-start(bf16[464,128]{1,0:T(8,128)(2,1)S(1)} %get-tuple-element.119.own), channel_id=1, source_target_pairs={{0,2},{1,3},{8,10},{9,11},{16,18},{17,19},{24,26},{25,27}} | collective-permute-start | bytes 356360 | tf_op jit(solution)/shard_map/ppermute | solution.py:722
  20.5 1.3 %collective-permute-start.7 = (bf16[464,128]{1,0:T(8,128)(2,1)S(1)}, bf16[464,128]{1,0:T(8,128)(2,1)S(1)}, u32[]{:S(2)}, u32[]{:S(2)}) collective-permute-start(bf16[464,128]{1,0:T(8,128)(2,1)S(1)} %get-tuple-element.125.own), channel_id=1, source_target_pairs={{0,2},{1,3},{8,10},{9,11},{16,18},{17,19},{24,26},{25,27}} | collective-permute-start | bytes 356360 | tf_op jit(solution)/shard_map/ppermute | solution.py:722
  21.8 3.1 %intra.1 = (f32[128,3584]{1,0:T(8,128)S(1)}, f32[128,3712]{1,0:T(8,128)S(1)}) custom-call(f32[136,3712]{1,0:T(8,128)S(1)} %get-tuple-element.112.rows, f32[8,3840]{1,0:T(8,128)S(1)} %get-tuple-element.107.full, bf16[128,3712]{1,0:T(8,128)(2,1)S(1)} %get-tuple-element.157.conv, f32[2,128,128]{2,1,0:T(8,128)S(1)} %get-tuple-element.133.cols, ...), custom_call_target="tpu_custom_call" | custom-call | flops 117440512 | bytes 7159808 | tf_op jit(solution)/shard_map/intra/pallas_call | solution.py:699
  26.4 2.4 %factors.1 = (f32[128,3584]{1,0:T(8,128)S(1)}, f32[128,3584]{1,0:T(8,128)S(1)}, f32[128,3584]{1,0:T(8,128)S(1)}, bf16[1792,128]{1,0:T(8,128)(2,1)S(1)}, f32[3,128,3712]{2,1,0:T(8,128)S(1)}) custom-call(f32[2,128,128]{2,1,0:T(8,128)S(1)} %get-tuple-element.133.cols, bf16[128,3584]{1,0:T(8,128)(2,1)S(1)} %bitcast.18, bf16[128,3584]{1,0:T(8,128)(2,1)S(1)} %bitcast.20, ...), custom_call_target="tpu_custom_call" | custom-call | flops 7340032 | bytes 15665152 | tf_op jit(solution)/shard_map/factors/pallas_call | solution.py:699
  37.3 4.0 %gates.1 = (bf16[128,3584]{1,0:T(8,128)(2,1)}, f32[128,3584]{1,0:T(8,128)S(1)}, f32[128,128]{1,0:T(8,128)S(1)}, f32[1,3584]{1,0:T(1,128)S(1)}, f32[8,128]{1,0:T(8,128)S(1)}, /*index=5*/f32[128,128]{1,0:T(8,128)S(1)}) custom-call(f32[128,3584]{1,0:T(8,128)S(1)} %get-tuple-element.150.mixed, bf16[128,3712]{1,0:T(8,128)(2,1)S(1)} %get-tuple-element.157.conv, ...), custom_call_target="tpu_custom_call" | custom-call | flops 117440512 | bytes 8196096 | tf_op jit(solution)/shard_map/gates/pallas_call | solution.py:699
  42.8 5.4 %back.1 = (f32[128,3584]{1,0:T(8,128)S(1)}, f32[128,128]{1,0:T(8,128)S(1)}, f32[128,128]{1,0:T(8,128)S(1)}) custom-call(f32[128,3584]{1,0:T(8,128)S(1)} %get-tuple-element.164.grad_mixed, bf16[128,3712]{1,0:T(8,128)(2,1)S(1)} %get-tuple-element.157.conv, f32[2,128,128]{2,1,0:T(8,128)S(1)} %get-tuple-element.133.cols, ...), custom_call_target="tpu_custom_call" | custom-call | flops 234881024 | bytes 5148672 | tf_op jit(solution)/shard_map/back/pallas_call | solution.py:699
  48.3 1.3 %collective-permute-start.21 = (bf16[448,128]{1,0:T(8,128)(2,1)S(1)}, bf16[448,128]{1,0:T(8,128)(2,1)S(1)}, u32[]{:S(2)}, u32[]{:S(2)}) collective-permute-start(bf16[448,128]{1,0:T(8,128)(2,1)S(1)} %pass.15), channel_id=1, source_target_pairs={{2,0},{3,1},{10,8},{11,9},{18,16},{19,17},{26,24},{27,25}} | collective-permute-start | bytes 344072 | tf_op jit(solution)/shard_map/ppermute | solution.py:722
  49.7 1.5 %collective-permute-start.19 = (bf16[448,128]{1,0:T(8,128)(2,1)S(1)}, bf16[448,128]{1,0:T(8,128)(2,1)S(1)}, u32[]{:S(2)}, u32[]{:S(2)}) collective-permute-start(bf16[448,128]{1,0:T(8,128)(2,1)S(1)} %pass.14), channel_id=1, source_target_pairs={{2,0},{3,1},{10,8},{11,9},{18,16},{19,17},{26,24},{27,25}} | collective-permute-start | bytes 344072 | tf_op jit(solution)/shard_map/ppermute | solution.py:722
  51.2 8.7 %collective-permute-done.21.refs_2_ = bf16[448,128]{1,0:T(8,128)(2,1)S(1)} collective-permute-done((bf16[448,128]{1,0:T(8,128)(2,1)S(1)}, bf16[448,128]{1,0:T(8,128)(2,1)S(1)}, u32[]{:S(2)}, u32[]{:S(2)}) %collective-permute-start.21) | collective-permute-done | bytes 114720 | tf_op jit(solution)/shard_map/ppermute | solution.py:722
  60.1 1.8 %collective-permute-done.19.refs_2_ = bf16[448,128]{1,0:T(8,128)(2,1)S(1)} collective-permute-done((bf16[448,128]{1,0:T(8,128)(2,1)S(1)}, bf16[448,128]{1,0:T(8,128)(2,1)S(1)}, u32[]{:S(2)}, u32[]{:S(2)}) %collective-permute-start.19) | collective-permute-done | bytes 114720 | tf_op jit(solution)/shard_map/ppermute | solution.py:722
  62.2 1.5 %close_own.1 = (f32[144,3712]{1,0:T(8,128)S(1)}, f32[8,3840]{1,0:T(8,128)S(1)}, f32[128,128]{1,0:T(8,128)S(1)}, f32[8,128]{1,0:T(8,128)S(1)}, f32[128,128]{1,0:T(8,128)S(1)}) custom-call(f32[136,3712]{1,0:T(8,128)S(1)} %get-tuple-element.112.rows, f32[3,128,3712]{2,1,0:T(8,128)S(1)} %get-tuple-element.135.shifted, ...), custom_call_target="tpu_custom_call" | custom-call | bytes 15851520 | tf_op jit(solution)/shard_map/close_own/pallas_call | solution.py:699
  63.7 1.6 %close.1 = (f32[144,3712]{1,0:T(8,128)S(1)}, f32[8,3840]{1,0:T(8,128)S(1)}, f32[128,128]{1,0:T(8,128)S(1)}, f32[8,1024]{1,0:T(8,128)S(1)}, f32[8,1024]{1,0:T(8,1...) custom-call(f32[144,3712]{1,0:T(8,128)S(1)} %get-tuple-element.171.slopes_in,, ...), custom_call_target="tpu_custom_call", output_to_operand_aliasing={{0}: (0, {}), {1}: (1, {})} | custom-call | bytes 18528256 | tf_op jit(solution)/shard_map/close/pallas_call | solution.py:699
  65.3 1.6 %collective-permute-start.24 = (f32[8,1024]{1,0:T(8,128)S(1)}, f32[8,1024]{1,0:T(8,128)S(1)}, u32[]{:S(2)}, u32[]{:S(2)}) collective-permute-start(f32[8,1024]{1,0:T(8,128)S(1)} %get-tuple-element.185), channel_id=1, source_target_pairs={{0,8},{8,16},{16,24},{24,0},{1,9},{9,17},{17,25},{25,1},{2,10},{10... | collective-permute-start | bytes 98312 | tf_op jit(solution)/shard_map/ppermute | solution.py:722
  66.9 1.5 %collective-permute-start.25 = (f32[8,1024]{1,0:T(8,128)S(1)}, f32[8,1024]{1,0:T(8,128)S(1)}, u32[]{:S(2)}, u32[]{:S(2)}) collective-permute-start(f32[8,1024]{1,0:T(8,128)S(1)} %get-tuple-element.186), channel_id=1, source_target_pairs={{0,16},{8,24},{16,0},{24,8},{1,17},{9,25},{17,1},{25,9},{2,18},{10... | collective-permute-start | bytes 98312 | tf_op jit(solution)/shard_map/ppermute | solution.py:722
  68.4 1.4 %collective-permute-start.26 = (f32[8,1024]{1,0:T(8,128)S(1)}, f32[8,1024]{1,0:T(8,128)S(1)}, u32[]{:S(2)}, u32[]{:S(2)}) collective-permute-start(f32[8,1024]{1,0:T(8,128)S(1)} %get-tuple-element.187), channel_id=1, source_target_pairs={{0,24},{8,0},{16,8},{24,16},{1,25},{9,1},{17,9},{25,17},{2,26},{10... | collective-permute-start | bytes 98312 | tf_op jit(solution)/shard_map/ppermute | solution.py:722
  70.8 1.5 %collective-permute-done.26.refs_3_ = f32[8,1024]{1,0:T(8,128)S(1)} collective-permute-done((f32[8,1024]{1,0:T(8,128)S(1)}, f32[8,1024]{1,0:T(8,128)S(1)}, u32[]{:S(2)}, u32[]{:S(2)}) %collective-permute-start.26) | collective-permute-done | bytes 32800 | tf_op jit(solution)/shard_map/ppermute | solution.py:722
  72.4 1.3 %collective-permute-done.27.other.from_core = f32[24,1024]{1,0:T(8,128)S(1)} collective-permute-done((f32[24,1024]{1,0:T(8,128)S(1)}, f32[24,1024]{1,0:T(8,128)S(1)}, u32[]{:S(2)}, u32[]{:S(2)}) %collective-permute-start.27) | collective-permute-done | bytes 98336 | tf_op jit(solution)/shard_map/ppermute | solution.py:722
  75.8 2.4 %inputs.1 = (bf16[128,3712]{1,0:T(8,128)(2,1)}, f32[16,3712]{1,0:T(8,128)S(1)}, f32[56,128]{1,0:T(8,128)}) custom-call(f32[8,3840]{1,0:T(8,128)S(1)} %get-tuple-element.107.full, f32[144,3712]{1,0:T(8,128)S(1)} %get-tuple-element.189.slopes, f32[128,128]{1,0:T(8,128)S(1)} %get-tuple-element.190.grad_raw), custom_call_target="tpu_custom_call" | custom-call | flops 7602176 | bytes 3543040 | tf_op jit(solution)/shard_map/inputs/pallas_call | solution.py:699
  78.1 1.5 %collective-permute-done.28.from_chip.refs_3_ = f32[24,1024]{1,0:T(8,128)S(1)} collective-permute-done((f32[24,1024]{1,0:T(8,128)S(1)}, f32[24,1024]{1,0:T(8,128)S(1)}, u32[]{:S(2)}, u32[]{:S(2)}) %collective-permute-start.28) | collective-permute-done | bytes 98336 | tf_op jit(solution)/shard_map/ppermute | solution.py:722
  (84 shorter events, 22.3 us)
Async XLA Ops:
  2.4 7.2 %collective-permute-start.2 = (f32[8,1024]{1,0:T(8,128)}, f32[8,1024]{1,0:T(8,128)S(1)}, u32[]{:S(2)}, u32[]{:S(2)}) collective-permute-start(f32[8,1024]{1,0:T(8,128)} %get-tuple-element.106), channel_id=1, source_target_pairs={{0,24},{8,16},{16,8},{24,0},{1,25},{9,17},{17,9},{25,1},{2,26},{10... | collective-permute-start | bytes 98312 | tf_op jit(solution)/shard_map/ppermute | solution.py:722
  6.4 4.1 %collective-permute-start.1 = (f32[8,1024]{1,0:T(8,128)}, f32[8,1024]{1,0:T(8,128)S(1)}, u32[]{:S(2)}, u32[]{:S(2)}) collective-permute-start(f32[8,1024]{1,0:T(8,128)} %get-tuple-element.106), channel_id=1, source_target_pairs={{0,16},{8,24},{16,0},{24,8},{1,17},{9,25},{17,1},{25,9},{2,18},{10... | collective-permute-start | bytes 98312 | tf_op jit(solution)/shard_map/ppermute | solution.py:722
  6.9 4.1 %collective-permute-start = (f32[8,1024]{1,0:T(8,128)}, f32[8,1024]{1,0:T(8,128)S(1)}, u32[]{:S(2)}, u32[]{:S(2)}) collective-permute-start(f32[8,1024]{1,0:T(8,128)} %get-tuple-element.106), channel_id=1, source_target_pairs={{0,8},{8,0},{16,24},{24,16},{1,9},{9,1},{17,25},{25,17},{2,10},{10... | collective-permute-start | bytes 98312 | tf_op jit(solution)/shard_map/ppermute | solution.py:722
  7.0 4.5 %collective-permute-start.3 = (bf16[8,3712]{1,0:T(8,128)(2,1)}, bf16[8,3712]{1,0:T(8,128)(2,1)S(1)}, u32[]{:S(2)}, u32[]{:S(2)}) collective-permute-start(bf16[8,3712]{1,0:T(8,128)(2,1)} %get-tuple-element.109), channel_id=1, source_target_pairs={{0,1},{1,2},{2,3},{3,4},{4,5},{5,6},{6,7},{8,9},{9,10},{10,11},{11... | collective-permute-start | bytes 178184 | tf_op jit(solution)/shard_map/ppermute | solution.py:722
  12.4 2.9 %collective-permute-start.4 = (bf16[464,128]{1,0:T(8,128)(2,1)S(1)}, bf16[464,128]{1,0:T(8,128)(2,1)S(1)}, u32[]{:S(2)}, u32[]{:S(2)}) collective-permute-start(bf16[464,128]{1,0:T(8,128)(2,1)S(1)} %get-tuple-element.118), channel_id=1, source_target_pairs={{0,1},{1,0},{2,3},{3,2},{4,5},{5,4},{6,7},{7,6},{8,9},{9,8},{10,11... | collective-permute-start | bytes 356360 | tf_op jit(solution)/shard_map/ppermute | solution.py:722
  14.5 5.9 %collective-permute-start.6 = (bf16[464,128]{1,0:T(8,128)(2,1)S(1)}, bf16[464,128]{1,0:T(8,128)(2,1)S(1)}, u32[]{:S(2)}, u32[]{:S(2)}) collective-permute-start(bf16[464,128]{1,0:T(8,128)(2,1)S(1)} %get-tuple-element.124), channel_id=1, source_target_pairs={{0,1},{1,0},{2,3},{3,2},{4,5},{5,4},{6,7},{7,6},{8,9},{9,8},{10,11... | collective-permute-start | bytes 356360 | tf_op jit(solution)/shard_map/ppermute | solution.py:722
  15.4 9.5 %collective-permute-start.5 = (bf16[464,128]{1,0:T(8,128)(2,1)S(1)}, bf16[464,128]{1,0:T(8,128)(2,1)S(1)}, u32[]{:S(2)}, u32[]{:S(2)}) collective-permute-start(bf16[464,128]{1,0:T(8,128)(2,1)S(1)} %get-tuple-element.119.own), channel_id=1, source_target_pairs={{0,2},{1,3},{8,10},{9,11},{16,18},{17,19},{24,26},{25,27}} | collective-permute-start | bytes 356360 | tf_op jit(solution)/shard_map/ppermute | solution.py:722
  20.5 5.1 %collective-permute-start.7 = (bf16[464,128]{1,0:T(8,128)(2,1)S(1)}, bf16[464,128]{1,0:T(8,128)(2,1)S(1)}, u32[]{:S(2)}, u32[]{:S(2)}) collective-permute-start(bf16[464,128]{1,0:T(8,128)(2,1)S(1)} %get-tuple-element.125.own), channel_id=1, source_target_pairs={{0,2},{1,3},{8,10},{9,11},{16,18},{17,19},{24,26},{25,27}} | collective-permute-start | bytes 356360 | tf_op jit(solution)/shard_map/ppermute | solution.py:722
  24.9 3.8 %collective-permute-start.8 = (bf16[448,128]{1,0:T(8,128)(2,1)S(1)}, bf16[448,128]{1,0:T(8,128)(2,1)S(1)}, u32[]{:S(2)}, u32[]{:S(2)}) collective-permute-start(bf16[448,128]{1,0:T(8,128)(2,1)S(1)} %pass.8), channel_id=1, source_target_pairs={{2,4},{3,5},{10,12},{11,13},{18,20},{19,21},{26,28},{27,29}} | collective-permute-start | bytes 344072 | tf_op jit(solution)/shard_map/ppermute | solution.py:722
  25.7 3.8 %collective-permute-start.10 = (bf16[448,128]{1,0:T(8,128)(2,1)S(1)}, bf16[448,128]{1,0:T(8,128)(2,1)S(1)}, u32[]{:S(2)}, u32[]{:S(2)}) collective-permute-start(bf16[448,128]{1,0:T(8,128)(2,1)S(1)} %pass.9), channel_id=1, source_target_pairs={{2,4},{3,5},{10,12},{11,13},{18,20},{19,21},{26,28},{27,29}} | collective-permute-start | bytes 344072 | tf_op jit(solution)/shard_map/ppermute | solution.py:722
  28.8 1.6 %collective-permute-start.9 = (bf16[448,128]{1,0:T(8,128)(2,1)S(1)}, bf16[448,128]{1,0:T(8,128)(2,1)S(1)}, u32[]{:S(2)}, u32[]{:S(2)}) collective-permute-start(bf16[448,128]{1,0:T(8,128)(2,1)S(1)} %pass.10), channel_id=1, source_target_pairs={{4,6},{5,7},{12,14},{13,15},{20,22},{21,23},{28,30},{29,31}} | collective-permute-start | bytes 344072 | tf_op jit(solution)/shard_map/ppermute | solution.py:722
  36.0 5.4 %collective-permute-start.17 = (bf16[464,128]{1,0:T(8,128)(2,1)S(1)}, bf16[464,128]{1,0:T(8,128)(2,1)S(1)}, u32[]{:S(2)}, u32[]{:S(2)}) collective-permute-start(bf16[464,128]{1,0:T(8,128)(2,1)S(1)} %get-tuple-element.156.own), channel_id=1, source_target_pairs={{6,4},{7,5},{14,12},{15,13},{22,20},{23,21},{30,28},{31,29}} | collective-permute-start | bytes 356360 | tf_op jit(solution)/shard_map/ppermute | solution.py:722
  36.6 5.4 %collective-permute-start.16 = (bf16[464,128]{1,0:T(8,128)(2,1)S(1)}, bf16[464,128]{1,0:T(8,128)(2,1)S(1)}, u32[]{:S(2)}, u32[]{:S(2)}) collective-permute-start(bf16[464,128]{1,0:T(8,128)(2,1)S(1)} %get-tuple-element.154.own), channel_id=1, source_target_pairs={{6,4},{7,5},{14,12},{15,13},{22,20},{23,21},{30,28},{31,29}} | collective-permute-start | bytes 356360 | tf_op jit(solution)/shard_map/ppermute | solution.py:722
  41.4 6.9 %collective-permute-start.20 = (bf16[448,128]{1,0:T(8,128)(2,1)S(1)}, bf16[448,128]{1,0:T(8,128)(2,1)S(1)}, u32[]{:S(2)}, u32[]{:S(2)}) collective-permute-start(bf16[448,128]{1,0:T(8,128)(2,1)S(1)} %pass.13), channel_id=1, source_target_pairs={{4,2},{5,3},{12,10},{13,11},{20,18},{21,19},{28,26},{29,27}} | collective-permute-start | bytes 344072 | tf_op jit(solution)/shard_map/ppermute | solution.py:722
  42.1 7.5 %collective-permute-start.18 = (bf16[448,128]{1,0:T(8,128)(2,1)S(1)}, bf16[448,128]{1,0:T(8,128)(2,1)S(1)}, u32[]{:S(2)}, u32[]{:S(2)}) collective-permute-start(bf16[448,128]{1,0:T(8,128)(2,1)S(1)} %pass.12), channel_id=1, source_target_pairs={{4,2},{5,3},{12,10},{13,11},{20,18},{21,19},{28,26},{29,27}} | collective-permute-start | bytes 344072 | tf_op jit(solution)/shard_map/ppermute | solution.py:722
  48.3 11.5 %collective-permute-start.21 = (bf16[448,128]{1,0:T(8,128)(2,1)S(1)}, bf16[448,128]{1,0:T(8,128)(2,1)S(1)}, u32[]{:S(2)}, u32[]{:S(2)}) collective-permute-start(bf16[448,128]{1,0:T(8,128)(2,1)S(1)} %pass.15), channel_id=1, source_target_pairs={{2,0},{3,1},{10,8},{11,9},{18,16},{19,17},{26,24},{27,25}} | collective-permute-start | bytes 344072 | tf_op jit(solution)/shard_map/ppermute | solution.py:722
  49.7 12.3 %collective-permute-start.19 = (bf16[448,128]{1,0:T(8,128)(2,1)S(1)}, bf16[448,128]{1,0:T(8,128)(2,1)S(1)}, u32[]{:S(2)}, u32[]{:S(2)}) collective-permute-start(bf16[448,128]{1,0:T(8,128)(2,1)S(1)} %pass.14), channel_id=1, source_target_pairs={{2,0},{3,1},{10,8},{11,9},{18,16},{19,17},{26,24},{27,25}} | collective-permute-start | bytes 344072 | tf_op jit(solution)/shard_map/ppermute | solution.py:722
  60.0 3.6 %collective-permute-start.23 = (bf16[448,128]{1,0:T(8,128)(2,1)S(1)}, bf16[448,128]{1,0:T(8,128)(2,1)S(1)}, u32[]{:S(2)}, u32[]{:S(2)}) collective-permute-start(bf16[448,128]{1,0:T(8,128)(2,1)S(1)} %get-tuple-element.182), channel_id=1, source_target_pairs={{0,1},{1,0},{2,3},{3,2},{4,5},{5,4},{6,7},{7,6},{8,9},{9,8},{10,11... | collective-permute-start | bytes 344072 | tf_op jit(solution)/shard_map/ppermute | solution.py:722
  65.3 4.9 %collective-permute-start.24 = (f32[8,1024]{1,0:T(8,128)S(1)}, f32[8,1024]{1,0:T(8,128)S(1)}, u32[]{:S(2)}, u32[]{:S(2)}) collective-permute-start(f32[8,1024]{1,0:T(8,128)S(1)} %get-tuple-element.185), channel_id=1, source_target_pairs={{0,8},{8,16},{16,24},{24,0},{1,9},{9,17},{17,25},{25,1},{2,10},{10... | collective-permute-start | bytes 98312 | tf_op jit(solution)/shard_map/ppermute | solution.py:722
  66.9 3.9 %collective-permute-start.25 = (f32[8,1024]{1,0:T(8,128)S(1)}, f32[8,1024]{1,0:T(8,128)S(1)}, u32[]{:S(2)}, u32[]{:S(2)}) collective-permute-start(f32[8,1024]{1,0:T(8,128)S(1)} %get-tuple-element.186), channel_id=1, source_target_pairs={{0,16},{8,24},{16,0},{24,8},{1,17},{9,25},{17,1},{25,9},{2,18},{10... | collective-permute-start | bytes 98312 | tf_op jit(solution)/shard_map/ppermute | solution.py:722
  68.4 3.9 %collective-permute-start.26 = (f32[8,1024]{1,0:T(8,128)S(1)}, f32[8,1024]{1,0:T(8,128)S(1)}, u32[]{:S(2)}, u32[]{:S(2)}) collective-permute-start(f32[8,1024]{1,0:T(8,128)S(1)} %get-tuple-element.187), channel_id=1, source_target_pairs={{0,24},{8,0},{16,8},{24,16},{1,25},{9,1},{17,9},{25,17},{2,26},{10... | collective-permute-start | bytes 98312 | tf_op jit(solution)/shard_map/ppermute | solution.py:722
  73.7 6.0 %collective-permute-start.28 = (f32[24,1024]{1,0:T(8,128)S(1)}, f32[24,1024]{1,0:T(8,128)S(1)}, u32[]{:S(2)}, u32[]{:S(2)}) collective-permute-start(f32[24,1024]{1,0:T(8,128)S(1)} %get-tuple-element.193), channel_id=1, source_target_pairs={{0,6},{1,7},{2,0},{3,1},{4,2},{5,3},{6,4},{7,5},{8,14},{9,15},{10,... | collective-permute-start | bytes 294920 | tf_op jit(solution)/shard_map/ppermute | solution.py:722
  73.8 6.6 %collective-permute-start.30 = (f32[8,1024]{1,0:T(8,128)S(1)}, f32[8,1024]{1,0:T(8,128)S(1)}, u32[]{:S(2)}, u32[]{:S(2)}) collective-permute-start(f32[8,1024]{1,0:T(8,128)S(1)} %get-tuple-element.188.refs_0_), channel_id=1, source_target_pairs={{0,4},{1,5},{2,6},{3,7},{4,0},{5,1},{6,2},{7,3},{8,12},{9,13},{10,... | collective-permute-start | bytes 98312 | tf_op jit(solution)/shard_map/ppermute | solution.py:722
  74.8 5.7 %collective-permute-start.29 = (f32[8,1024]{1,0:T(8,128)S(1)}, f32[8,1024]{1,0:T(8,128)S(1)}, u32[]{:S(2)}, u32[]{:S(2)}) collective-permute-start(f32[8,1024]{1,0:T(8,128)S(1)} %get-tuple-element.188.refs_0_), channel_id=1, source_target_pairs={{0,2},{1,3},{2,4},{3,5},{4,6},{5,7},{6,0},{7,1},{8,10},{9,11},{10,... | collective-permute-start | bytes 98312 | tf_op jit(solution)/shard_map/ppermute | solution.py:722
  (10 other events, 27.6 us)

commit v6 on v5

--- a/solution.py
+++ b/solution.py
@@ -306,13 +306,13 @@
         slope[:, here] = gate * (1.0 + pre * (1.0 - gate))
 
 
-def mix_side(own, local, conv, silus, grown, decays, entries, mixed, gated):
+def mix_groups(groups, local, conv, silus, grown, decays, entries, mixed, gated):
     length, features = local.shape
     shape = (length, LANES)
     read = conv[:, features + N : features + 2 * N]
     square_sum = jnp.zeros(shape, F32)
     cross_sum = jnp.zeros(shape, F32)
-    for stream, entry in enumerate(entries):
+    for (own, stream), entry in zip(groups, entries):
         number = group_at(own, stream)
         group = entry.shape[0] // N
         for pair in range(group):
@@ -327,9 +327,9 @@
     return square_sum, cross_sum
 
 
-def mix_kernel(local, conv, silus, grown, decays, *refs):
-    entries, (mixed, gated, sums) = refs[:STREAMS], refs[STREAMS:]
-    square, cross = mix_side(True, local, conv, silus, grown, decays, entries, mixed, gated)
+def mix_kernel(groups, local, conv, silus, grown, decays, *refs):
+    entries, (mixed, gated, sums) = refs[:-3], refs[-3:]
+    square, cross = mix_groups(groups, local, conv, silus, grown, decays, entries, mixed, gated)
     sums[0] = square
     sums[1] = cross
 
@@ -350,9 +350,10 @@
 
 
 def norm_kernel(mixed_in, gated_in, local, conv, silus, grown, decays, sums, decs, *refs):
-    entries, (mixed, gated, stats, out) = refs[:STREAMS], refs[STREAMS:]
+    entry, mixed, gated, stats, out = refs
     length, features = local.shape
-    square, cross = mix_side(False, local, conv, silus, grown, decays, entries, mixed, gated)
+    groups = [(False, STREAMS - 1)]
+    square, cross = mix_groups(groups, local, conv, silus, grown, decays, [entry], mixed, gated)
     square = jnp.sum(square + sums[0], axis=1, keepdims=True)
     cross = jnp.sum(cross + sums[1], axis=1, keepdims=True)
     scale = lax.rsqrt(square * (1.0 / features) + EPS)
@@ -900,11 +901,17 @@
     conv = held[0]
     silus, grown, decays = work["factors"]
     given = [work["local"], conv, silus, grown, decays]
-    mixed, gated, sums = call(mix_kernel, [wide, wide, sums_like], given + entry_own, name="mix")
+    groups = [(True, stream) for stream in range(STREAMS)] + [(False, stream) for stream in range(STREAMS - 1)]
+    mixed, gated, sums = call(
+        functools.partial(mix_kernel, groups),
+        [wide, wide, sums_like],
+        given + entry_own + entry_got[:-1],
+        name="mix",
+    )
     mixed, gated, stats, other = call(
         norm_kernel,
         [wide, wide, square, message],
-        [mixed, gated] + given + [sums, decs] + entry_got,
+        [mixed, gated] + given + [sums, decs, entry_got[-1]],
         name="norm",
         aliases={0: 0, 1: 1},
     )

time: 81.5 us -> 81.3 us (level)
  transfers between devices with their start and end apart: 31 -> 31, of which waited for: 12 -> 11; matrix products, arithmetic and copies ran while one was open for 2% -> 2% of each run, Pallas kernels for 31% -> 32%
where the time goes in v6:
time: 81.3 us; the launch traced here: 81 us
  Pallas kernels  31.7 us (39%)
  starting transfers between devices  29.2 us (36%)
  waiting for transfers between devices  17.6 us (22%)
  other arithmetic  1.32 us (2%)
  between operations  1.11 us (1%)
    pallas_call x39, Pallas kernels, call(): pl.pallas_call(kernel, out_shape=outs, in_specs=specs, out_specs=[pl.Bloc...  31.7 us
    ppermute x31, starting transfers between devices, shift(): lax.ppermute(value, axis, [(i, j) for i, j in pairs if 0 <= j < count])  29.2 us
    ppermute x31, waiting for transfers between devices, shift(): lax.ppermute(value, axis, [(i, j) for i, j in pairs if 0 <= j < count])  17.6 us
  transfers between devices with their start and end apart: 31, of which 11 were waited for; matrix products, arithmetic and copies ran while one was open for 2% of the time, Pallas kernels for 32%

profile of v6, /device:TPU:0, one launch (start us, length us, event | category | flops | bytes accessed | tf_op | source)
XLA Modules:
  0.0 81.0 jit_solution(175313736654168569)
XLA Ops:
  0.6 1.8 %open.1 = (bf16[8,3712]{1,0:T(8,128)(2,1)}, f32[8,1024]{1,0:T(8,128)}, f32[16,1024]{1,0:T(8,128)}) custom-call(bf16[128,3712]{1,0:T(8,128)(2,1)} %bitcast.22, f32[56,128]{1,0:T(8,128)} %bitcast.25, f32[4,928]{1,0:T(4,128)} %cw.1, f32[1,928]{1,0:T(1,128)} %bitcast.26, f32[1,14]{1,0:T(1,128)} %bitcast.27, f32[1,14]{1,0:T(1,128)} %bitcast.28, ...), custom_call_target="tpu_custom_call" | custom-call | bytes 1158952 | tf_op jit(solution)/shard_map/open/pallas_call | solution.py:700
  2.4 4.0 %collective-permute-start.2 = (f32[8,1024]{1,0:T(8,128)}, f32[8,1024]{1,0:T(8,128)S(1)}, u32[]{:S(2)}, u32[]{:S(2)}) collective-permute-start(f32[8,1024]{1,0:T(8,128)} %get-tuple-element.106), channel_id=1, source_target_pairs={{0,24},{8,16},{16,8},{24,0},{1,25},{9,17},{17,9},{25,1},{2,26},{10... | collective-permute-start | bytes 98312 | tf_op jit(solution)/shard_map/ppermute | solution.py:723
  7.0 1.3 %collective-permute-start.3 = (bf16[8,3712]{1,0:T(8,128)(2,1)}, bf16[8,3712]{1,0:T(8,128)(2,1)S(1)}, u32[]{:S(2)}, u32[]{:S(2)}) collective-permute-start(bf16[8,3712]{1,0:T(8,128)(2,1)} %get-tuple-element.109), channel_id=1, source_target_pairs={{0,1},{1,2},{2,3},{3,4},{4,5},{5,6},{6,7},{8,9},{9,10},{10,11},{11... | collective-permute-start | bytes 178184 | tf_op jit(solution)/shard_map/ppermute | solution.py:723
  8.3 1.3 %pad_convert_fusion.lifted = f32[136,3712]{1,0:T(8,128)S(1)} fusion(bf16[128,3712]{1,0:T(8,128)(2,1)} %bitcast.23), kind=kLoop, calls=%fused_computation | loop fusion | flops 504832 | bytes 2969600 | tf_op jit(solution)/shard_map/jit(_pad)/pad | solution.py:825
  12.4 1.4 %collective-permute-start.4 = (bf16[464,128]{1,0:T(8,128)(2,1)S(1)}, bf16[464,128]{1,0:T(8,128)(2,1)S(1)}, u32[]{:S(2)}, u32[]{:S(2)}) collective-permute-start(bf16[464,128]{1,0:T(8,128)(2,1)S(1)} %get-tuple-element.118), channel_id=1, source_target_pairs={{0,1},{1,0},{2,3},{3,2},{4,5},{5,4},{6,7},{7,6},{8,9},{9,8},{10,11... | collective-permute-start | bytes 356360 | tf_op jit(solution)/shard_map/ppermute | solution.py:723
  15.4 4.2 %collective-permute-start.5 = (bf16[464,128]{1,0:T(8,128)(2,1)S(1)}, bf16[464,128]{1,0:T(8,128)(2,1)S(1)}, u32[]{:S(2)}, u32[]{:S(2)}) collective-permute-start(bf16[464,128]{1,0:T(8,128)(2,1)S(1)} %get-tuple-element.119.own), channel_id=1, source_target_pairs={{0,2},{1,3},{8,10},{9,11},{16,18},{17,19},{24,26},{25,27}} | collective-permute-start | bytes 356360 | tf_op jit(solution)/shard_map/ppermute | solution.py:723
  20.5 1.3 %collective-permute-start.7 = (bf16[464,128]{1,0:T(8,128)(2,1)S(1)}, bf16[464,128]{1,0:T(8,128)(2,1)S(1)}, u32[]{:S(2)}, u32[]{:S(2)}) collective-permute-start(bf16[464,128]{1,0:T(8,128)(2,1)S(1)} %get-tuple-element.125.own), channel_id=1, source_target_pairs={{0,2},{1,3},{8,10},{9,11},{16,18},{17,19},{24,26},{25,27}} | collective-permute-start | bytes 356360 | tf_op jit(solution)/shard_map/ppermute | solution.py:723
  21.8 3.1 %intra.1 = (f32[128,3584]{1,0:T(8,128)S(1)}, f32[128,3712]{1,0:T(8,128)S(1)}) custom-call(f32[136,3712]{1,0:T(8,128)S(1)} %get-tuple-element.112.rows, f32[8,3840]{1,0:T(8,128)S(1)} %get-tuple-element.107.full, bf16[128,3712]{1,0:T(8,128)(2,1)S(1)} %get-tuple-element.157.conv, f32[2,128,128]{2,1,0:T(8,128)S(1)} %get-tuple-element.133.cols, ...), custom_call_target="tpu_custom_call" | custom-call | flops 117440512 | bytes 7159808 | tf_op jit(solution)/shard_map/intra/pallas_call | solution.py:700
  26.4 2.4 %factors.1 = (f32[128,3584]{1,0:T(8,128)S(1)}, f32[128,3584]{1,0:T(8,128)S(1)}, f32[128,3584]{1,0:T(8,128)S(1)}, bf16[1792,128]{1,0:T(8,128)(2,1)S(1)}, f32[3,128,3712]{2,1,0:T(8,128)S(1)}) custom-call(f32[2,128,128]{2,1,0:T(8,128)S(1)} %get-tuple-element.133.cols, bf16[128,3584]{1,0:T(8,128)(2,1)S(1)} %bitcast.18, bf16[128,3584]{1,0:T(8,128)(2,1)S(1)} %bitcast.20, ...), custom_call_target="tpu_custom_call" | custom-call | flops 7340032 | bytes 15665152 | tf_op jit(solution)/shard_map/factors/pallas_call | solution.py:700
  37.4 4.0 %gates.1 = (bf16[128,3584]{1,0:T(8,128)(2,1)}, f32[128,3584]{1,0:T(8,128)S(1)}, f32[128,128]{1,0:T(8,128)S(1)}, f32[1,3584]{1,0:T(1,128)S(1)}, f32[8,128]{1,0:T(8,128)S(1)}, /*index=5*/f32[128,128]{1,0:T(8,128)S(1)}) custom-call(f32[128,3584]{1,0:T(8,128)S(1)} %get-tuple-element.150.mixed, bf16[128,3712]{1,0:T(8,128)(2,1)S(1)} %get-tuple-element.157.conv, ...), custom_call_target="tpu_custom_call" | custom-call | flops 117440512 | bytes 8196096 | tf_op jit(solution)/shard_map/gates/pallas_call | solution.py:700
  42.9 5.5 %back.1 = (f32[128,3584]{1,0:T(8,128)S(1)}, f32[128,128]{1,0:T(8,128)S(1)}, f32[128,128]{1,0:T(8,128)S(1)}) custom-call(f32[128,3584]{1,0:T(8,128)S(1)} %get-tuple-element.164.grad_mixed, bf16[128,3712]{1,0:T(8,128)(2,1)S(1)} %get-tuple-element.157.conv, f32[2,128,128]{2,1,0:T(8,128)S(1)} %get-tuple-element.133.cols, ...), custom_call_target="tpu_custom_call" | custom-call | flops 234881024 | bytes 5148672 | tf_op jit(solution)/shard_map/back/pallas_call | solution.py:700
  48.4 1.3 %collective-permute-start.21 = (bf16[448,128]{1,0:T(8,128)(2,1)S(1)}, bf16[448,128]{1,0:T(8,128)(2,1)S(1)}, u32[]{:S(2)}, u32[]{:S(2)}) collective-permute-start(bf16[448,128]{1,0:T(8,128)(2,1)S(1)} %pass.15), channel_id=1, source_target_pairs={{2,0},{3,1},{10,8},{11,9},{18,16},{19,17},{26,24},{27,25}} | collective-permute-start | bytes 344072 | tf_op jit(solution)/shard_map/ppermute | solution.py:723
  49.8 1.5 %collective-permute-start.19 = (bf16[448,128]{1,0:T(8,128)(2,1)S(1)}, bf16[448,128]{1,0:T(8,128)(2,1)S(1)}, u32[]{:S(2)}, u32[]{:S(2)}) collective-permute-start(bf16[448,128]{1,0:T(8,128)(2,1)S(1)} %pass.14), channel_id=1, source_target_pairs={{2,0},{3,1},{10,8},{11,9},{18,16},{19,17},{26,24},{27,25}} | collective-permute-start | bytes 344072 | tf_op jit(solution)/shard_map/ppermute | solution.py:723
  51.3 8.6 %collective-permute-done.21.refs_2_ = bf16[448,128]{1,0:T(8,128)(2,1)S(1)} collective-permute-done((bf16[448,128]{1,0:T(8,128)(2,1)S(1)}, bf16[448,128]{1,0:T(8,128)(2,1)S(1)}, u32[]{:S(2)}, u32[]{:S(2)}) %collective-permute-start.21) | collective-permute-done | bytes 114720 | tf_op jit(solution)/shard_map/ppermute | solution.py:723
  60.1 1.7 %collective-permute-done.19.refs_2_ = bf16[448,128]{1,0:T(8,128)(2,1)S(1)} collective-permute-done((bf16[448,128]{1,0:T(8,128)(2,1)S(1)}, bf16[448,128]{1,0:T(8,128)(2,1)S(1)}, u32[]{:S(2)}, u32[]{:S(2)}) %collective-permute-start.19) | collective-permute-done | bytes 114720 | tf_op jit(solution)/shard_map/ppermute | solution.py:723
  62.1 1.5 %close_own.1 = (f32[144,3712]{1,0:T(8,128)S(1)}, f32[8,3840]{1,0:T(8,128)S(1)}, f32[128,128]{1,0:T(8,128)S(1)}, f32[8,128]{1,0:T(8,128)S(1)}, f32[128,128]{1,0:T(8,128)S(1)}) custom-call(f32[136,3712]{1,0:T(8,128)S(1)} %get-tuple-element.112.rows, f32[3,128,3712]{2,1,0:T(8,128)S(1)} %get-tuple-element.135.shifted, ...), custom_call_target="tpu_custom_call" | custom-call | bytes 15851520 | tf_op jit(solution)/shard_map/close_own/pallas_call | solution.py:700
  63.5 1.6 %close.1 = (f32[144,3712]{1,0:T(8,128)S(1)}, f32[8,3840]{1,0:T(8,128)S(1)}, f32[128,128]{1,0:T(8,128)S(1)}, f32[8,1024]{1,0:T(8,128)S(1)}, f32[8,1024]{1,0:T(8,1...) custom-call(f32[144,3712]{1,0:T(8,128)S(1)} %get-tuple-element.171.slopes_in,, ...), custom_call_target="tpu_custom_call", output_to_operand_aliasing={{0}: (0, {}), {1}: (1, {})} | custom-call | bytes 18528256 | tf_op jit(solution)/shard_map/close/pallas_call | solution.py:700
  65.2 1.5 %collective-permute-start.24 = (f32[8,1024]{1,0:T(8,128)S(1)}, f32[8,1024]{1,0:T(8,128)S(1)}, u32[]{:S(2)}, u32[]{:S(2)}) collective-permute-start(f32[8,1024]{1,0:T(8,128)S(1)} %get-tuple-element.185), channel_id=1, source_target_pairs={{0,8},{8,16},{16,24},{24,0},{1,9},{9,17},{17,25},{25,1},{2,10},{10... | collective-permute-start | bytes 98312 | tf_op jit(solution)/shard_map/ppermute | solution.py:723
  66.7 1.5 %collective-permute-start.25 = (f32[8,1024]{1,0:T(8,128)S(1)}, f32[8,1024]{1,0:T(8,128)S(1)}, u32[]{:S(2)}, u32[]{:S(2)}) collective-permute-start(f32[8,1024]{1,0:T(8,128)S(1)} %get-tuple-element.186), channel_id=1, source_target_pairs={{0,16},{8,24},{16,0},{24,8},{1,17},{9,25},{17,1},{25,9},{2,18},{10... | collective-permute-start | bytes 98312 | tf_op jit(solution)/shard_map/ppermute | solution.py:723
  68.2 1.4 %collective-permute-start.26 = (f32[8,1024]{1,0:T(8,128)S(1)}, f32[8,1024]{1,0:T(8,128)S(1)}, u32[]{:S(2)}, u32[]{:S(2)}) collective-permute-start(f32[8,1024]{1,0:T(8,128)S(1)} %get-tuple-element.187), channel_id=1, source_target_pairs={{0,24},{8,0},{16,8},{24,16},{1,25},{9,1},{17,9},{25,17},{2,26},{10... | collective-permute-start | bytes 98312 | tf_op jit(solution)/shard_map/ppermute | solution.py:723
  70.6 1.5 %collective-permute-done.26.refs_3_ = f32[8,1024]{1,0:T(8,128)S(1)} collective-permute-done((f32[8,1024]{1,0:T(8,128)S(1)}, f32[8,1024]{1,0:T(8,128)S(1)}, u32[]{:S(2)}, u32[]{:S(2)}) %collective-permute-start.26) | collective-permute-done | bytes 32800 | tf_op jit(solution)/shard_map/ppermute | solution.py:723
  72.3 1.3 %collective-permute-done.27.other.from_core = f32[24,1024]{1,0:T(8,128)S(1)} collective-permute-done((f32[24,1024]{1,0:T(8,128)S(1)}, f32[24,1024]{1,0:T(8,128)S(1)}, u32[]{:S(2)}, u32[]{:S(2)}) %collective-permute-start.27) | collective-permute-done | bytes 98336 | tf_op jit(solution)/shard_map/ppermute | solution.py:723
  75.6 2.4 %inputs.1 = (bf16[128,3712]{1,0:T(8,128)(2,1)}, f32[16,3712]{1,0:T(8,128)S(1)}, f32[56,128]{1,0:T(8,128)}) custom-call(f32[8,3840]{1,0:T(8,128)S(1)} %get-tuple-element.107.full, f32[144,3712]{1,0:T(8,128)S(1)} %get-tuple-element.189.slopes, f32[128,128]{1,0:T(8,128)S(1)} %get-tuple-element.190.grad_raw), custom_call_target="tpu_custom_call" | custom-call | flops 7602176 | bytes 3543040 | tf_op jit(solution)/shard_map/inputs/pallas_call | solution.py:700
  78.0 1.5 %collective-permute-done.28.from_chip.refs_3_ = f32[24,1024]{1,0:T(8,128)S(1)} collective-permute-done((f32[24,1024]{1,0:T(8,128)S(1)}, f32[24,1024]{1,0:T(8,128)S(1)}, u32[]{:S(2)}, u32[]{:S(2)}) %collective-permute-start.28) | collective-permute-done | bytes 98336 | tf_op jit(solution)/shard_map/ppermute | solution.py:723
  (84 shorter events, 22.4 us)
Async XLA Ops:
  2.4 7.2 %collective-permute-start.2 = (f32[8,1024]{1,0:T(8,128)}, f32[8,1024]{1,0:T(8,128)S(1)}, u32[]{:S(2)}, u32[]{:S(2)}) collective-permute-start(f32[8,1024]{1,0:T(8,128)} %get-tuple-element.106), channel_id=1, source_target_pairs={{0,24},{8,16},{16,8},{24,0},{1,25},{9,17},{17,9},{25,1},{2,26},{10... | collective-permute-start | bytes 98312 | tf_op jit(solution)/shard_map/ppermute | solution.py:723
  6.4 4.1 %collective-permute-start.1 = (f32[8,1024]{1,0:T(8,128)}, f32[8,1024]{1,0:T(8,128)S(1)}, u32[]{:S(2)}, u32[]{:S(2)}) collective-permute-start(f32[8,1024]{1,0:T(8,128)} %get-tuple-element.106), channel_id=1, source_target_pairs={{0,16},{8,24},{16,0},{24,8},{1,17},{9,25},{17,1},{25,9},{2,18},{10... | collective-permute-start | bytes 98312 | tf_op jit(solution)/shard_map/ppermute | solution.py:723
  6.9 4.1 %collective-permute-start = (f32[8,1024]{1,0:T(8,128)}, f32[8,1024]{1,0:T(8,128)S(1)}, u32[]{:S(2)}, u32[]{:S(2)}) collective-permute-start(f32[8,1024]{1,0:T(8,128)} %get-tuple-element.106), channel_id=1, source_target_pairs={{0,8},{8,0},{16,24},{24,16},{1,9},{9,1},{17,25},{25,17},{2,10},{10... | collective-permute-start | bytes 98312 | tf_op jit(solution)/shard_map/ppermute | solution.py:723
  7.0 4.5 %collective-permute-start.3 = (bf16[8,3712]{1,0:T(8,128)(2,1)}, bf16[8,3712]{1,0:T(8,128)(2,1)S(1)}, u32[]{:S(2)}, u32[]{:S(2)}) collective-permute-start(bf16[8,3712]{1,0:T(8,128)(2,1)} %get-tuple-element.109), channel_id=1, source_target_pairs={{0,1},{1,2},{2,3},{3,4},{4,5},{5,6},{6,7},{8,9},{9,10},{10,11},{11... | collective-permute-start | bytes 178184 | tf_op jit(solution)/shard_map/ppermute | solution.py:723
  12.4 2.9 %collective-permute-start.4 = (bf16[464,128]{1,0:T(8,128)(2,1)S(1)}, bf16[464,128]{1,0:T(8,128)(2,1)S(1)}, u32[]{:S(2)}, u32[]{:S(2)}) collective-permute-start(bf16[464,128]{1,0:T(8,128)(2,1)S(1)} %get-tuple-element.118), channel_id=1, source_target_pairs={{0,1},{1,0},{2,3},{3,2},{4,5},{5,4},{6,7},{7,6},{8,9},{9,8},{10,11... | collective-permute-start | bytes 356360 | tf_op jit(solution)/shard_map/ppermute | solution.py:723
  14.5 5.9 %collective-permute-start.6 = (bf16[464,128]{1,0:T(8,128)(2,1)S(1)}, bf16[464,128]{1,0:T(8,128)(2,1)S(1)}, u32[]{:S(2)}, u32[]{:S(2)}) collective-permute-start(bf16[464,128]{1,0:T(8,128)(2,1)S(1)} %get-tuple-element.124), channel_id=1, source_target_pairs={{0,1},{1,0},{2,3},{3,2},{4,5},{5,4},{6,7},{7,6},{8,9},{9,8},{10,11... | collective-permute-start | bytes 356360 | tf_op jit(solution)/shard_map/ppermute | solution.py:723
  15.4 9.5 %collective-permute-start.5 = (bf16[464,128]{1,0:T(8,128)(2,1)S(1)}, bf16[464,128]{1,0:T(8,128)(2,1)S(1)}, u32[]{:S(2)}, u32[]{:S(2)}) collective-permute-start(bf16[464,128]{1,0:T(8,128)(2,1)S(1)} %get-tuple-element.119.own), channel_id=1, source_target_pairs={{0,2},{1,3},{8,10},{9,11},{16,18},{17,19},{24,26},{25,27}} | collective-permute-start | bytes 356360 | tf_op jit(solution)/shard_map/ppermute | solution.py:723
  20.5 5.1 %collective-permute-start.7 = (bf16[464,128]{1,0:T(8,128)(2,1)S(1)}, bf16[464,128]{1,0:T(8,128)(2,1)S(1)}, u32[]{:S(2)}, u32[]{:S(2)}) collective-permute-start(bf16[464,128]{1,0:T(8,128)(2,1)S(1)} %get-tuple-element.125.own), channel_id=1, source_target_pairs={{0,2},{1,3},{8,10},{9,11},{16,18},{17,19},{24,26},{25,27}} | collective-permute-start | bytes 356360 | tf_op jit(solution)/shard_map/ppermute | solution.py:723
  24.9 3.8 %collective-permute-start.8 = (bf16[448,128]{1,0:T(8,128)(2,1)S(1)}, bf16[448,128]{1,0:T(8,128)(2,1)S(1)}, u32[]{:S(2)}, u32[]{:S(2)}) collective-permute-start(bf16[448,128]{1,0:T(8,128)(2,1)S(1)} %pass.8), channel_id=1, source_target_pairs={{2,4},{3,5},{10,12},{11,13},{18,20},{19,21},{26,28},{27,29}} | collective-permute-start | bytes 344072 | tf_op jit(solution)/shard_map/ppermute | solution.py:723
  25.7 3.8 %collective-permute-start.10 = (bf16[448,128]{1,0:T(8,128)(2,1)S(1)}, bf16[448,128]{1,0:T(8,128)(2,1)S(1)}, u32[]{:S(2)}, u32[]{:S(2)}) collective-permute-start(bf16[448,128]{1,0:T(8,128)(2,1)S(1)} %pass.9), channel_id=1, source_target_pairs={{2,4},{3,5},{10,12},{11,13},{18,20},{19,21},{26,28},{27,29}} | collective-permute-start | bytes 344072 | tf_op jit(solution)/shard_map/ppermute | solution.py:723
  30.8 2.1 %collective-permute-start.13 = (bf16[448,128]{1,0:T(8,128)(2,1)S(1)}, bf16[448,128]{1,0:T(8,128)(2,1)S(1)}, u32[]{:S(2)}, u32[]{:S(2)}) collective-permute-start(bf16[448,128]{1,0:T(8,128)(2,1)S(1)} %get-tuple-element.149), channel_id=1, source_target_pairs={{0,1},{1,0},{2,3},{3,2},{4,5},{5,4},{6,7},{7,6},{8,9},{9,8},{10,11... | collective-permute-start | bytes 344072 | tf_op jit(solution)/shard_map/ppermute | solution.py:723
  36.1 5.3 %collective-permute-start.17 = (bf16[464,128]{1,0:T(8,128)(2,1)S(1)}, bf16[464,128]{1,0:T(8,128)(2,1)S(1)}, u32[]{:S(2)}, u32[]{:S(2)}) collective-permute-start(bf16[464,128]{1,0:T(8,128)(2,1)S(1)} %get-tuple-element.156.own), channel_id=1, source_target_pairs={{6,4},{7,5},{14,12},{15,13},{22,20},{23,21},{30,28},{31,29}} | collective-permute-start | bytes 356360 | tf_op jit(solution)/shard_map/ppermute | solution.py:723
  36.7 5.4 %collective-permute-start.16 = (bf16[464,128]{1,0:T(8,128)(2,1)S(1)}, bf16[464,128]{1,0:T(8,128)(2,1)S(1)}, u32[]{:S(2)}, u32[]{:S(2)}) collective-permute-start(bf16[464,128]{1,0:T(8,128)(2,1)S(1)} %get-tuple-element.154.own), channel_id=1, source_target_pairs={{6,4},{7,5},{14,12},{15,13},{22,20},{23,21},{30,28},{31,29}} | collective-permute-start | bytes 356360 | tf_op jit(solution)/shard_map/ppermute | solution.py:723
  41.5 6.9 %collective-permute-start.20 = (bf16[448,128]{1,0:T(8,128)(2,1)S(1)}, bf16[448,128]{1,0:T(8,128)(2,1)S(1)}, u32[]{:S(2)}, u32[]{:S(2)}) collective-permute-start(bf16[448,128]{1,0:T(8,128)(2,1)S(1)} %pass.13), channel_id=1, source_target_pairs={{4,2},{5,3},{12,10},{13,11},{20,18},{21,19},{28,26},{29,27}} | collective-permute-start | bytes 344072 | tf_op jit(solution)/shard_map/ppermute | solution.py:723
  42.2 7.5 %collective-permute-start.18 = (bf16[448,128]{1,0:T(8,128)(2,1)S(1)}, bf16[448,128]{1,0:T(8,128)(2,1)S(1)}, u32[]{:S(2)}, u32[]{:S(2)}) collective-permute-start(bf16[448,128]{1,0:T(8,128)(2,1)S(1)} %pass.12), channel_id=1, source_target_pairs={{4,2},{5,3},{12,10},{13,11},{20,18},{21,19},{28,26},{29,27}} | collective-permute-start | bytes 344072 | tf_op jit(solution)/shard_map/ppermute | solution.py:723
  48.4 11.5 %collective-permute-start.21 = (bf16[448,128]{1,0:T(8,128)(2,1)S(1)}, bf16[448,128]{1,0:T(8,128)(2,1)S(1)}, u32[]{:S(2)}, u32[]{:S(2)}) collective-permute-start(bf16[448,128]{1,0:T(8,128)(2,1)S(1)} %pass.15), channel_id=1, source_target_pairs={{2,0},{3,1},{10,8},{11,9},{18,16},{19,17},{26,24},{27,25}} | collective-permute-start | bytes 344072 | tf_op jit(solution)/shard_map/ppermute | solution.py:723
  49.8 12.1 %collective-permute-start.19 = (bf16[448,128]{1,0:T(8,128)(2,1)S(1)}, bf16[448,128]{1,0:T(8,128)(2,1)S(1)}, u32[]{:S(2)}, u32[]{:S(2)}) collective-permute-start(bf16[448,128]{1,0:T(8,128)(2,1)S(1)} %pass.14), channel_id=1, source_target_pairs={{2,0},{3,1},{10,8},{11,9},{18,16},{19,17},{26,24},{27,25}} | collective-permute-start | bytes 344072 | tf_op jit(solution)/shard_map/ppermute | solution.py:723
  60.0 3.5 %collective-permute-start.23 = (bf16[448,128]{1,0:T(8,128)(2,1)S(1)}, bf16[448,128]{1,0:T(8,128)(2,1)S(1)}, u32[]{:S(2)}, u32[]{:S(2)}) collective-permute-start(bf16[448,128]{1,0:T(8,128)(2,1)S(1)} %get-tuple-element.182), channel_id=1, source_target_pairs={{0,1},{1,0},{2,3},{3,2},{4,5},{5,4},{6,7},{7,6},{8,9},{9,8},{10,11... | collective-permute-start | bytes 344072 | tf_op jit(solution)/shard_map/ppermute | solution.py:723
  65.2 4.9 %collective-permute-start.24 = (f32[8,1024]{1,0:T(8,128)S(1)}, f32[8,1024]{1,0:T(8,128)S(1)}, u32[]{:S(2)}, u32[]{:S(2)}) collective-permute-start(f32[8,1024]{1,0:T(8,128)S(1)} %get-tuple-element.185), channel_id=1, source_target_pairs={{0,8},{8,16},{16,24},{24,0},{1,9},{9,17},{17,25},{25,1},{2,10},{10... | collective-permute-start | bytes 98312 | tf_op jit(solution)/shard_map/ppermute | solution.py:723
  66.7 3.9 %collective-permute-start.25 = (f32[8,1024]{1,0:T(8,128)S(1)}, f32[8,1024]{1,0:T(8,128)S(1)}, u32[]{:S(2)}, u32[]{:S(2)}) collective-permute-start(f32[8,1024]{1,0:T(8,128)S(1)} %get-tuple-element.186), channel_id=1, source_target_pairs={{0,16},{8,24},{16,0},{24,8},{1,17},{9,25},{17,1},{25,9},{2,18},{10... | collective-permute-start | bytes 98312 | tf_op jit(solution)/shard_map/ppermute | solution.py:723
  68.2 3.9 %collective-permute-start.26 = (f32[8,1024]{1,0:T(8,128)S(1)}, f32[8,1024]{1,0:T(8,128)S(1)}, u32[]{:S(2)}, u32[]{:S(2)}) collective-permute-start(f32[8,1024]{1,0:T(8,128)S(1)} %get-tuple-element.187), channel_id=1, source_target_pairs={{0,24},{8,0},{16,8},{24,16},{1,25},{9,1},{17,9},{25,17},{2,26},{10... | collective-permute-start | bytes 98312 | tf_op jit(solution)/shard_map/ppermute | solution.py:723
  73.6 6.0 %collective-permute-start.28 = (f32[24,1024]{1,0:T(8,128)S(1)}, f32[24,1024]{1,0:T(8,128)S(1)}, u32[]{:S(2)}, u32[]{:S(2)}) collective-permute-start(f32[24,1024]{1,0:T(8,128)S(1)} %get-tuple-element.193), channel_id=1, source_target_pairs={{0,6},{1,7},{2,0},{3,1},{4,2},{5,3},{6,4},{7,5},{8,14},{9,15},{10,... | collective-permute-start | bytes 294920 | tf_op jit(solution)/shard_map/ppermute | solution.py:723
  73.6 6.6 %collective-permute-start.30 = (f32[8,1024]{1,0:T(8,128)S(1)}, f32[8,1024]{1,0:T(8,128)S(1)}, u32[]{:S(2)}, u32[]{:S(2)}) collective-permute-start(f32[8,1024]{1,0:T(8,128)S(1)} %get-tuple-element.188.refs_0_), channel_id=1, source_target_pairs={{0,4},{1,5},{2,6},{3,7},{4,0},{5,1},{6,2},{7,3},{8,12},{9,13},{10,... | collective-permute-start | bytes 98312 | tf_op jit(solution)/shard_map/ppermute | solution.py:723
  74.6 5.7 %collective-permute-start.29 = (f32[8,1024]{1,0:T(8,128)S(1)}, f32[8,1024]{1,0:T(8,128)S(1)}, u32[]{:S(2)}, u32[]{:S(2)}) collective-permute-start(f32[8,1024]{1,0:T(8,128)S(1)} %get-tuple-element.188.refs_0_), channel_id=1, source_target_pairs={{0,2},{1,3},{2,4},{3,5},{4,6},{5,7},{6,0},{7,1},{8,10},{9,11},{10,... | collective-permute-start | bytes 98312 | tf_op jit(solution)/shard_map/ppermute | solution.py:723
  (10 other events, 27.6 us)

commit v7 on v6

--- a/solution.py
+++ b/solution.py
@@ -918,16 +918,17 @@
     got = [shift(other, "seq", lambda i: i ^ 1)]
     given = [conv, silus, grown, decays, gated, decs]
 
-    def norm_next(own, stream, signals):
+    def norm_next(own, streams):
         return call(
-            functools.partial(norm_next_kernel, own, (stream,)),
-            [message],
-            [after(stats, *signals)] + given,
+            functools.partial(norm_next_kernel, own, streams),
+            [message] * len(streams),
+            [stats] + given,
             name="norm_next",
-        )[0]
+        )
 
     for stream in range(1, STREAMS):
-        got.append(shift(norm_next(False, stream, []), "seq", lambda i: i ^ 1))
+        got.append(shift(norm_next(False, (stream,))[0], "seq", lambda i: i ^ 1))
+    mine = norm_next(True, tuple(range(STREAMS)))
 
     def gates(signal, value):
         work["gates"] = call(
@@ -963,7 +964,7 @@
     side = half * LANES
     scratch = [pltpu.VMEM((length, side), BF16)] * 2 + [pltpu.VMEM((N, side), BF16), pltpu.VMEM((8, side), F32)]
 
-    leave_own, leave_got = entering_states(functools.partial(norm_next, True), got, True, (gates, back))
+    leave_own, leave_got = entering_states(lambda stream, signals: mine[stream], got, True, (gates, back))
     grad_gate, _, out_sums, grad_gain, grad_small, _ = work["gates"]
     grad_values, in_sums, grad_vecs = work["back"]
     slopes, whole, *sums = call(

time: 81.3 us -> 81.2 us (level)
    pallas_call x39 -> x38, Pallas kernels: 31.7 us -> 31.5 us  [call(): pl.pallas_call(kernel, out_shape=outs, in_specs=specs, out_specs=[pl.Bloc...]
  transfers between devices with their start and end apart: 31 -> 31, of which waited for: 11 -> 12; matrix products, arithmetic and copies ran while one was open for 2% -> 2% of each run, Pallas kernels for 32% -> 31%
where the time goes in v7:
time: 81.2 us; the launch traced here: 80.9 us
  Pallas kernels  31.5 us (39%)
  starting transfers between devices  29.2 us (36%)
  waiting for transfers between devices  17.7 us (22%)
  other arithmetic  1.32 us (2%)
  between operations  1.12 us (1%)
    pallas_call x38, Pallas kernels, call(): pl.pallas_call(kernel, out_shape=outs, in_specs=specs, out_specs=[pl.Bloc...  31.5 us
    ppermute x31, starting transfers between devices, shift(): lax.ppermute(value, axis, [(i, j) for i, j in pairs if 0 <= j < count])  29.2 us
    ppermute x31, waiting for transfers between devices, shift(): lax.ppermute(value, axis, [(i, j) for i, j in pairs if 0 <= j < count])  17.7 us
  transfers between devices with their start and end apart: 31, of which 12 were waited for; matrix products, arithmetic and copies ran while one was open for 2% of the time, Pallas kernels for 31%

profile of v7, /device:TPU:0, one launch (start us, length us, event | category | flops | bytes accessed | tf_op | source)
XLA Modules:
  0.0 80.9 jit_solution(16531031160849952382)
XLA Ops:
  0.6 1.8 %open.1 = (bf16[8,3712]{1,0:T(8,128)(2,1)}, f32[8,1024]{1,0:T(8,128)}, f32[16,1024]{1,0:T(8,128)}) custom-call(bf16[128,3712]{1,0:T(8,128)(2,1)} %bitcast.22, f32[56,128]{1,0:T(8,128)} %bitcast.25, f32[4,928]{1,0:T(4,128)} %cw.1, f32[1,928]{1,0:T(1,128)} %bitcast.26, f32[1,14]{1,0:T(1,128)} %bitcast.27, f32[1,14]{1,0:T(1,128)} %bitcast.28, ...), custom_call_target="tpu_custom_call" | custom-call | bytes 1158952 | tf_op jit(solution)/shard_map/open/pallas_call | solution.py:700
  2.4 4.0 %collective-permute-start.2 = (f32[8,1024]{1,0:T(8,128)}, f32[8,1024]{1,0:T(8,128)S(1)}, u32[]{:S(2)}, u32[]{:S(2)}) collective-permute-start(f32[8,1024]{1,0:T(8,128)} %get-tuple-element.107), channel_id=1, source_target_pairs={{0,24},{8,16},{16,8},{24,0},{1,25},{9,17},{17,9},{25,1},{2,26},{10... | collective-permute-start | bytes 98312 | tf_op jit(solution)/shard_map/ppermute | solution.py:723
  7.0 1.3 %collective-permute-start.3 = (bf16[8,3712]{1,0:T(8,128)(2,1)}, bf16[8,3712]{1,0:T(8,128)(2,1)S(1)}, u32[]{:S(2)}, u32[]{:S(2)}) collective-permute-start(bf16[8,3712]{1,0:T(8,128)(2,1)} %get-tuple-element.110), channel_id=1, source_target_pairs={{0,1},{1,2},{2,3},{3,4},{4,5},{5,6},{6,7},{8,9},{9,10},{10,11},{11... | collective-permute-start | bytes 178184 | tf_op jit(solution)/shard_map/ppermute | solution.py:723
  8.3 1.3 %pad_convert_fusion.lifted = f32[136,3712]{1,0:T(8,128)S(1)} fusion(bf16[128,3712]{1,0:T(8,128)(2,1)} %bitcast.23), kind=kLoop, calls=%fused_computation | loop fusion | flops 504832 | bytes 2969600 | tf_op jit(solution)/shard_map/jit(_pad)/pad | solution.py:825
  12.4 1.4 %collective-permute-start.4 = (bf16[464,128]{1,0:T(8,128)(2,1)S(1)}, bf16[464,128]{1,0:T(8,128)(2,1)S(1)}, u32[]{:S(2)}, u32[]{:S(2)}) collective-permute-start(bf16[464,128]{1,0:T(8,128)(2,1)S(1)} %get-tuple-element.119), channel_id=1, source_target_pairs={{0,1},{1,0},{2,3},{3,2},{4,5},{5,4},{6,7},{7,6},{8,9},{9,8},{10,11... | collective-permute-start | bytes 356360 | tf_op jit(solution)/shard_map/ppermute | solution.py:723
  15.4 4.2 %collective-permute-start.5 = (bf16[464,128]{1,0:T(8,128)(2,1)S(1)}, bf16[464,128]{1,0:T(8,128)(2,1)S(1)}, u32[]{:S(2)}, u32[]{:S(2)}) collective-permute-start(bf16[464,128]{1,0:T(8,128)(2,1)S(1)} %get-tuple-element.120.own), channel_id=1, source_target_pairs={{0,2},{1,3},{8,10},{9,11},{16,18},{17,19},{24,26},{25,27}} | collective-permute-start | bytes 356360 | tf_op jit(solution)/shard_map/ppermute | solution.py:723
  20.5 1.3 %collective-permute-start.7 = (bf16[464,128]{1,0:T(8,128)(2,1)S(1)}, bf16[464,128]{1,0:T(8,128)(2,1)S(1)}, u32[]{:S(2)}, u32[]{:S(2)}) collective-permute-start(bf16[464,128]{1,0:T(8,128)(2,1)S(1)} %get-tuple-element.126.own), channel_id=1, source_target_pairs={{0,2},{1,3},{8,10},{9,11},{16,18},{17,19},{24,26},{25,27}} | collective-permute-start | bytes 356360 | tf_op jit(solution)/shard_map/ppermute | solution.py:723
  21.8 3.1 %intra.1 = (f32[128,3584]{1,0:T(8,128)S(1)}, f32[128,3712]{1,0:T(8,128)S(1)}) custom-call(f32[136,3712]{1,0:T(8,128)S(1)} %get-tuple-element.113.rows, f32[8,3840]{1,0:T(8,128)S(1)} %get-tuple-element.108.full, bf16[128,3712]{1,0:T(8,128)(2,1)S(1)} %get-tuple-element.159.conv, f32[2,128,128]{2,1,0:T(8,128)S(1)} %get-tuple-element.134.cols, ...), custom_call_target="tpu_custom_call" | custom-call | flops 117440512 | bytes 7159808 | tf_op jit(solution)/shard_map/intra/pallas_call | solution.py:700
  26.4 2.4 %factors.1 = (f32[128,3584]{1,0:T(8,128)S(1)}, f32[128,3584]{1,0:T(8,128)S(1)}, f32[128,3584]{1,0:T(8,128)S(1)}, bf16[1792,128]{1,0:T(8,128)(2,1)S(1)}, f32[3,128,3712]{2,1,0:T(8,128)S(1)}) custom-call(f32[2,128,128]{2,1,0:T(8,128)S(1)} %get-tuple-element.134.cols, bf16[128,3584]{1,0:T(8,128)(2,1)S(1)} %bitcast.18, bf16[128,3584]{1,0:T(8,128)(2,1)S(1)} %bitcast.20, ...), custom_call_target="tpu_custom_call" | custom-call | flops 7340032 | bytes 15665152 | tf_op jit(solution)/shard_map/factors/pallas_call | solution.py:700
  37.3 4.0 %gates.1 = (bf16[128,3584]{1,0:T(8,128)(2,1)}, f32[128,3584]{1,0:T(8,128)S(1)}, f32[128,128]{1,0:T(8,128)S(1)}, f32[1,3584]{1,0:T(1,128)S(1)}, f32[8,128]{1,0:T(8,128)S(1)}, /*index=5*/f32[128,128]{1,0:T(8,128)S(1)}) custom-call(f32[128,3584]{1,0:T(8,128)S(1)} %get-tuple-element.151.mixed, bf16[128,3712]{1,0:T(8,128)(2,1)S(1)} %get-tuple-element.159.conv, ...), custom_call_target="tpu_custom_call" | custom-call | flops 117440512 | bytes 8196096 | tf_op jit(solution)/shard_map/gates/pallas_call | solution.py:700
  42.8 5.5 %back.1 = (f32[128,3584]{1,0:T(8,128)S(1)}, f32[128,128]{1,0:T(8,128)S(1)}, f32[128,128]{1,0:T(8,128)S(1)}) custom-call(f32[128,3584]{1,0:T(8,128)S(1)} %get-tuple-element.166.grad_mixed, bf16[128,3712]{1,0:T(8,128)(2,1)S(1)} %get-tuple-element.159.conv, f32[2,128,128]{2,1,0:T(8,128)S(1)} %get-tuple-element.134.cols, ...), custom_call_target="tpu_custom_call" | custom-call | flops 234881024 | bytes 5148672 | tf_op jit(solution)/shard_map/back/pallas_call | solution.py:700
  48.3 1.3 %collective-permute-start.21 = (bf16[448,128]{1,0:T(8,128)(2,1)S(1)}, bf16[448,128]{1,0:T(8,128)(2,1)S(1)}, u32[]{:S(2)}, u32[]{:S(2)}) collective-permute-start(bf16[448,128]{1,0:T(8,128)(2,1)S(1)} %pass.15), channel_id=1, source_target_pairs={{2,0},{3,1},{10,8},{11,9},{18,16},{19,17},{26,24},{27,25}} | collective-permute-start | bytes 344072 | tf_op jit(solution)/shard_map/ppermute | solution.py:723
  49.7 1.5 %collective-permute-start.19 = (bf16[448,128]{1,0:T(8,128)(2,1)S(1)}, bf16[448,128]{1,0:T(8,128)(2,1)S(1)}, u32[]{:S(2)}, u32[]{:S(2)}) collective-permute-start(bf16[448,128]{1,0:T(8,128)(2,1)S(1)} %pass.14), channel_id=1, source_target_pairs={{2,0},{3,1},{10,8},{11,9},{18,16},{19,17},{26,24},{27,25}} | collective-permute-start | bytes 344072 | tf_op jit(solution)/shard_map/ppermute | solution.py:723
  51.2 8.7 %collective-permute-done.21.refs_2_ = bf16[448,128]{1,0:T(8,128)(2,1)S(1)} collective-permute-done((bf16[448,128]{1,0:T(8,128)(2,1)S(1)}, bf16[448,128]{1,0:T(8,128)(2,1)S(1)}, u32[]{:S(2)}, u32[]{:S(2)}) %collective-permute-start.21) | collective-permute-done | bytes 114720 | tf_op jit(solution)/shard_map/ppermute | solution.py:723
  60.1 1.6 %collective-permute-done.19.refs_2_ = bf16[448,128]{1,0:T(8,128)(2,1)S(1)} collective-permute-done((bf16[448,128]{1,0:T(8,128)(2,1)S(1)}, bf16[448,128]{1,0:T(8,128)(2,1)S(1)}, u32[]{:S(2)}, u32[]{:S(2)}) %collective-permute-start.19) | collective-permute-done | bytes 114720 | tf_op jit(solution)/shard_map/ppermute | solution.py:723
  62.0 1.5 %close_own.1 = (f32[144,3712]{1,0:T(8,128)S(1)}, f32[8,3840]{1,0:T(8,128)S(1)}, f32[128,128]{1,0:T(8,128)S(1)}, f32[8,128]{1,0:T(8,128)S(1)}, f32[128,128]{1,0:T(8,128)S(1)}) custom-call(f32[136,3712]{1,0:T(8,128)S(1)} %get-tuple-element.113.rows, f32[3,128,3712]{2,1,0:T(8,128)S(1)} %get-tuple-element.136.shifted, ...), custom_call_target="tpu_custom_call" | custom-call | bytes 15851520 | tf_op jit(solution)/shard_map/close_own/pallas_call | solution.py:700
  63.4 1.6 %close.1 = (f32[144,3712]{1,0:T(8,128)S(1)}, f32[8,3840]{1,0:T(8,128)S(1)}, f32[128,128]{1,0:T(8,128)S(1)}, f32[8,1024]{1,0:T(8,128)S(1)}, f32[8,1024]{1,0:T(8,1...) custom-call(f32[144,3712]{1,0:T(8,128)S(1)} %get-tuple-element.173.slopes_in,, ...), custom_call_target="tpu_custom_call", output_to_operand_aliasing={{0}: (0, {}), {1}: (1, {})} | custom-call | bytes 18528256 | tf_op jit(solution)/shard_map/close/pallas_call | solution.py:700
  65.1 1.5 %collective-permute-start.24 = (f32[8,1024]{1,0:T(8,128)S(1)}, f32[8,1024]{1,0:T(8,128)S(1)}, u32[]{:S(2)}, u32[]{:S(2)}) collective-permute-start(f32[8,1024]{1,0:T(8,128)S(1)} %get-tuple-element.187), channel_id=1, source_target_pairs={{0,8},{8,16},{16,24},{24,0},{1,9},{9,17},{17,25},{25,1},{2,10},{10... | collective-permute-start | bytes 98312 | tf_op jit(solution)/shard_map/ppermute | solution.py:723
  66.6 1.5 %collective-permute-start.25 = (f32[8,1024]{1,0:T(8,128)S(1)}, f32[8,1024]{1,0:T(8,128)S(1)}, u32[]{:S(2)}, u32[]{:S(2)}) collective-permute-start(f32[8,1024]{1,0:T(8,128)S(1)} %get-tuple-element.188), channel_id=1, source_target_pairs={{0,16},{8,24},{16,0},{24,8},{1,17},{9,25},{17,1},{25,9},{2,18},{10... | collective-permute-start | bytes 98312 | tf_op jit(solution)/shard_map/ppermute | solution.py:723
  68.1 1.4 %collective-permute-start.26 = (f32[8,1024]{1,0:T(8,128)S(1)}, f32[8,1024]{1,0:T(8,128)S(1)}, u32[]{:S(2)}, u32[]{:S(2)}) collective-permute-start(f32[8,1024]{1,0:T(8,128)S(1)} %get-tuple-element.189), channel_id=1, source_target_pairs={{0,24},{8,0},{16,8},{24,16},{1,25},{9,1},{17,9},{25,17},{2,26},{10... | collective-permute-start | bytes 98312 | tf_op jit(solution)/shard_map/ppermute | solution.py:723
  70.5 1.5 %collective-permute-done.26.refs_3_ = f32[8,1024]{1,0:T(8,128)S(1)} collective-permute-done((f32[8,1024]{1,0:T(8,128)S(1)}, f32[8,1024]{1,0:T(8,128)S(1)}, u32[]{:S(2)}, u32[]{:S(2)}) %collective-permute-start.26) | collective-permute-done | bytes 32800 | tf_op jit(solution)/shard_map/ppermute | solution.py:723
  72.2 1.3 %collective-permute-done.27.other.from_core = f32[24,1024]{1,0:T(8,128)S(1)} collective-permute-done((f32[24,1024]{1,0:T(8,128)S(1)}, f32[24,1024]{1,0:T(8,128)S(1)}, u32[]{:S(2)}, u32[]{:S(2)}) %collective-permute-start.27) | collective-permute-done | bytes 98336 | tf_op jit(solution)/shard_map/ppermute | solution.py:723
  75.5 2.4 %inputs.1 = (bf16[128,3712]{1,0:T(8,128)(2,1)}, f32[16,3712]{1,0:T(8,128)S(1)}, f32[56,128]{1,0:T(8,128)}) custom-call(f32[8,3840]{1,0:T(8,128)S(1)} %get-tuple-element.108.full, f32[144,3712]{1,0:T(8,128)S(1)} %get-tuple-element.191.slopes, f32[128,128]{1,0:T(8,128)S(1)} %get-tuple-element.192.grad_raw), custom_call_target="tpu_custom_call" | custom-call | flops 7602176 | bytes 3543040 | tf_op jit(solution)/shard_map/inputs/pallas_call | solution.py:700
  77.9 1.5 %collective-permute-done.28.from_chip.refs_3_ = f32[24,1024]{1,0:T(8,128)S(1)} collective-permute-done((f32[24,1024]{1,0:T(8,128)S(1)}, f32[24,1024]{1,0:T(8,128)S(1)}, u32[]{:S(2)}, u32[]{:S(2)}) %collective-permute-start.28) | collective-permute-done | bytes 98336 | tf_op jit(solution)/shard_map/ppermute | solution.py:723
  (83 shorter events, 22.3 us)
Async XLA Ops:
  2.4 7.2 %collective-permute-start.2 = (f32[8,1024]{1,0:T(8,128)}, f32[8,1024]{1,0:T(8,128)S(1)}, u32[]{:S(2)}, u32[]{:S(2)}) collective-permute-start(f32[8,1024]{1,0:T(8,128)} %get-tuple-element.107), channel_id=1, source_target_pairs={{0,24},{8,16},{16,8},{24,0},{1,25},{9,17},{17,9},{25,1},{2,26},{10... | collective-permute-start | bytes 98312 | tf_op jit(solution)/shard_map/ppermute | solution.py:723
  6.4 4.1 %collective-permute-start.1 = (f32[8,1024]{1,0:T(8,128)}, f32[8,1024]{1,0:T(8,128)S(1)}, u32[]{:S(2)}, u32[]{:S(2)}) collective-permute-start(f32[8,1024]{1,0:T(8,128)} %get-tuple-element.107), channel_id=1, source_target_pairs={{0,16},{8,24},{16,0},{24,8},{1,17},{9,25},{17,1},{25,9},{2,18},{10... | collective-permute-start | bytes 98312 | tf_op jit(solution)/shard_map/ppermute | solution.py:723
  6.9 4.1 %collective-permute-start = (f32[8,1024]{1,0:T(8,128)}, f32[8,1024]{1,0:T(8,128)S(1)}, u32[]{:S(2)}, u32[]{:S(2)}) collective-permute-start(f32[8,1024]{1,0:T(8,128)} %get-tuple-element.107), channel_id=1, source_target_pairs={{0,8},{8,0},{16,24},{24,16},{1,9},{9,1},{17,25},{25,17},{2,10},{10... | collective-permute-start | bytes 98312 | tf_op jit(solution)/shard_map/ppermute | solution.py:723
  7.0 4.5 %collective-permute-start.3 = (bf16[8,3712]{1,0:T(8,128)(2,1)}, bf16[8,3712]{1,0:T(8,128)(2,1)S(1)}, u32[]{:S(2)}, u32[]{:S(2)}) collective-permute-start(bf16[8,3712]{1,0:T(8,128)(2,1)} %get-tuple-element.110), channel_id=1, source_target_pairs={{0,1},{1,2},{2,3},{3,4},{4,5},{5,6},{6,7},{8,9},{9,10},{10,11},{11... | collective-permute-start | bytes 178184 | tf_op jit(solution)/shard_map/ppermute | solution.py:723
  12.4 2.9 %collective-permute-start.4 = (bf16[464,128]{1,0:T(8,128)(2,1)S(1)}, bf16[464,128]{1,0:T(8,128)(2,1)S(1)}, u32[]{:S(2)}, u32[]{:S(2)}) collective-permute-start(bf16[464,128]{1,0:T(8,128)(2,1)S(1)} %get-tuple-element.119), channel_id=1, source_target_pairs={{0,1},{1,0},{2,3},{3,2},{4,5},{5,4},{6,7},{7,6},{8,9},{9,8},{10,11... | collective-permute-start | bytes 356360 | tf_op jit(solution)/shard_map/ppermute | solution.py:723
  14.5 5.9 %collective-permute-start.6 = (bf16[464,128]{1,0:T(8,128)(2,1)S(1)}, bf16[464,128]{1,0:T(8,128)(2,1)S(1)}, u32[]{:S(2)}, u32[]{:S(2)}) collective-permute-start(bf16[464,128]{1,0:T(8,128)(2,1)S(1)} %get-tuple-element.125), channel_id=1, source_target_pairs={{0,1},{1,0},{2,3},{3,2},{4,5},{5,4},{6,7},{7,6},{8,9},{9,8},{10,11... | collective-permute-start | bytes 356360 | tf_op jit(solution)/shard_map/ppermute | solution.py:723
  15.4 9.4 %collective-permute-start.5 = (bf16[464,128]{1,0:T(8,128)(2,1)S(1)}, bf16[464,128]{1,0:T(8,128)(2,1)S(1)}, u32[]{:S(2)}, u32[]{:S(2)}) collective-permute-start(bf16[464,128]{1,0:T(8,128)(2,1)S(1)} %get-tuple-element.120.own), channel_id=1, source_target_pairs={{0,2},{1,3},{8,10},{9,11},{16,18},{17,19},{24,26},{25,27}} | collective-permute-start | bytes 356360 | tf_op jit(solution)/shard_map/ppermute | solution.py:723
  20.5 5.1 %collective-permute-start.7 = (bf16[464,128]{1,0:T(8,128)(2,1)S(1)}, bf16[464,128]{1,0:T(8,128)(2,1)S(1)}, u32[]{:S(2)}, u32[]{:S(2)}) collective-permute-start(bf16[464,128]{1,0:T(8,128)(2,1)S(1)} %get-tuple-element.126.own), channel_id=1, source_target_pairs={{0,2},{1,3},{8,10},{9,11},{16,18},{17,19},{24,26},{25,27}} | collective-permute-start | bytes 356360 | tf_op jit(solution)/shard_map/ppermute | solution.py:723
  24.9 3.8 %collective-permute-start.8 = (bf16[448,128]{1,0:T(8,128)(2,1)S(1)}, bf16[448,128]{1,0:T(8,128)(2,1)S(1)}, u32[]{:S(2)}, u32[]{:S(2)}) collective-permute-start(bf16[448,128]{1,0:T(8,128)(2,1)S(1)} %pass.8), channel_id=1, source_target_pairs={{2,4},{3,5},{10,12},{11,13},{18,20},{19,21},{26,28},{27,29}} | collective-permute-start | bytes 344072 | tf_op jit(solution)/shard_map/ppermute | solution.py:723
  25.7 3.8 %collective-permute-start.10 = (bf16[448,128]{1,0:T(8,128)(2,1)S(1)}, bf16[448,128]{1,0:T(8,128)(2,1)S(1)}, u32[]{:S(2)}, u32[]{:S(2)}) collective-permute-start(bf16[448,128]{1,0:T(8,128)(2,1)S(1)} %pass.9), channel_id=1, source_target_pairs={{2,4},{3,5},{10,12},{11,13},{18,20},{19,21},{26,28},{27,29}} | collective-permute-start | bytes 344072 | tf_op jit(solution)/shard_map/ppermute | solution.py:723
  30.8 2.1 %collective-permute-start.13 = (bf16[448,128]{1,0:T(8,128)(2,1)S(1)}, bf16[448,128]{1,0:T(8,128)(2,1)S(1)}, u32[]{:S(2)}, u32[]{:S(2)}) collective-permute-start(bf16[448,128]{1,0:T(8,128)(2,1)S(1)} %get-tuple-element.150), channel_id=1, source_target_pairs={{0,1},{1,0},{2,3},{3,2},{4,5},{5,4},{6,7},{7,6},{8,9},{9,8},{10,11... | collective-permute-start | bytes 344072 | tf_op jit(solution)/shard_map/ppermute | solution.py:723
  35.9 5.5 %collective-permute-start.17 = (bf16[464,128]{1,0:T(8,128)(2,1)S(1)}, bf16[464,128]{1,0:T(8,128)(2,1)S(1)}, u32[]{:S(2)}, u32[]{:S(2)}) collective-permute-start(bf16[464,128]{1,0:T(8,128)(2,1)S(1)} %get-tuple-element.158.own), channel_id=1, source_target_pairs={{6,4},{7,5},{14,12},{15,13},{22,20},{23,21},{30,28},{31,29}} | collective-permute-start | bytes 356360 | tf_op jit(solution)/shard_map/ppermute | solution.py:723
  36.7 5.4 %collective-permute-start.16 = (bf16[464,128]{1,0:T(8,128)(2,1)S(1)}, bf16[464,128]{1,0:T(8,128)(2,1)S(1)}, u32[]{:S(2)}, u32[]{:S(2)}) collective-permute-start(bf16[464,128]{1,0:T(8,128)(2,1)S(1)} %get-tuple-element.156.own), channel_id=1, source_target_pairs={{6,4},{7,5},{14,12},{15,13},{22,20},{23,21},{30,28},{31,29}} | collective-permute-start | bytes 356360 | tf_op jit(solution)/shard_map/ppermute | solution.py:723
  41.4 6.9 %collective-permute-start.20 = (bf16[448,128]{1,0:T(8,128)(2,1)S(1)}, bf16[448,128]{1,0:T(8,128)(2,1)S(1)}, u32[]{:S(2)}, u32[]{:S(2)}) collective-permute-start(bf16[448,128]{1,0:T(8,128)(2,1)S(1)} %pass.13), channel_id=1, source_target_pairs={{4,2},{5,3},{12,10},{13,11},{20,18},{21,19},{28,26},{29,27}} | collective-permute-start | bytes 344072 | tf_op jit(solution)/shard_map/ppermute | solution.py:723
  42.1 7.5 %collective-permute-start.18 = (bf16[448,128]{1,0:T(8,128)(2,1)S(1)}, bf16[448,128]{1,0:T(8,128)(2,1)S(1)}, u32[]{:S(2)}, u32[]{:S(2)}) collective-permute-start(bf16[448,128]{1,0:T(8,128)(2,1)S(1)} %pass.12), channel_id=1, source_target_pairs={{4,2},{5,3},{12,10},{13,11},{20,18},{21,19},{28,26},{29,27}} | collective-permute-start | bytes 344072 | tf_op jit(solution)/shard_map/ppermute | solution.py:723
  48.3 11.5 %collective-permute-start.21 = (bf16[448,128]{1,0:T(8,128)(2,1)S(1)}, bf16[448,128]{1,0:T(8,128)(2,1)S(1)}, u32[]{:S(2)}, u32[]{:S(2)}) collective-permute-start(bf16[448,128]{1,0:T(8,128)(2,1)S(1)} %pass.15), channel_id=1, source_target_pairs={{2,0},{3,1},{10,8},{11,9},{18,16},{19,17},{26,24},{27,25}} | collective-permute-start | bytes 344072 | tf_op jit(solution)/shard_map/ppermute | solution.py:723
  49.7 12.0 %collective-permute-start.19 = (bf16[448,128]{1,0:T(8,128)(2,1)S(1)}, bf16[448,128]{1,0:T(8,128)(2,1)S(1)}, u32[]{:S(2)}, u32[]{:S(2)}) collective-permute-start(bf16[448,128]{1,0:T(8,128)(2,1)S(1)} %pass.14), channel_id=1, source_target_pairs={{2,0},{3,1},{10,8},{11,9},{18,16},{19,17},{26,24},{27,25}} | collective-permute-start | bytes 344072 | tf_op jit(solution)/shard_map/ppermute | solution.py:723
  60.0 3.4 %collective-permute-start.23 = (bf16[448,128]{1,0:T(8,128)(2,1)S(1)}, bf16[448,128]{1,0:T(8,128)(2,1)S(1)}, u32[]{:S(2)}, u32[]{:S(2)}) collective-permute-start(bf16[448,128]{1,0:T(8,128)(2,1)S(1)} %get-tuple-element.184), channel_id=1, source_target_pairs={{0,1},{1,0},{2,3},{3,2},{4,5},{5,4},{6,7},{7,6},{8,9},{9,8},{10,11... | collective-permute-start | bytes 344072 | tf_op jit(solution)/shard_map/ppermute | solution.py:723
  65.1 4.9 %collective-permute-start.24 = (f32[8,1024]{1,0:T(8,128)S(1)}, f32[8,1024]{1,0:T(8,128)S(1)}, u32[]{:S(2)}, u32[]{:S(2)}) collective-permute-start(f32[8,1024]{1,0:T(8,128)S(1)} %get-tuple-element.187), channel_id=1, source_target_pairs={{0,8},{8,16},{16,24},{24,0},{1,9},{9,17},{17,25},{25,1},{2,10},{10... | collective-permute-start | bytes 98312 | tf_op jit(solution)/shard_map/ppermute | solution.py:723
  66.6 3.9 %collective-permute-start.25 = (f32[8,1024]{1,0:T(8,128)S(1)}, f32[8,1024]{1,0:T(8,128)S(1)}, u32[]{:S(2)}, u32[]{:S(2)}) collective-permute-start(f32[8,1024]{1,0:T(8,128)S(1)} %get-tuple-element.188), channel_id=1, source_target_pairs={{0,16},{8,24},{16,0},{24,8},{1,17},{9,25},{17,1},{25,9},{2,18},{10... | collective-permute-start | bytes 98312 | tf_op jit(solution)/shard_map/ppermute | solution.py:723
  68.1 3.9 %collective-permute-start.26 = (f32[8,1024]{1,0:T(8,128)S(1)}, f32[8,1024]{1,0:T(8,128)S(1)}, u32[]{:S(2)}, u32[]{:S(2)}) collective-permute-start(f32[8,1024]{1,0:T(8,128)S(1)} %get-tuple-element.189), channel_id=1, source_target_pairs={{0,24},{8,0},{16,8},{24,16},{1,25},{9,1},{17,9},{25,17},{2,26},{10... | collective-permute-start | bytes 98312 | tf_op jit(solution)/shard_map/ppermute | solution.py:723
  73.5 6.0 %collective-permute-start.28 = (f32[24,1024]{1,0:T(8,128)S(1)}, f32[24,1024]{1,0:T(8,128)S(1)}, u32[]{:S(2)}, u32[]{:S(2)}) collective-permute-start(f32[24,1024]{1,0:T(8,128)S(1)} %get-tuple-element.195), channel_id=1, source_target_pairs={{0,6},{1,7},{2,0},{3,1},{4,2},{5,3},{6,4},{7,5},{8,14},{9,15},{10,... | collective-permute-start | bytes 294920 | tf_op jit(solution)/shard_map/ppermute | solution.py:723
  73.5 6.6 %collective-permute-start.30 = (f32[8,1024]{1,0:T(8,128)S(1)}, f32[8,1024]{1,0:T(8,128)S(1)}, u32[]{:S(2)}, u32[]{:S(2)}) collective-permute-start(f32[8,1024]{1,0:T(8,128)S(1)} %get-tuple-element.190.refs_0_), channel_id=1, source_target_pairs={{0,4},{1,5},{2,6},{3,7},{4,0},{5,1},{6,2},{7,3},{8,12},{9,13},{10,... | collective-permute-start | bytes 98312 | tf_op jit(solution)/shard_map/ppermute | solution.py:723
  74.5 5.7 %collective-permute-start.29 = (f32[8,1024]{1,0:T(8,128)S(1)}, f32[8,1024]{1,0:T(8,128)S(1)}, u32[]{:S(2)}, u32[]{:S(2)}) collective-permute-start(f32[8,1024]{1,0:T(8,128)S(1)} %get-tuple-element.190.refs_0_), channel_id=1, source_target_pairs={{0,2},{1,3},{2,4},{3,5},{4,6},{5,7},{6,0},{7,1},{8,10},{9,11},{10,... | collective-permute-start | bytes 98312 | tf_op jit(solution)/shard_map/ppermute | solution.py:723
  (10 other events, 28.1 us)
